TPU v7x, 32 devices: a whole 2x2x4 slice. The times are simulated.
32 devices in a mesh: arc: 8 (over z, x), coef: 4 (over y, core).
Axes of the slice: x: 2, y: 2, z: 4, core: 2. Of those that a mesh axis runs over, the one named last changes fastest.
Arguments:
- local_design: bfloat16 [32, 256, 512], P(('arc', 'coef')), may hold values from -0.25 to 0.25
- global_design: bfloat16 [32, 2304, 512], P(('arc', 'coef')), may hold values from -0.046875 to 0.046875
- local_prior: float32 [32, 256], P(('arc', 'coef')), may hold values from 0.2 to 2
- obs_count: int32 [32], P(('arc', 'coef')), may hold values from 128 to 512, as said below
- band_mask: int32 [32, 4], P(('arc', 'coef')), may hold values 0 or 1
- owner_columns: int32 [2048], replicated, may hold values from 0 to 2047, each once
- kaula_prior: float32 [4, 128], P('coef'), may hold values from 0.05 to 0.5
Outputs:
- normal_rows: float32 [4, 512, 768], P('coef', 'arc')
- panel_factor: float32 [4, 128, 128], P('coef')
Inputs may be any that keep to these rules, and one draw needn't show every extreme that they name: Arc a uses its first obs_count[a] rows; some arc uses all 512. `owner_columns`: each coefficient index appears once.
All inputs are finite; a program needn't handle non-finite values. No bound on the sum of `band_mask` on one device may be relied on, other than what follows from the above.
Results may differ from a plain program's by a relative error of at most 0.0006.
Values may be sent and summed in bfloat16 or wider, within the bound.
No kernel may reach another device: no remote copies, remote signals or barrier semaphores. Data moves between devices by JAX's collectives and lax.ppermute only.
A program may use at most 128 MiB of HBM per device.

v0:
```python
import jax
import jax.numpy as jnp
from jax import lax
from jax.sharding import PartitionSpec as P

OB = 512
KB = 256
P_SIZE = 128


def reduce_one(local_one, global_one, prior_one, count_one, sense_one):
    row_total = local_one.shape[1]
    row_valid = (lax.iota(jnp.int32, row_total) < count_one).astype(jnp.bfloat16)
    band_cols = jnp.repeat(sense_one, OB)
    column_valid = jnp.concatenate([band_cols, jnp.ones((KB,), jnp.int32)]).astype(jnp.bfloat16)
    local_rows = local_one * row_valid[None, :]
    global_rows = global_one * row_valid[None, :] * column_valid[:, None]
    inner = (((1,), (1,)), ((), ()))
    local_normal = lax.dot_general(
        local_rows, local_rows, inner, preferred_element_type=jnp.float32
    ) + jnp.diag(prior_one)
    coupling = lax.dot_general(local_rows, global_rows, inner, preferred_element_type=jnp.float32)
    factor = jnp.linalg.cholesky(local_normal)
    solved = jax.scipy.linalg.cho_solve((factor, True), coupling).astype(jnp.bfloat16)
    removed = lax.dot_general(
        solved, local_rows, (((0,), (0,)), ((), ())), preferred_element_type=jnp.float32
    )
    return (global_rows.astype(jnp.float32) - removed).astype(jnp.bfloat16)


def per_device(
    local_design, global_design, local_prior, obs_count, band_mask, owner_columns, kaula_prior
):
    reduced = jax.vmap(reduce_one)(local_design, global_design, local_prior, obs_count, band_mask)
    n_owner = lax.axis_size("coef")
    arc_local = reduced.shape[0]
    row_length = reduced.shape[2]
    stride = OB // P_SIZE
    owned_rows = jnp.take(reduced, owner_columns, axis=1).reshape(
        arc_local, n_owner, OB, row_length
    )
    border = reduced[:, n_owner * OB :, :]
    partner = jnp.concatenate(
        [owned_rows, jnp.broadcast_to(border[:, None], (arc_local, n_owner, KB, row_length))],
        axis=2,
    )
    per_arc = OB // lax.axis_size("arc")
    blocks = n_owner * per_arc * lax.axis_size("arc") // (n_owner * per_arc)
    product = jnp.einsum("acim,ackm->cik", owned_rows, partner, preferred_element_type=jnp.float32)
    product = product.reshape(n_owner, blocks, per_arc, product.shape[2]).transpose(1, 0, 2, 3)
    arc_part = lax.psum_scatter(
        product.reshape(blocks * n_owner * per_arc, product.shape[3]),
        "arc",
        scatter_dimension=0,
        tiled=True,
    )
    normal_rows = lax.psum_scatter(
        arc_part.reshape(n_owner, per_arc, arc_part.shape[1]),
        "coef",
        scatter_dimension=0,
        tiled=True,
    )
    panel_strip = normal_rows[:, :, :OB:stride]
    all_rows = lax.all_gather(panel_strip, "arc", axis=1, tiled=True)
    panel_block = all_rows[:, ::stride, :]
    shifted = panel_block + jax.vmap(jnp.diag)(kaula_prior)
    panel_factor = jax.vmap(jnp.linalg.cholesky)(shifted)
    return (normal_rows, panel_factor)


def solution(mesh):
    in_specs = (
        P(("arc", "coef"), None, None),
        P(("arc", "coef"), None, None),
        P(("arc", "coef"), None),
        P(("arc", "coef")),
        P(("arc", "coef"), None),
        P(),
        P("coef", None),
    )
    out_specs = (P("coef", "arc", None), P("coef", None, None))
    return jax.shard_map(
        per_device, mesh=mesh, in_specs=in_specs, out_specs=out_specs, check_vma=False
    )
```

profile of v0, /device:TPU:0, one launch (start us, length us, event | category | flops | bytes accessed | tf_op | source)
XLA Modules:
  0.0 300.7 jit_solution(16476463251603540198)
XLA Ops:
  10.1 1.4 convolution_add_fusion
  11.7 11.7 %custom-call.24 = f32[1,128,128]{2,1,0:T(8,128)S(1)} custom-call(f32[1,128,128]{2,1,0:T(8,128)S(1)} %cholesky.159), custom_call_target="Cholesky" | custom-call | tf_op jit(solution)/shard_map/vmap(jit(cholesky))/cholesky | solution.py:23
  23.7 9.8 %custom-call.25 = f32[1,1,128,128]{2,3,1,0:T(8,128)S(1)} custom-call(f32[1,1,128,128]{3,2,1,0:T(8,128)S(1)} %copy.37), custom_call_target="InvertDiagBlocksLowerTriangular" | custom-call | tf_op jit(solution)/shard_map/vmap(jit(cholesky))/cholesky | solution.py:23
  34.0 11.7 %custom-call.26 = f32[1,128,128]{2,1,0:T(8,128)S(1)} custom-call(f32[1,128,128]{2,1,0:T(8,128)S(1)} %fusion.16), custom_call_target="Cholesky" | custom-call | tf_op jit(solution)/shard_map/vmap(jit(cholesky))/cholesky | solution.py:23
  47.9 5.2 %while.1 = (s32[]{:T(128)}, f32[1,256,256]{2,1,0:T(8,128)S(1)}, s32[2,2]{1,0:T(2,128)S(1)}, f32[2,1,128,128]{3,2,1,0:T(8,128)}, s32[]{:T(128)}) while((s32[]{:T(128)}, f32[1,256,256]{2,1,0:T(8,128)S(1)}, s32[2,2]{1,0:T(2,128)S(1)}, f32[2,1,128,128]{3,2,1,0:T(8,128)}, s32[]{:T(128)}) %tuple.30), condition=%wide.while_cond, body=%wide.while_body.sunk | while | flops 2 | bytes 132205 | solution.py:24
  48.7 1.9 bitcast_dynamic-update-slice_fusion.3
  51.2 1.9 bitcast_dynamic-update-slice_fusion.3
  53.1 20.5 %custom-call.27 = f32[1,2,128,128]{2,3,1,0:T(8,128)S(1)} custom-call(f32[1,2,128,128]{3,2,1,0:T(8,128)} %bitcast.124), custom_call_target="InvertDiagBlocksLowerTriangular" | custom-call | tf_op jit(solution)/shard_map/vmap(jit(_cho_solve))/triangular_solve | solution.py:24
  74.6 1.1 fusion.10
  75.7 1.1 fusion.3
  76.9 1.1 fusion.32
  78.0 1.1 fusion.39
  79.1 1.2 convolution_subtract_fusion
  80.3 1.1 convolution_convert_fusion
  81.4 1.7 fusion.1
  83.1 9.2 %gather_fusion = bf16[2048,512]{1,0:T(8,128)(2,1)} fusion(bf16[2304,512]{1,0:T(8,128)(2,1)S(1)} %bitcast.113, s32[2048]{0:T(1024)S(1)} %fusion.33), kind=kCustom, calls=%fused_computation | custom fusion | bytes 4202496 | tf_op jit(solution)/shard_map/jit(_take)/gather | solution.py:39
  92.3 1.9 broadcast_select_fusion
  94.5 2.5 fusion.4
  97.1 3.3 %copy.39 = f32[4,8,64,768]{3,2,0,1:T(8,128)} copy(f32[4,8,64,768]{3,2,1,0:T(8,128)S(1)} %bitcast.117) | data formatting | bytes 12582912 | tf_op jit(solution)/shard_map/reshape | solution.py:50
  100.7 120.5 %reduce-scatter.3.cloned.1.call-done = f32[256,768]{1,0:T(8,128)} async-done(((f32[2048,768]{1,0:T(8,128)}), f32[256,768]{1,0:T(8,128)}) %reduce-scatter.3.cloned.1.call-update) | async-done | bytes 786448 | tf_op jit(solution)/shard_map/reduce_scatter | solution.py:51
  221.3 25.5 %reduce-scatter.5.cloned.1.call-done = f32[1,64,768]{2,1,0:T(8,128)} async-done(((f32[4,64,768]{2,1,0:T(8,128)}), f32[1,64,768]{2,1,0:T(8,128)}) %reduce-scatter.5.cloned.1.call-update) | async-done | bytes 196624 | tf_op jit(solution)/shard_map/reduce_scatter | solution.py:57
  246.8 2.0 slice.78
  248.8 30.8 %all_gather.3 = f32[1,512,128]{2,0,1:T(1,128)S(1)} all-gather(f32[1,64,128]{2,0,1:T(1,128)S(1)} %bitcast.120), channel_id=1, replica_groups=mesh['arc'=8,'coef'=4] {'arc'}, dimensions={1}, use_global_device_ids=true | all-gather | bytes 294912 | tf_op jit(solution)/shard_map/all_gather | solution.py:64
  279.9 11.7 %custom-call.28 = f32[1,128,128]{2,1,0:T(8,128)S(1)} custom-call(f32[1,128,128]{2,1,0:T(8,128)S(1)} %fusion.29), custom_call_target="Cholesky" | custom-call | tf_op jit(solution)/shard_map/vmap(jit(cholesky))/cholesky | solution.py:67
  (56 shorter events, 9.4 us)
Async XLA Ops:
  7.2 214.1 %reduce-scatter.3.cloned.1.call-start = ((), (), s32[]{:S(2)}) async-start(), calls=%async_computation.2 | async-start | bytes 7077888 | tf_op jit(solution)/shard_map/reduce_scatter | solution.py:51
  11.4 62.2 %copy-start.2 = (bf16[1,2304,512]{2,1,0:T(8,128)(2,1)S(1)}, bf16[1,2304,512]{2,1,0:T(8,128)(2,1)}, u32[]{:S(2)}) copy-start(bf16[1,2304,512]{2,1,0:T(8,128)(2,1)} %param.8) | copy-start | bytes 7077892
  11.5 62.2 %copy-start.4 = (bf16[1,256,512]{2,1,0:T(8,128)(2,1)S(1)}, bf16[1,256,512]{2,1,0:T(8,128)(2,1)}, u32[]{:S(2)}) copy-start(bf16[1,256,512]{2,1,0:T(8,128)(2,1)} %param.7) | copy-start | bytes 786436
  79.1 2.3 copy-start.3
  92.3 2.2 copy-start
  100.4 179.4 %copy-start.1 = (f32[1,128]{1,0:T(1,128)S(1)}, f32[1,128]{1,0:T(1,128)}, u32[]{:S(2)}) copy-start(f32[1,128]{1,0:T(1,128)} %param.13) | copy-start | bytes 1540
  100.4 146.4 %reduce-scatter.5.cloned.1.call-start = ((), (), s32[]{:S(2)}) async-start(), calls=%async_computation.3 | async-start | bytes 983040 | tf_op jit(solution)/shard_map/reduce_scatter | solution.py:57
Sparse Core Ops, SparseCore 0:
  100.5 120.6 reduce-scatter.2
  224.3 22.3 reduce-scatter.4
where the time goes:
time: 301 us
  waiting for transfers between devices  146 us (49%)
  other arithmetic  71.8 us (24%)
  blocking collectives  30.8 us (10%)
  local copies, waits for them, and re-layouts  21.6 us (7%)
  between operations  16.2 us (5%)
  matrix products  13.8 us (5%)
    reduce_scatter x1, waiting for transfers between devices, per_device(): lax.psum_scatter(product.reshape(blocks * n_owner * per_arc, product.shap...  121 us
    another operation x6, other arithmetic, reduce_one(): factor = jnp.linalg.cholesky(local_normal)  34.1 us
    all_gather x1, blocking collectives, per_device(): all_rows = lax.all_gather(panel_strip, 'arc', axis=1, tiled=True)  30.8 us
    reduce_scatter x1, waiting for transfers between devices, per_device(): lax.psum_scatter(arc_part.reshape(n_owner, per_arc, arc_part.shape[1]), '...  25.5 us
    another operation x3, other arithmetic, reduce_one(): jax.scipy.linalg.cho_solve((factor, True), coupling).astype(jnp.bfloat16)  20.5 us
    another operation x3, other arithmetic, per_device(): panel_factor = jax.vmap(jnp.linalg.cholesky)(shifted)  12.5 us
    gather x1, local copies, waits for them, and re-layouts, per_device(): jnp.take(reduced, owner_columns, axis=1)  9.16 us
    another operation x6, matrix products, reduce_one(): jax.scipy.linalg.cho_solve((factor, True), coupling).astype(jnp.bfloat16)  6.79 us
  transfers between devices with their start and end apart: 2, of which 2 were waited for; matrix products, arithmetic and copies ran while one was open for 0% of the time, Pallas kernels for 0%

commit v1 on v0

v1 whole, which is shorter than its diff:
```python
import functools

import jax
import jax.numpy as jnp
from jax import lax
from jax.experimental import pallas as pl
from jax.experimental.pallas import tpu as pltpu
from jax.sharding import PartitionSpec as P

OB = 512
KB = 256
P_SIZE = 128
STRIDE = OB // P_SIZE
WIDTH = OB + KB
HALF = WIDTH // 2
PAIR = 2
F16_TOP = 8192.0
INNER = (((1,), (1,)), ((), ()))
AXES = ("arc", "coef")


def reduce_one(local_one, global_one, prior_one, count_one, sense_one):
    row_total = local_one.shape[1]
    row_valid = (lax.iota(jnp.int32, row_total) < count_one).astype(jnp.bfloat16)
    band_cols = jnp.repeat(sense_one, OB)
    column_valid = jnp.concatenate([band_cols, jnp.ones((KB,), jnp.int32)]).astype(jnp.bfloat16)
    local_rows = local_one * row_valid[None, :]
    global_rows = global_one * row_valid[None, :] * column_valid[:, None]
    local_normal = lax.dot_general(
        local_rows, local_rows, INNER, preferred_element_type=jnp.float32
    ) + jnp.diag(prior_one)
    coupling = lax.dot_general(local_rows, global_rows, INNER, preferred_element_type=jnp.float32)
    factor = jnp.linalg.cholesky(local_normal)
    solved = jax.scipy.linalg.cho_solve((factor, True), coupling).astype(jnp.bfloat16)
    removed = lax.dot_general(
        solved, local_rows, (((0,), (0,)), ((), ())), preferred_element_type=jnp.float32
    )
    return (global_rows.astype(jnp.float32) - removed).astype(jnp.bfloat16)


def dot(a, b):
    return lax.dot_general(a, b, INNER, preferred_element_type=jnp.float32)


def product_kernel(n_y, n_z, place_ref, mine_ref, other_ref, prod_ref, panel_ref, left, top):
    z, x = place_ref[0], place_ref[1]
    blocks = n_z * PAIR
    rows = OB // blocks
    border_mine = mine_ref[pl.ds(2 * n_y * OB, KB), :]
    border_other = other_ref[pl.ds(n_y * OB, KB), :]
    pick = lax.broadcasted_iota(jnp.int32, (P_SIZE, OB), 1) == STRIDE * lax.broadcasted_iota(
        jnp.int32, (P_SIZE, OB), 0
    )
    pick = pick.astype(jnp.float32).astype(jnp.bfloat16)
    for y in range(n_y):
        own_mine = mine_ref[pl.ds(y * OB, OB), :]
        own_other = other_ref[pl.ds(y * OB, OB), :]
        for i in range(PAIR):
            for j in range(n_z):
                at = (i * n_z + j) * rows
                source = pl.multiple_of(y * OB + ((z ^ j) * PAIR + (x ^ i)) * rows, rows)
                left[0, pl.ds(at, rows), :] = mine_ref[pl.ds(source, rows), :]
                left[1, pl.ds(at, rows), :] = other_ref[pl.ds(source, rows), :]
        square = dot(left[0], own_mine) + dot(left[1], own_other)
        side = dot(left[0], border_mine) + dot(left[1], border_other)
        prod_ref[y, :, :OB] = square
        prod_ref[y, :, OB:] = side
        largest = jnp.maximum(
            jnp.max(jnp.abs(square), axis=0, keepdims=True).max(axis=1, keepdims=True),
            jnp.max(jnp.abs(side), axis=0, keepdims=True).max(axis=1, keepdims=True),
        )
        largest = jnp.broadcast_to(largest, top.shape)
        top[...] = largest if y == 0 else jnp.maximum(top[...], largest)
        strip_mine = lax.dot_general(
            pick, own_mine, (((1,), (0,)), ((), ())), preferred_element_type=jnp.float32
        ).astype(jnp.bfloat16)
        strip_other = lax.dot_general(
            pick, own_other, (((1,), (0,)), ((), ())), preferred_element_type=jnp.float32
        ).astype(jnp.bfloat16)
        panel_ref[y, :P_SIZE, :] = dot(strip_mine, strip_mine) + dot(strip_other, strip_other)
    for y in range(n_y):
        panel_ref[y, P_SIZE:, :] = top[...]


def products(mine, other, place, n_y, n_z):
    return pl.pallas_call(
        functools.partial(product_kernel, n_y, n_z),
        out_shape=(
            jax.ShapeDtypeStruct((n_y, OB, WIDTH), jnp.float32),
            jax.ShapeDtypeStruct((n_y, P_SIZE + 8, P_SIZE), jnp.float32),
        ),
        in_specs=[
            pl.BlockSpec(memory_space=pltpu.SMEM),
            pl.BlockSpec(memory_space=pltpu.VMEM),
            pl.BlockSpec(memory_space=pltpu.VMEM),
        ],
        out_specs=(
            pl.BlockSpec(memory_space=pltpu.VMEM),
            pl.BlockSpec(memory_space=pltpu.VMEM),
        ),
        scratch_shapes=[
            pltpu.VMEM((2, OB, mine.shape[1]), jnp.bfloat16),
            pltpu.VMEM((8, P_SIZE), jnp.float32),
        ],
        compiler_params=pltpu.CompilerParams(vmem_limit_bytes=48 * 1024 * 1024),
        name="products",
    )(place, mine, other)


def encode(values, bound):
    return (values * (F16_TOP / jnp.maximum(bound, 1e-30))).astype(jnp.float16)


def decode(values, bound):
    return values.astype(jnp.float32) * (bound * (1.0 / F16_TOP))


def per_device(
    local_design, global_design, local_prior, obs_count, band_mask, owner_columns, kaula_prior
):
    n_arc, n_coef = lax.axis_size("arc"), lax.axis_size("coef")
    n_z, n_y = n_arc // PAIR, n_coef // PAIR
    rows = OB // n_arc
    arc, coef = lax.axis_index("arc"), lax.axis_index("coef")
    z, x, y, core = arc // PAIR, arc % PAIR, coef // PAIR, coef % PAIR

    def swap(values, dz=0, dx=0, dy=0, dk=0):
        pairs = []
        for a in range(n_arc):
            for c in range(n_coef):
                to_a = ((a // PAIR) ^ dz) * PAIR + ((a % PAIR) ^ dx)
                to_c = ((c // PAIR) ^ dy) * PAIR + ((c % PAIR) ^ dk)
                pairs.append((a * n_coef + c, to_a * n_coef + to_c))
        return lax.ppermute(values, AXES, pairs)

    reduced = reduce_one(
        local_design[0], global_design[0], local_prior[0], obs_count[0], band_mask[0]
    )
    owners = owner_columns.reshape(n_y, PAIR, OB)
    owners = jnp.take(owners, y ^ jnp.arange(n_y), axis=0, mode="clip")
    owners = jnp.take(owners, core ^ jnp.arange(PAIR), axis=1, mode="clip")
    owners = owners.transpose(1, 0, 2).reshape(-1)
    ordered = reduced.at[owners].get(mode="promise_in_bounds")
    mine = jnp.concatenate([ordered, reduced[n_coef * OB :]], axis=0)
    other = swap(mine[n_y * OB :], dk=1)
    product, panels = products(mine, other, jnp.stack([z, x]), n_y, n_z)

    product = product.reshape(n_y, PAIR, n_z, rows, WIDTH)
    first, second = product[..., :HALF], product[..., HALF:]
    own_top = panels[0, P_SIZE, 0]

    over_y = [None] + [swap(encode(first[j], own_top), dy=j) for j in range(1, n_y)]
    over_x = swap(encode(second[:, 1], own_top), dx=1)
    panel_y = [panels[0]] + [swap(panels[j], dy=j) for j in range(1, n_y)]
    panel_x = [swap(panels[j], dx=1, dy=j) for j in range(n_y)]

    tops_y = [p[P_SIZE, 0] for p in panel_y]
    tops_x = [p[P_SIZE, 0] for p in panel_x]
    first_sum = first[0]
    for j in range(1, n_y):
        first_sum = first_sum + decode(over_y[j], tops_y[j])
    second_sum = second[:, 0] + decode(over_x, tops_x[0])
    panel_sum = functools.reduce(jnp.add, panel_y) + functools.reduce(jnp.add, panel_x)

    first_bound, first_from = sum(tops_y), sum(tops_x)
    over_x = swap(encode(first_sum[1], first_bound), dx=1)
    over_y = [None] + [
        swap(encode(second_sum[j], tops_y[0] + tops_x[0]), dy=j) for j in range(1, n_y)
    ]
    panel_z = [panel_sum] + [swap(panel_sum, dz=j) for j in range(1, n_z)]
    first_sum = first_sum[0] + decode(over_x, first_from)
    second_total = second_sum[0]
    for j in range(1, n_y):
        second_total = second_total + decode(over_y[j], tops_y[j] + tops_x[j])

    total = jnp.concatenate([first_sum, second_total], axis=-1)
    tops_z = [p[P_SIZE, 0] for p in panel_z]
    over_z = [swap(encode(total[j], tops_z[0]), dz=j) for j in range(1, n_z)]
    while len(panel_z) > 1:
        panel_z = [panel_z[2 * i] + panel_z[2 * i + 1] for i in range(len(panel_z) // 2)]
    panel_factor = jnp.linalg.cholesky(panel_z[0][:P_SIZE] + jnp.diag(kaula_prior[0]))
    normal_rows = total[0]
    for j in range(1, n_z):
        normal_rows = normal_rows + decode(over_z[j - 1], tops_z[j])
    return normal_rows[None], panel_factor[None]


def solution(mesh):
    in_specs = (
        P(AXES, None, None),
        P(AXES, None, None),
        P(AXES, None),
        P(AXES),
        P(AXES, None),
        P(),
        P("coef", None),
    )
    out_specs = (P("coef", "arc", None), P("coef", None, None))
    return jax.shard_map(
        per_device, mesh=mesh, in_specs=in_specs, out_specs=out_specs, check_vma=False
    )
```

time: 301 us -> 162 us (0.54)
  waiting for transfers between devices: 146 us -> 10.3 us
  blocking collectives: 30.8 us -> 0 us
  starting transfers between devices: 0.3 us -> 18.1 us
  other arithmetic: 71.8 us -> 79.2 us
  Pallas kernels: 0 us -> 4.55 us
  between operations: 16.2 us -> 12.8 us
  local copies, waits for them, and re-layouts: 21.6 us -> 24.8 us
    reduce_scatter x2 -> x0, waiting for transfers between devices: 146 us -> none  [the longest x1 121 us: per_device(): lax.psum_scatter(product.reshape(blocks * n_owner * per_arc, product.shap...]
    all_gather x1 -> x0, blocking collectives: 30.8 us -> none  [per_device(): all_rows = lax.all_gather(panel_strip, 'arc', axis=1, tiled=True)]
    ppermute x0 -> x14, starting transfers between devices: none -> 18.1 us  [swap(): return lax.ppermute(values, AXES, pairs)]
    ppermute x0 -> x14, waiting for transfers between devices: none -> 10.3 us  [swap(): return lax.ppermute(values, AXES, pairs)]
    slice x2 -> x10, local copies, waits for them, and re-layouts: 2.09 us -> 6.77 us  [the longest x4 3.42 us: per_device(): tops_z = [p[P_SIZE, 0] for p in panel_z]]
    pallas_call x0 -> x1, Pallas kernels: none -> 4.55 us  [products(): pl.pallas_call(functools.partial(product_kernel, n_y, n_z), out_shape=(ja...]
    convert_element_type x0 -> x5, other arithmetic: none -> 4.07 us  [encode(): return (values * (F16_TOP / jnp.maximum(bound, 1e-30))).astype(jnp.float16)]
    concatenate x0 -> x2, other arithmetic: none -> 3.66 us  [per_device(): mine = jnp.concatenate([ordered, reduced[n_coef * OB:]], axis=0)]
  transfers between devices with their start and end apart: 2 -> 14, of which waited for: 2 -> 4; matrix products, arithmetic and copies ran while one was open for 0% -> 15% of each run, Pallas kernels for 0% -> 0%
where the time goes in v1:
time: 162 us; the launch traced here: 161 us
  other arithmetic  79.2 us (49%)
  local copies, waits for them, and re-layouts  24.8 us (15%)
  starting transfers between devices  18.1 us (11%)
  between operations  12.8 us (8%)
  matrix products  11.2 us (7%)
  waiting for transfers between devices  10.3 us (6%)
  Pallas kernels  4.55 us (3%)
    another operation x6, other arithmetic, reduce_one(): factor = jnp.linalg.cholesky(local_normal)  34.2 us
    another operation x3, other arithmetic, reduce_one(): jax.scipy.linalg.cho_solve((factor, True), coupling).astype(jnp.bfloat16)  20.3 us
    ppermute x14, starting transfers between devices, swap(): return lax.ppermute(values, AXES, pairs)  18.1 us
    another operation x3, other arithmetic, per_device(): jnp.linalg.cholesky(panel_z[0][:P_SIZE] + jnp.diag(kaula_prior[0]))  12.5 us
    ppermute x14, waiting for transfers between devices, swap(): return lax.ppermute(values, AXES, pairs)  10.3 us
    gather x1, local copies, waits for them, and re-layouts, per_device(): ordered = reduced.at[owners].get(mode='promise_in_bounds')  9.17 us
    another operation x6, matrix products, reduce_one(): jax.scipy.linalg.cho_solve((factor, True), coupling).astype(jnp.bfloat16)  6.84 us
    pallas_call x1, Pallas kernels, products(): pl.pallas_call(functools.partial(product_kernel, n_y, n_z), out_shape=(ja...  4.55 us
  transfers between devices with their start and end apart: 14, of which 4 were waited for; matrix products, arithmetic and copies ran while one was open for 15% of the time, Pallas kernels for 0%

profile of v1, /device:TPU:0, one launch (start us, length us, event | category | flops | bytes accessed | tf_op | source)
XLA Modules:
  0.0 161.0 jit_solution(5791984400989869127)
XLA Ops:
  7.0 11.7 %cholesky.69 = f32[128,128]{1,0:T(8,128)S(1)} custom-call(f32[128,128]{1,0:T(8,128)S(1)} %cholesky.162), custom_call_target="Cholesky" | custom-call | tf_op jit(solution)/shard_map/jit(cholesky)/cholesky | solution.py:33
  19.0 9.8 %custom-call.21 = f32[1,128,128]{1,2,0:T(8,128)S(1)} custom-call(f32[1,128,128]{2,1,0:T(8,128)S(1)} %copy.38), custom_call_target="InvertDiagBlocksLowerTriangular" | custom-call | tf_op jit(solution)/shard_map/jit(cholesky)/cholesky | solution.py:33
  29.4 11.7 %cholesky.142 = f32[128,128]{1,0:T(8,128)S(1)} custom-call(f32[128,128]{1,0:T(8,128)S(1)} %convolution_subtract_fusion.3), custom_call_target="Cholesky" | custom-call | tf_op jit(solution)/shard_map/jit(cholesky)/cholesky | solution.py:33
  44.0 4.0 %while.1 = (s32[]{:T(128)}, f32[256,256]{1,0:T(8,128)S(1)}, s32[2,2]{1,0:T(2,128)S(1)}, f32[2,128,128]{2,1,0:T(8,128)S(1)}, s32[]{:T(128)}) while((s32[]{:T(128)}, f32[256,256]{1,0:T(8,128)S(1)}, s32[2,2]{1,0:T(2,128)S(1)}, f32[2,128,128]{2,1,0:T(8,128)S(1)}, s32[]{:T(128)}) %tuple.34), condition=%wide.while_cond, body=%wide.while_body.sunk | while | flops 2 | bytes 131189 | solution.py:34
  44.6 1.4 bitcast_dynamic-update-slice_fusion.2
  46.6 1.4 bitcast_dynamic-update-slice_fusion.2
  48.0 19.7 %custom-call.22 = f32[2,128,128]{1,2,0:T(8,128)S(1)} custom-call(f32[2,128,128]{2,1,0:T(8,128)S(1)} %get-tuple-element.13), custom_call_target="InvertDiagBlocksLowerTriangular" | custom-call | tf_op jit(solution)/shard_map/jit(_cho_solve)/triangular_solve | solution.py:34
  75.5 1.7 %fusion = bf16[2304,512]{1,0:T(8,128)(2,1)S(1)} fusion(bf16[1,2304,512]{2,1,0:T(8,128)(2,1)S(1)} %copy-done.7, bf16[128,2304]{1,0:T(8,128)(2,1)S(1)} %get-tuple-element.41, bf16[128,2304]{1,0:T(8,128)(2,1)S(1)} %convolution_convert_fusion, bf16[2304]{0:T(1024)(128)(2,1)S(1)} %concatenate.16, bf16[512]{0:T(512)(128)(2,1)S(1)} %fusion.64, ...), kind=kOutput, calls=%fused_computation.6 | convolution fusion | flops 612368384 | bytes 6166016 | tf_op jit(solution)/shard_map/dot_general | solution.py:35
  77.9 9.2 %gather_fusion.2 = bf16[2048,512]{1,0:T(8,128)(2,1)} fusion(bf16[2304,512]{1,0:T(8,128)(2,1)S(1)} %fusion, s32[2048]{0:T(1024)S(1)} %broadcast_clamp_fusion), kind=kCustom, calls=%fused_computation.2 | custom fusion | bytes 4202496 | tf_op jit(solution)/shard_map/gather | solution.py:143
  87.1 2.6 %fusion.6 = bf16[1280,512]{1,0:T(8,128)(2,1)} fusion(bf16[2048,512]{1,0:T(8,128)(2,1)} %gather_fusion.2, bf16[256,512]{1,0:T(8,128)(2,1)} %slice.197), kind=kLoop, calls=%fused_computation.19 | loop fusion | flops 2621440 | bytes 3670016 | tf_op jit(solution)/shard_map/concatenate | solution.py:144
  91.3 1.7 %collective-permute-done.other_ref = bf16[1280,512]{1,0:T(8,128)(2,1)S(1)} collective-permute-done((bf16[1280,512]{1,0:T(8,128)(2,1)}, bf16[1280,512]{1,0:T(8,128)(2,1)S(1)}, u32[]{:S(2)}, u32[]{:S(2)}) %collective-permute-start) | collective-permute-done | bytes 1310752 | tf_op jit(solution)/shard_map/ppermute | solution.py:134
  93.0 4.6 %products.1 = (f32[2,512,768]{2,1,0:T(8,128)}, f32[2,136,128]{2,1,0:T(8,128)S(1)}) custom-call(s32[2]{0:T(128)S(1)} %pad_add_fusion.place_ref, bf16[2304,512]{1,0:T(8,128)(2,1)S(1)} %pad_maximum_fusion.mine_ref, bf16[1280,512]{1,0:T(8,128)(2,1)S(1)} %collective-permute-done.other_ref), custom_call_target="tpu_custom_call" | custom-call | tf_op jit(solution)/shard_map/products/pallas_call | solution.py:86
  98.2 3.9 %collective-permute-start.5 = (f32[136,128]{0,1:T(8,128)S(1)}, f32[136,128]{0,1:T(8,128)S(1)}, u32[]{:S(2)}, u32[]{:S(2)}) collective-permute-start(f32[136,128]{0,1:T(8,128)S(1)} %get-tuple-element.36), channel_id=1, source_target_pairs={{0,6},{1,7},{2,4},{3,5},{4,2},{5,3},{6,0},{7,1},{8,14},{9,15},{10,... | collective-permute-start | bytes 208904 | tf_op jit(solution)/shard_map/ppermute | solution.py:134
  103.4 2.0 %fusion.20 = f16[2,4,64,384]{3,2,1,0:T(8,128)(2,1)} fusion(f32[2,2,4,64,768]{4,3,2,1,0:T(8,128)} %bitcast.149, f32[]{:T(128)} %bitcast.19), kind=kLoop, calls=%fused_computation.44 | loop fusion | flops 393216 | bytes 1179652 | tf_op jit(solution)/shard_map/convert_element_type | solution.py:111
  105.4 3.6 %collective-permute-done.4 = f32[136,128]{0,1:T(8,128)S(1)} collective-permute-done((f32[136,128]{0,1:T(8,128)S(1)}, f32[136,128]{0,1:T(8,128)S(1)}, u32[]{:S(2)}, u32[]{:S(2)}) %collective-permute-start.4) | collective-permute-done | bytes 69664 | tf_op jit(solution)/shard_map/ppermute | solution.py:134
  109.0 3.7 %collective-permute-start.13 = (f32[136,128]{0,1:T(8,128)S(1)}, f32[136,128]{0,1:T(8,128)S(1)}, u32[]{:S(2)}, u32[]{:S(2)}) collective-permute-start(f32[136,128]{0,1:T(8,128)S(1)} %add_add_fusion), channel_id=1, source_target_pairs={{0,24},{1,25},{2,26},{3,27},{4,28},{5,29},{6,30},{7,31},{8,16},{9,... | collective-permute-start | bytes 208904 | tf_op jit(solution)/shard_map/ppermute | solution.py:134
  113.5 2.0 %fusion.19 = f16[2,4,64,384]{3,2,1,0:T(8,128)(2,1)} fusion(f32[2,2,4,64,768]{4,3,2,1,0:T(8,128)} %bitcast.150, f32[]{:T(128)} %bitcast.19), kind=kLoop, calls=%fused_computation.43 | loop fusion | flops 393216 | bytes 1179652 | tf_op jit(solution)/shard_map/convert_element_type | solution.py:111
  116.0 1.4 collective-permute-start.1
  128.2 11.7 %cholesky.154 = f32[128,128]{1,0:T(8,128)S(1)} custom-call(f32[128,128]{1,0:T(8,128)S(1)} %fusion.58), custom_call_target="Cholesky" | custom-call | tf_op jit(solution)/shard_map/jit(cholesky)/cholesky | solution.py:181
  140.8 1.3 fusion.16
  142.2 1.4 collective-permute-start.3
  144.3 3.6 %collective-permute-done.3 = f16[4,64,384]{2,1,0:T(8,128)(2,1)S(1)} collective-permute-done((f16[4,64,384]{2,1,0:T(8,128)(2,1)S(1)}, f16[4,64,384]{2,1,0:T(8,128)(2,1)S(1)}, u32[]{:S(2)}, u32[]{:S(2)}) %collective-permute-start.3) | collective-permute-done | bytes 196640 | tf_op jit(solution)/shard_map/ppermute | solution.py:134
  148.0 1.4 collective-permute-done.7
  150.8 2.9 %collective-permute-start.10 = (f16[64,768]{1,0:T(8,128)(2,1)S(1)}, f16[64,768]{1,0:T(8,128)(2,1)S(1)}, u32[]{:S(2)}, u32[]{:S(2)}) collective-permute-start(f16[64,768]{1,0:T(8,128)(2,1)S(1)} %get-tuple-element.33), channel_id=1, source_target_pairs={{0,16},{1,17},{2,18},{3,19},{4,20},{5,21},{6,22},{7,23},{8,24},{9,... | collective-permute-start | bytes 294920 | tf_op jit(solution)/shard_map/ppermute | solution.py:134
  (109 shorter events, 34.0 us)
Async XLA Ops:
  5.9 61.8 %copy-start.2 = (bf16[1,256,512]{2,1,0:T(8,128)(2,1)S(1)}, bf16[1,256,512]{2,1,0:T(8,128)(2,1)}, u32[]{:S(2)}) copy-start(bf16[1,256,512]{2,1,0:T(8,128)(2,1)} %param.7) | copy-start | bytes 786436
  5.9 61.8 %copy-start.6 = (bf16[1,2304,512]{2,1,0:T(8,128)(2,1)S(1)}, bf16[1,2304,512]{2,1,0:T(8,128)(2,1)}, u32[]{:S(2)}) copy-start(bf16[1,2304,512]{2,1,0:T(8,128)(2,1)} %param.8) | copy-start | bytes 7077892
  73.2 2.3 %copy-start.7 = (bf16[1,2304,512]{2,1,0:T(8,128)(2,1)S(1)}, bf16[1,2304,512]{2,1,0:T(8,128)(2,1)}, u32[]{:S(2)}) copy-start(bf16[1,2304,512]{2,1,0:T(8,128)(2,1)} %param.8) | copy-start | bytes 7077892
  87.1 3.1 %copy-start = (bf16[2048,512]{1,0:T(8,128)(2,1)S(1)}, bf16[2048,512]{1,0:T(8,128)(2,1)}, u32[]{:S(2)}) copy-start(bf16[2048,512]{1,0:T(8,128)(2,1)} %gather_fusion.2) | copy-start | bytes 6291460
  89.6 3.3 %collective-permute-start = (bf16[1280,512]{1,0:T(8,128)(2,1)}, bf16[1280,512]{1,0:T(8,128)(2,1)S(1)}, u32[]{:S(2)}, u32[]{:S(2)}) collective-permute-start(bf16[1280,512]{1,0:T(8,128)(2,1)} %fusion.6), channel_id=1, source_target_pairs={{0,1},{1,0},{2,3},{3,2},{4,5},{5,4},{6,7},{7,6},{8,9},{9,8},{10,11... | collective-permute-start | bytes 3932168 | tf_op jit(solution)/shard_map/ppermute | solution.py:134
  97.5 30.5 %copy-start.5 = (f32[1,128]{1,0:T(1,128)S(1)}, f32[1,128]{1,0:T(1,128)}, u32[]{:S(2)}) copy-start(f32[1,128]{1,0:T(1,128)} %param.13) | copy-start | bytes 1540
  98.2 42.6 %copy-start.1 = (f32[2,512,768]{2,1,0:T(8,128)S(1)}, f32[2,512,768]{2,1,0:T(8,128)}, u32[]{:S(2)}) copy-start(f32[2,512,768]{2,1,0:T(8,128)} %get-tuple-element.4) | copy-start | bytes 9437188
  98.2 10.8 %collective-permute-start.5 = (f32[136,128]{0,1:T(8,128)S(1)}, f32[136,128]{0,1:T(8,128)S(1)}, u32[]{:S(2)}, u32[]{:S(2)}) collective-permute-start(f32[136,128]{0,1:T(8,128)S(1)} %get-tuple-element.36), channel_id=1, source_target_pairs={{0,6},{1,7},{2,4},{3,5},{4,2},{5,3},{6,0},{7,1},{8,14},{9,15},{10,... | collective-permute-start | bytes 208904 | tf_op jit(solution)/shard_map/ppermute | solution.py:134
  102.1 6.9 %collective-permute-start.2 = (f32[136,128]{0,1:T(8,128)S(1)}, f32[136,128]{0,1:T(8,128)S(1)}, u32[]{:S(2)}, u32[]{:S(2)}) collective-permute-start(f32[136,128]{0,1:T(8,128)S(1)} %get-tuple-element.36), channel_id=1, source_target_pairs={{0,2},{1,3},{2,0},{3,1},{4,6},{5,7},{6,4},{7,5},{8,10},{9,11},{10,... | collective-permute-start | bytes 208904 | tf_op jit(solution)/shard_map/ppermute | solution.py:134
  102.6 6.4 %collective-permute-start.4 = (f32[136,128]{0,1:T(8,128)S(1)}, f32[136,128]{0,1:T(8,128)S(1)}, u32[]{:S(2)}, u32[]{:S(2)}) collective-permute-start(f32[136,128]{0,1:T(8,128)S(1)} %get-tuple-element.35), channel_id=1, source_target_pairs={{0,4},{1,5},{2,6},{3,7},{4,0},{5,1},{6,2},{7,3},{8,12},{9,13},{10,... | collective-permute-start | bytes 208904 | tf_op jit(solution)/shard_map/ppermute | solution.py:134
  109.0 18.3 %collective-permute-start.13 = (f32[136,128]{0,1:T(8,128)S(1)}, f32[136,128]{0,1:T(8,128)S(1)}, u32[]{:S(2)}, u32[]{:S(2)}) collective-permute-start(f32[136,128]{0,1:T(8,128)S(1)} %add_add_fusion), channel_id=1, source_target_pairs={{0,24},{1,25},{2,26},{3,27},{4,28},{5,29},{6,30},{7,31},{8,16},{9,... | collective-permute-start | bytes 208904 | tf_op jit(solution)/shard_map/ppermute | solution.py:134
  112.7 14.7 %collective-permute-start.11 = (f32[136,128]{0,1:T(8,128)S(1)}, f32[136,128]{0,1:T(8,128)S(1)}, u32[]{:S(2)}, u32[]{:S(2)}) collective-permute-start(f32[136,128]{0,1:T(8,128)S(1)} %add_add_fusion), channel_id=1, source_target_pairs={{0,16},{1,17},{2,18},{3,19},{4,20},{5,21},{6,22},{7,23},{8,24},{9,... | collective-permute-start | bytes 208904 | tf_op jit(solution)/shard_map/ppermute | solution.py:134
  112.7 14.7 %collective-permute-start.9 = (f32[136,128]{0,1:T(8,128)S(1)}, f32[136,128]{0,1:T(8,128)S(1)}, u32[]{:S(2)}, u32[]{:S(2)}) collective-permute-start(f32[136,128]{0,1:T(8,128)S(1)} %add_add_fusion), channel_id=1, source_target_pairs={{0,8},{1,9},{2,10},{3,11},{4,12},{5,13},{6,14},{7,15},{8,0},{9,1},... | collective-permute-start | bytes 208904 | tf_op jit(solution)/shard_map/ppermute | solution.py:134
  116.0 24.8 %collective-permute-start.1 = (f16[2,4,64,384]{3,2,1,0:T(8,128)(2,1)}, f16[2,4,64,384]{3,2,1,0:T(8,128)(2,1)}, u32[]{:S(2)}, u32[]{:S(2)}) collective-permute-start(f16[2,4,64,384]{3,2,1,0:T(8,128)(2,1)} %fusion.19), channel_id=1, source_target_pairs={{0,2},{1,3},{2,0},{3,1},{4,6},{5,7},{6,4},{7,5},{8,10},{9,11},{10,... | collective-permute-start | bytes 1179656 | tf_op jit(solution)/shard_map/ppermute | solution.py:134
  117.4 23.4 %collective-permute-start.6 = (f16[2,4,64,384]{3,2,1,0:T(8,128)(2,1)}, f16[2,4,64,384]{3,2,1,0:T(8,128)(2,1)}, u32[]{:S(2)}, u32[]{:S(2)}) collective-permute-start(f16[2,4,64,384]{3,2,1,0:T(8,128)(2,1)} %fusion.20), channel_id=1, source_target_pairs={{0,4},{1,5},{2,6},{3,7},{4,0},{5,1},{6,2},{7,3},{8,12},{9,13},{10,... | collective-permute-start | bytes 1179656 | tf_op jit(solution)/shard_map/ppermute | solution.py:134
  127.4 0.7 copy-start.3
  127.4 0.7 copy-start.4
  142.2 5.7 %collective-permute-start.3 = (f16[4,64,384]{2,1,0:T(8,128)(2,1)S(1)}, f16[4,64,384]{2,1,0:T(8,128)(2,1)S(1)}, u32[]{:S(2)}, u32[]{:S(2)}) collective-permute-start(f16[4,64,384]{2,1,0:T(8,128)(2,1)S(1)} %fusion.32), channel_id=1, source_target_pairs={{0,4},{1,5},{2,6},{3,7},{4,0},{5,1},{6,2},{7,3},{8,12},{9,13},{10,... | collective-permute-start | bytes 589832 | tf_op jit(solution)/shard_map/ppermute | solution.py:134
  143.7 5.7 %collective-permute-start.7 = (f16[4,64,384]{2,1,0:T(8,128)(2,1)S(1)}, f16[4,64,384]{2,1,0:T(8,128)(2,1)S(1)}, u32[]{:S(2)}, u32[]{:S(2)}) collective-permute-start(f16[4,64,384]{2,1,0:T(8,128)(2,1)S(1)} %fusion.33), channel_id=1, source_target_pairs={{0,2},{1,3},{2,0},{3,1},{4,6},{5,7},{6,4},{7,5},{8,10},{9,11},{10,... | collective-permute-start | bytes 589832 | tf_op jit(solution)/shard_map/ppermute | solution.py:134
  149.5 10.7 %collective-permute-start.8 = (f16[64,768]{1,0:T(8,128)(2,1)S(1)}, f16[64,768]{1,0:T(8,128)(2,1)S(1)}, u32[]{:S(2)}, u32[]{:S(2)}) collective-permute-start(f16[64,768]{1,0:T(8,128)(2,1)S(1)} %get-tuple-element.32), channel_id=1, source_target_pairs={{0,8},{1,9},{2,10},{3,11},{4,12},{5,13},{6,14},{7,15},{8,0},{9,1},... | collective-permute-start | bytes 294920 | tf_op jit(solution)/shard_map/ppermute | solution.py:134
  150.8 9.4 %collective-permute-start.10 = (f16[64,768]{1,0:T(8,128)(2,1)S(1)}, f16[64,768]{1,0:T(8,128)(2,1)S(1)}, u32[]{:S(2)}, u32[]{:S(2)}) collective-permute-start(f16[64,768]{1,0:T(8,128)(2,1)S(1)} %get-tuple-element.33), channel_id=1, source_target_pairs={{0,16},{1,17},{2,18},{3,19},{4,20},{5,21},{6,22},{7,23},{8,24},{9,... | collective-permute-start | bytes 294920 | tf_op jit(solution)/shard_map/ppermute | solution.py:134
  153.8 6.5 %collective-permute-start.12 = (f16[64,768]{1,0:T(8,128)(2,1)S(1)}, f16[64,768]{1,0:T(8,128)(2,1)S(1)}, u32[]{:S(2)}, u32[]{:S(2)}) collective-permute-start(f16[64,768]{1,0:T(8,128)(2,1)S(1)} %get-tuple-element.34), channel_id=1, source_target_pairs={{0,24},{1,25},{2,26},{3,27},{4,28},{5,29},{6,30},{7,31},{8,16},{9,... | collective-permute-start | bytes 294920 | tf_op jit(solution)/shard_map/ppermute | solution.py:134

commit v2 on v1

--- a/solution.py
+++ b/solution.py
@@ -18,24 +18,190 @@
 INNER = (((1,), (1,)), ((), ()))
 AXES = ("arc", "coef")
 
-
-def reduce_one(local_one, global_one, prior_one, count_one, sense_one):
-    row_total = local_one.shape[1]
-    row_valid = (lax.iota(jnp.int32, row_total) < count_one).astype(jnp.bfloat16)
-    band_cols = jnp.repeat(sense_one, OB)
-    column_valid = jnp.concatenate([band_cols, jnp.ones((KB,), jnp.int32)]).astype(jnp.bfloat16)
-    local_rows = local_one * row_valid[None, :]
-    global_rows = global_one * row_valid[None, :] * column_valid[:, None]
-    local_normal = lax.dot_general(
-        local_rows, local_rows, INNER, preferred_element_type=jnp.float32
-    ) + jnp.diag(prior_one)
-    coupling = lax.dot_general(local_rows, global_rows, INNER, preferred_element_type=jnp.float32)
-    factor = jnp.linalg.cholesky(local_normal)
-    solved = jax.scipy.linalg.cho_solve((factor, True), coupling).astype(jnp.bfloat16)
-    removed = lax.dot_general(
-        solved, local_rows, (((0,), (0,)), ((), ())), preferred_element_type=jnp.float32
-    )
-    return (global_rows.astype(jnp.float32) - removed).astype(jnp.bfloat16)
+LANES = 128
+BLOCK = 8
+GROUP = 4
+ROWS = (((1,), (0,)), ((), ()))
+COLS = (((0,), (0,)), ((), ()))
+
+
+def mm(a, b, dims=ROWS):
+    return lax.dot_general(a, b, dims, preferred_element_type=jnp.float32)
+
+
+def split3(value):
+    high = value.astype(jnp.bfloat16)
+    rest = value - high.astype(jnp.float32)
+    middle = rest.astype(jnp.bfloat16)
+    low = (rest - middle.astype(jnp.float32)).astype(jnp.bfloat16)
+    return high, middle, low
+
+
+def product_six(a, b):
+    a0, a1, a2 = split3(a)
+    b0, b1, b2 = split3(b)
+    return (mm(a0, b2) + mm(a1, b1) + mm(a2, b0)) + (mm(a0, b1) + mm(a1, b0)) + mm(a0, b0)
+
+
+def product_three(a, b):
+    a0, a1, _ = split3(a)
+    b0, b1, _ = split3(b)
+    return (mm(a0, b1) + mm(a1, b0)) + mm(a0, b0)
+
+
+def row_of(value, i):
+    return jnp.broadcast_to(value[i : i + 1, :], (BLOCK, LANES))
+
+
+def reciprocal(value):
+    guess = pl.reciprocal(value, approx=True)
+    guess = guess * (2.0 - value * guess)
+    return guess * (2.0 - value * guess)
+
+
+def eliminate_group(rows, base):
+    sub = lax.broadcasted_iota(jnp.int32, (BLOCK, LANES), 0)
+    lane = lax.broadcasted_iota(jnp.int32, (BLOCK, LANES), 1)
+    count = len(rows)
+    for q in range(count):
+        half, at = divmod(base + BLOCK * q, LANES)
+        factors = [
+            [
+                jnp.broadcast_to(rows[r][half][:, at + j : at + j + 1], (BLOCK, LANES))
+                for j in range(BLOCK)
+            ]
+            for r in range(count)
+        ]
+        inside = (lane >= at) & (lane < at + BLOCK)
+        unit = (lane - at == sub).astype(jnp.float32)
+        for r in range(count):
+            rows[r][half] = jnp.where(inside, unit if r == q else 0.0, rows[r][half])
+        columns, own = list(factors[q]), rows[q]
+        for i in range(BLOCK):
+            scale = reciprocal(row_of(columns[i], i))
+            pivot = sub == i
+            for h in range(len(own)):
+                scaled = row_of(own[h], i) * scale
+                own[h] = jnp.where(pivot, scaled, own[h] - columns[i] * scaled)
+            for j in range(i + 1, BLOCK):
+                scaled = row_of(columns[j], i) * scale
+                columns[j] = jnp.where(pivot, scaled, columns[j] - columns[i] * scaled)
+        for r in range(count):
+            if r != q:
+                for h in range(len(own)):
+                    value = rows[r][h]
+                    for j in range(BLOCK):
+                        value = value - factors[r][j] * row_of(own[h], j)
+                    rows[r][h] = value
+    return rows
+
+
+def sweep_group(a_ref, base):
+    n = a_ref.shape[0]
+    depth = BLOCK * GROUP
+    before = a_ref[base : base + depth, :]
+    rows = [
+        [
+            a_ref[base + BLOCK * r : base + BLOCK * (r + 1), LANES * h : LANES * (h + 1)]
+            for h in range(n // LANES)
+        ]
+        for r in range(GROUP)
+    ]
+    rows = eliminate_group(rows, base)
+    after = jnp.concatenate([jnp.concatenate(row, axis=1) for row in rows], axis=0)
+    column = lax.broadcasted_iota(jnp.int32, (depth, n), 1)
+    row = lax.broadcasted_iota(jnp.int32, (depth, n), 0)
+    inside = (column >= base) & (column < base + depth)
+    before = jnp.where(inside, jnp.where(column - base == row, -1.0, 0.0), before)
+    after = jnp.where(inside, -after, after)
+    u0, u1, u2 = split3(before)
+    w0, w1, w2 = split3(after)
+    update = mm(
+        jnp.concatenate([u0, u0, u0, u1, u1, u2], axis=0),
+        jnp.concatenate([w0, w1, w2, w0, w1, w0], axis=0),
+        COLS,
+    )
+    row = lax.broadcasted_iota(jnp.int32, (n, n), 0)
+    column = lax.broadcasted_iota(jnp.int32, (n, n), 1)
+    outside = ((row < base) | (row >= base + depth)) & ((column < base) | (column >= base + depth))
+    a_ref[...] = jnp.where(outside, a_ref[...], 0.0) - update
+
+
+def local_kernel(
+    n_y, place_ref, count_ref, band_ref, owner_ref, local_ref, global_ref, prior_ref,
+    out_ref, work_ref, normal_ref, rows_ref,
+):
+    n, m = local_ref.shape
+    owned = n_y * PAIR * OB
+    y, core, count = place_ref[2], place_ref[3], count_ref[0]
+    used = lax.broadcasted_iota(jnp.int32, (n, m), 1) < count
+    rows_ref[...] = jnp.where(used, local_ref[...].astype(jnp.float32), 0.0).astype(jnp.bfloat16)
+    local_rows = rows_ref[...]
+    row = lax.broadcasted_iota(jnp.int32, (n, n), 0)
+    column = lax.broadcasted_iota(jnp.int32, (n, n), 1)
+    prior = jnp.broadcast_to(prior_ref[...], (n, n))
+    normal = mm(local_rows, local_rows, INNER) + jnp.where(row == column, prior, 0.0)
+    work_ref[...] = normal
+    normal_ref[...] = normal
+
+    lane = lax.broadcasted_iota(jnp.int32, (LANES, LANES), 1)
+    used = lax.broadcasted_iota(jnp.int32, (LANES, m), 1) < count
+
+    def gather_rows(t):
+        position, part = divmod(t * LANES, OB)
+        core_away, y_away = divmod(position, n_y)
+        owner = (y ^ y_away) * PAIR + (core ^ core_away)
+        wanted = owner_ref[owner, part // LANES : part // LANES + 1, :]
+        wanted = jnp.broadcast_to(wanted.astype(jnp.float32), (LANES, LANES)).T.astype(jnp.int32)
+        hot = []
+        for k in range(owned // LANES):
+            sensed = band_ref[0, k * LANES // OB].astype(jnp.float32)
+            hot.append(jnp.where(wanted == lane + k * LANES, sensed, 0.0).astype(jnp.bfloat16))
+        got = mm(jnp.concatenate(hot, axis=1), global_ref[0:owned, :])
+        out_ref[t * LANES : (t + 1) * LANES, :] = jnp.where(used, got, 0.0).astype(jnp.bfloat16)
+
+    steps = n // (BLOCK * GROUP)
+    tiles = owned // LANES
+    for p in range(steps):
+        sweep_group(work_ref, p * BLOCK * GROUP)
+        for t in range(p * tiles // steps, (p + 1) * tiles // steps):
+            gather_rows(t)
+    used = lax.broadcasted_iota(jnp.int32, (KB, m), 1) < count
+    border = global_ref[owned:, :].astype(jnp.float32)
+    out_ref[owned:, :] = jnp.where(used, border, 0.0).astype(jnp.bfloat16)
+
+    inverse = -work_ref[...]
+    local_rows = rows_ref[...]
+    i0, i1, i2 = split3(inverse)
+    gain = mm(i2, local_rows) + mm(i1, local_rows) + mm(i0, local_rows)
+    left = local_rows.astype(jnp.float32) - product_six(normal_ref[...], gain)
+    gain = gain + product_three(inverse, left)
+    g0, g1, g2 = split3(gain)
+    for t in range((owned + KB) // KB):
+        tile = out_ref[t * KB : (t + 1) * KB, :]
+        solved = (mm(tile, g2, INNER) + mm(tile, g1, INNER) + mm(tile, g0, INNER)).astype(jnp.bfloat16)
+        out_ref[t * KB : (t + 1) * KB, :] = (
+            tile.astype(jnp.float32) - mm(solved, local_rows)
+        ).astype(jnp.bfloat16)
+
+
+def reduce_rows(place, count, band, owners, local_rows, global_rows, prior, n_y):
+    n, m = local_rows.shape
+    scalar = pl.BlockSpec(memory_space=pltpu.SMEM)
+    array = pl.BlockSpec(memory_space=pltpu.VMEM)
+    return pl.pallas_call(
+        functools.partial(local_kernel, n_y),
+        out_shape=jax.ShapeDtypeStruct(global_rows.shape, jnp.bfloat16),
+        in_specs=[scalar, scalar, scalar, array, array, array, array],
+        out_specs=array,
+        scratch_shapes=[
+            pltpu.VMEM((n, n), jnp.float32),
+            pltpu.VMEM((n, n), jnp.float32),
+            pltpu.VMEM((n, m), jnp.bfloat16),
+        ],
+        compiler_params=pltpu.CompilerParams(vmem_limit_bytes=48 * 1024 * 1024),
+        name="reduce_rows",
+    )(place, count, band, owners, local_rows, global_rows, prior)
 
 
 def dot(a, b):
@@ -133,17 +299,19 @@
                 pairs.append((a * n_coef + c, to_a * n_coef + to_c))
         return lax.ppermute(values, AXES, pairs)
 
-    reduced = reduce_one(
-        local_design[0], global_design[0], local_prior[0], obs_count[0], band_mask[0]
-    )
-    owners = owner_columns.reshape(n_y, PAIR, OB)
-    owners = jnp.take(owners, y ^ jnp.arange(n_y), axis=0, mode="clip")
-    owners = jnp.take(owners, core ^ jnp.arange(PAIR), axis=1, mode="clip")
-    owners = owners.transpose(1, 0, 2).reshape(-1)
-    ordered = reduced.at[owners].get(mode="promise_in_bounds")
-    mine = jnp.concatenate([ordered, reduced[n_coef * OB :]], axis=0)
+    place = jnp.stack([z, x, y, core])
+    mine = reduce_rows(
+        place,
+        obs_count,
+        band_mask,
+        owner_columns.reshape(n_coef, OB // LANES, LANES),
+        local_design[0],
+        global_design[0],
+        local_prior,
+        n_y,
+    )
     other = swap(mine[n_y * OB :], dk=1)
-    product, panels = products(mine, other, jnp.stack([z, x]), n_y, n_z)
+    product, panels = products(mine, other, place, n_y, n_z)
 
     product = product.reshape(n_y, PAIR, n_z, rows, WIDTH)
     first, second = product[..., :HALF], product[..., HALF:]

time: 162 us -> 96.8 us (0.60)
  other arithmetic: 79.2 us -> 19.5 us
  Pallas kernels: 4.55 us -> 23.4 us
  local copies, waits for them, and re-layouts: 24.8 us -> 12.5 us
  matrix products: 11.2 us -> 0 us
    another operation x11 -> x1, other arithmetic: 55.1 us -> 0.08 us  [per_device(): place = jnp.stack([z, x, y, core])]
    pallas_call x0 -> x1, Pallas kernels: none -> 18.8 us  [reduce_rows(): pl.pallas_call(functools.partial(local_kernel, n_y), out_shape=jax.ShapeD...]
    gather x4 -> x0, local copies, waits for them, and re-layouts: 10.3 us -> none  [the longest x1 9.17 us: per_device(): ordered = reduced.at[owners].get(mode='promise_in_bounds')]
    another operation x8 -> x0, matrix products: 7.31 us -> none  [the longest x6 6.84 us: reduce_one(): jax.scipy.linalg.cho_solve((factor, True), coupling).astype(jnp.bfloat16)]
    another operation x13 -> x0, local copies, waits for them, and re-layouts: 4.94 us -> none
    unnamed x19, local copies, waits for them, and re-layouts: 1.53 us -> 6.05 us
    dot_general x3 -> x0, matrix products: 3.87 us -> none  [the longest x1 1.67 us: reduce_one(): lax.dot_general(solved, local_rows, (((0,), (0,)), ((), ())), preferred_e...]
    concatenate x2 -> x0, other arithmetic: 3.66 us -> none  [per_device(): mine = jnp.concatenate([ordered, reduced[n_coef * OB:]], axis=0)]
  transfers between devices with their start and end apart: 14 -> 14, of which waited for: 4 -> 5; matrix products, arithmetic and copies ran while one was open for 15% -> 24% of each run, Pallas kernels for 0% -> 0%
where the time goes in v2:
time: 96.8 us; the launch traced here: 96.2 us
  Pallas kernels  23.4 us (24%)
  other arithmetic  19.5 us (20%)
  starting transfers between devices  18.1 us (19%)
  local copies, waits for them, and re-layouts  12.5 us (13%)
  waiting for transfers between devices  11.4 us (12%)
  between operations  11.3 us (12%)
    pallas_call x1, Pallas kernels, reduce_rows(): pl.pallas_call(functools.partial(local_kernel, n_y), out_shape=jax.ShapeD...  18.8 us
    ppermute x14, starting transfers between devices, swap(): return lax.ppermute(values, AXES, pairs)  18.1 us
    another operation x3, other arithmetic, per_device(): jnp.linalg.cholesky(panel_z[0][:P_SIZE] + jnp.diag(kaula_prior[0]))  12.5 us
    ppermute x14, waiting for transfers between devices, swap(): return lax.ppermute(values, AXES, pairs)  11.4 us
    unnamed x19, local copies, waits for them, and re-layouts  6.05 us
    pallas_call x1, Pallas kernels, products(): pl.pallas_call(functools.partial(product_kernel, n_y, n_z), out_shape=(ja...  4.55 us
    convert_element_type x5, other arithmetic, encode(): return (values * (F16_TOP / jnp.maximum(bound, 1e-30))).astype(jnp.float16)  4.07 us
    slice x4, local copies, waits for them, and re-layouts, per_device(): tops_z = [p[P_SIZE, 0] for p in panel_z]  3.42 us
  transfers between devices with their start and end apart: 14, of which 5 were waited for; matrix products, arithmetic and copies ran while one was open for 24% of the time, Pallas kernels for 0%

profile of v2, /device:TPU:0, one launch (start us, length us, event | category | flops | bytes accessed | tf_op | source)
XLA Modules:
  0.0 96.2 jit_solution(16642808400827533979)
XLA Ops:
  1.4 1.7 %copy-done = bf16[1,2304,512]{2,1,0:T(8,128)(2,1)S(1)} copy-done((bf16[1,2304,512]{2,1,0:T(8,128)(2,1)S(1)}, bf16[1,2304,512]{2,1,0:T(8,128)(2,1)}, u32[]{:S(2)}) %copy-start) | copy-done | bytes 2359320
  3.1 0.9 copy-done.1
  4.0 0.7 copy-done.2
  6.0 18.8 %reduce_rows.1.mine_ref = bf16[2304,512]{1,0:T(8,128)(2,1)S(1)} custom-call(s32[4]{0:T(128)S(1)} %pad_add_fusion.place_ref, s32[1]{0:T(128)S(6)} %copy.19.count_ref, s32[1,4]{1,0:T(1,128)S(1)} %copy-done.4, s32[4,4,128]{2,1,0:T(4,128)S(1)} %bitcast.86, bf16[256,512]{1,0:T(8,128)(2,1)S(1)} %bitcast.85, bf16[2304,512]{1,0:T(8,128)(2,1)S(1)} %bitcast.84, ...), custom_call_target="tpu_custom_call" | custom-call | tf_op jit(solution)/shard_map/reduce_rows/pallas_call | solution.py:192
  25.5 2.7 %collective-permute-done.other_ref = bf16[1280,512]{1,0:T(8,128)(2,1)S(1)} collective-permute-done((bf16[1280,512]{1,0:T(8,128)(2,1)S(1)}, bf16[1280,512]{1,0:T(8,128)(2,1)S(1)}, u32[]{:S(2)}, u32[]{:S(2)}) %collective-permute-start) | collective-permute-done | bytes 1310752 | tf_op jit(solution)/shard_map/ppermute | solution.py:300
  28.2 4.5 %products.1 = (f32[2,512,768]{2,1,0:T(8,128)}, f32[2,136,128]{2,1,0:T(8,128)S(1)}) custom-call(s32[4]{0:T(128)S(1)} %pad_add_fusion.place_ref, bf16[2304,512]{1,0:T(8,128)(2,1)S(1)} %reduce_rows.1.mine_ref, bf16[1280,512]{1,0:T(8,128)(2,1)S(1)} %collective-permute-done.other_ref), custom_call_target="tpu_custom_call" | custom-call | tf_op jit(solution)/shard_map/products/pallas_call | solution.py:252
  33.4 3.9 %collective-permute-start.5 = (f32[136,128]{0,1:T(8,128)S(1)}, f32[136,128]{0,1:T(8,128)S(1)}, u32[]{:S(2)}, u32[]{:S(2)}) collective-permute-start(f32[136,128]{0,1:T(8,128)S(1)} %get-tuple-element.14), channel_id=1, source_target_pairs={{0,6},{1,7},{2,4},{3,5},{4,2},{5,3},{6,0},{7,1},{8,14},{9,15},{10,... | collective-permute-start | bytes 208904 | tf_op jit(solution)/shard_map/ppermute | solution.py:300
  38.6 2.0 %fusion.6 = f16[2,4,64,384]{3,2,1,0:T(8,128)(2,1)} fusion(f32[2,2,4,64,768]{4,3,2,1,0:T(8,128)} %bitcast.87, f32[]{:T(128)} %bitcast.9), kind=kLoop, calls=%fused_computation.16 | loop fusion | flops 393216 | bytes 1179652 | tf_op jit(solution)/shard_map/convert_element_type | solution.py:277
  40.6 3.6 %collective-permute-done.4 = f32[136,128]{0,1:T(8,128)S(1)} collective-permute-done((f32[136,128]{0,1:T(8,128)S(1)}, f32[136,128]{0,1:T(8,128)S(1)}, u32[]{:S(2)}, u32[]{:S(2)}) %collective-permute-start.4) | collective-permute-done | bytes 69664 | tf_op jit(solution)/shard_map/ppermute | solution.py:300
  44.2 3.6 %collective-permute-start.13 = (f32[136,128]{0,1:T(8,128)S(1)}, f32[136,128]{0,1:T(8,128)S(1)}, u32[]{:S(2)}, u32[]{:S(2)}) collective-permute-start(f32[136,128]{0,1:T(8,128)S(1)} %add_add_fusion), channel_id=1, source_target_pairs={{0,24},{1,25},{2,26},{3,27},{4,28},{5,29},{6,30},{7,31},{8,16},{9,... | collective-permute-start | bytes 208904 | tf_op jit(solution)/shard_map/ppermute | solution.py:300
  47.9 0.8 collective-permute-start.9
  48.7 2.0 %fusion.5 = f16[2,4,64,384]{3,2,1,0:T(8,128)(2,1)} fusion(f32[2,2,4,64,768]{4,3,2,1,0:T(8,128)} %bitcast.88, f32[]{:T(128)} %bitcast.9), kind=kLoop, calls=%fused_computation.15 | loop fusion | flops 393216 | bytes 1179652 | tf_op jit(solution)/shard_map/convert_element_type | solution.py:277
  51.2 1.4 %collective-permute-start.1 = (f16[2,4,64,384]{3,2,1,0:T(8,128)(2,1)}, f16[2,4,64,384]{3,2,1,0:T(8,128)(2,1)}, u32[]{:S(2)}, u32[]{:S(2)}) collective-permute-start(f16[2,4,64,384]{3,2,1,0:T(8,128)(2,1)} %fusion.5), channel_id=1, source_target_pairs={{0,2},{1,3},{2,0},{3,1},{4,6},{5,7},{6,4},{7,5},{8,10},{9,11},{10,... | collective-permute-start | bytes 1179656 | tf_op jit(solution)/shard_map/ppermute | solution.py:300
  63.4 11.7 %cholesky.19 = f32[128,128]{1,0:T(8,128)S(1)} custom-call(f32[128,128]{1,0:T(8,128)S(1)} %fusion.32), custom_call_target="Cholesky" | custom-call | tf_op jit(solution)/shard_map/jit(cholesky)/cholesky | solution.py:349
  76.0 1.4 %fusion.2 = (f32[2,4,64,384]{3,2,1,0:T(8,128)S(1)}, f32[2,4,64,384]{3,2,1,0:T(8,128)S(1)}) fusion(f32[2,2,4,64,768]{4,3,2,1,0:T(8,128)S(1)} %bitcast.89, f16[2,4,64,384]{3,2,1,0:T(8,128)(2,1)} %collective-permute-done.6, f32[]{:T(128)} %bitcast.20, f32[]{:T(128)} %bitcast.12, f16[2,4,64,384]{3,2,1,0:T(8,128)(2,1)} %collective-permute-done.1), kind=kLoop, calls=%fused_computation.10 | loop fusion | flops 1179648 | bytes 3932168 | tf_op jit(solution)/shard_map/add | solution.py:330
  77.4 1.4 %collective-permute-start.3 = (f16[4,64,384]{2,1,0:T(8,128)(2,1)S(1)}, f16[4,64,384]{2,1,0:T(8,128)(2,1)S(1)}, u32[]{:S(2)}, u32[]{:S(2)}) collective-permute-start(f16[4,64,384]{2,1,0:T(8,128)(2,1)S(1)} %fusion.11), channel_id=1, source_target_pairs={{0,4},{1,5},{2,6},{3,7},{4,0},{5,1},{6,2},{7,3},{8,12},{9,13},{10,... | collective-permute-start | bytes 589832 | tf_op jit(solution)/shard_map/ppermute | solution.py:300
  79.5 3.6 %collective-permute-done.3 = f16[4,64,384]{2,1,0:T(8,128)(2,1)S(1)} collective-permute-done((f16[4,64,384]{2,1,0:T(8,128)(2,1)S(1)}, f16[4,64,384]{2,1,0:T(8,128)(2,1)S(1)}, u32[]{:S(2)}, u32[]{:S(2)}) %collective-permute-start.3) | collective-permute-done | bytes 196640 | tf_op jit(solution)/shard_map/ppermute | solution.py:300
  83.2 1.4 %collective-permute-done.7 = f16[4,64,384]{2,1,0:T(8,128)(2,1)S(1)} collective-permute-done((f16[4,64,384]{2,1,0:T(8,128)(2,1)S(1)}, f16[4,64,384]{2,1,0:T(8,128)(2,1)S(1)}, u32[]{:S(2)}, u32[]{:S(2)}) %collective-permute-start.7) | collective-permute-done | bytes 196640 | tf_op jit(solution)/shard_map/ppermute | solution.py:300
  84.7 1.3 %collective-permute-start.8 = (f16[64,768]{1,0:T(8,128)(2,1)S(1)}, f16[64,768]{1,0:T(8,128)(2,1)S(1)}, u32[]{:S(2)}, u32[]{:S(2)}) collective-permute-start(f16[64,768]{1,0:T(8,128)(2,1)S(1)} %get-tuple-element.10), channel_id=1, source_target_pairs={{0,8},{1,9},{2,10},{3,11},{4,12},{5,13},{6,14},{7,15},{8,0},{9,1},... | collective-permute-start | bytes 294920 | tf_op jit(solution)/shard_map/ppermute | solution.py:300
  86.0 2.9 %collective-permute-start.10 = (f16[64,768]{1,0:T(8,128)(2,1)S(1)}, f16[64,768]{1,0:T(8,128)(2,1)S(1)}, u32[]{:S(2)}, u32[]{:S(2)}) collective-permute-start(f16[64,768]{1,0:T(8,128)(2,1)S(1)} %get-tuple-element.11), channel_id=1, source_target_pairs={{0,16},{1,17},{2,18},{3,19},{4,20},{5,21},{6,22},{7,23},{8,24},{9,... | collective-permute-start | bytes 294920 | tf_op jit(solution)/shard_map/ppermute | solution.py:300
  90.9 1.2 %slice.137 = f32[1,1]{0,1:T(1,128)} slice(f32[136,128]{0,1:T(8,128)} %copy-done.6), slice={[128:129], [0:1]} | slice | bytes 8 | tf_op jit(solution)/shard_map/slice | solution.py:345
  92.8 1.2 %slice.134 = f32[1,1]{0,1:T(1,128)} slice(f32[136,128]{0,1:T(8,128)} %copy-done.7), slice={[128:129], [0:1]} | slice | bytes 8 | tf_op jit(solution)/shard_map/slice | solution.py:345
  94.6 0.7 copy.16
  95.5 0.7 fusion.21
  (56 shorter events, 10.7 us)
Async XLA Ops:
  1.4 1.7 %copy-start = (bf16[1,2304,512]{2,1,0:T(8,128)(2,1)S(1)}, bf16[1,2304,512]{2,1,0:T(8,128)(2,1)}, u32[]{:S(2)}) copy-start(bf16[1,2304,512]{2,1,0:T(8,128)(2,1)} %param.8) | copy-start | bytes 7077892
  3.1 0.9 copy-start.1
  4.0 0.7 copy-start.2
  4.7 0.7 copy-start.3
  5.4 0.7 copy-start.4
  25.0 38.3 %copy-start.8 = (f32[1,128]{1,0:T(1,128)S(1)}, f32[1,128]{1,0:T(1,128)}, u32[]{:S(2)}) copy-start(f32[1,128]{1,0:T(1,128)} %param.13) | copy-start | bytes 1540
  25.0 3.2 %collective-permute-start = (bf16[1280,512]{1,0:T(8,128)(2,1)S(1)}, bf16[1280,512]{1,0:T(8,128)(2,1)S(1)}, u32[]{:S(2)}, u32[]{:S(2)}) collective-permute-start(bf16[1280,512]{1,0:T(8,128)(2,1)S(1)} %slice.114), channel_id=1, source_target_pairs={{0,1},{1,0},{2,3},{3,2},{4,5},{5,4},{6,7},{7,6},{8,9},{9,8},{10,11... | collective-permute-start | bytes 3932168 | tf_op jit(solution)/shard_map/ppermute | solution.py:300
  32.7 43.3 %copy-start.5 = (f32[2,512,768]{2,1,0:T(8,128)S(1)}, f32[2,512,768]{2,1,0:T(8,128)}, u32[]{:S(2)}) copy-start(f32[2,512,768]{2,1,0:T(8,128)} %get-tuple-element.4) | copy-start | bytes 9437188
  33.4 10.8 %collective-permute-start.5 = (f32[136,128]{0,1:T(8,128)S(1)}, f32[136,128]{0,1:T(8,128)S(1)}, u32[]{:S(2)}, u32[]{:S(2)}) collective-permute-start(f32[136,128]{0,1:T(8,128)S(1)} %get-tuple-element.14), channel_id=1, source_target_pairs={{0,6},{1,7},{2,4},{3,5},{4,2},{5,3},{6,0},{7,1},{8,14},{9,15},{10,... | collective-permute-start | bytes 208904 | tf_op jit(solution)/shard_map/ppermute | solution.py:300
  37.3 6.9 %collective-permute-start.2 = (f32[136,128]{0,1:T(8,128)S(1)}, f32[136,128]{0,1:T(8,128)S(1)}, u32[]{:S(2)}, u32[]{:S(2)}) collective-permute-start(f32[136,128]{0,1:T(8,128)S(1)} %get-tuple-element.14), channel_id=1, source_target_pairs={{0,2},{1,3},{2,0},{3,1},{4,6},{5,7},{6,4},{7,5},{8,10},{9,11},{10,... | collective-permute-start | bytes 208904 | tf_op jit(solution)/shard_map/ppermute | solution.py:300
  37.8 6.4 %collective-permute-start.4 = (f32[136,128]{0,1:T(8,128)S(1)}, f32[136,128]{0,1:T(8,128)S(1)}, u32[]{:S(2)}, u32[]{:S(2)}) collective-permute-start(f32[136,128]{0,1:T(8,128)S(1)} %get-tuple-element.13), channel_id=1, source_target_pairs={{0,4},{1,5},{2,6},{3,7},{4,0},{5,1},{6,2},{7,3},{8,12},{9,13},{10,... | collective-permute-start | bytes 208904 | tf_op jit(solution)/shard_map/ppermute | solution.py:300
  44.2 18.3 %collective-permute-start.13 = (f32[136,128]{0,1:T(8,128)S(1)}, f32[136,128]{0,1:T(8,128)S(1)}, u32[]{:S(2)}, u32[]{:S(2)}) collective-permute-start(f32[136,128]{0,1:T(8,128)S(1)} %add_add_fusion), channel_id=1, source_target_pairs={{0,24},{1,25},{2,26},{3,27},{4,28},{5,29},{6,30},{7,31},{8,16},{9,... | collective-permute-start | bytes 208904 | tf_op jit(solution)/shard_map/ppermute | solution.py:300
  47.9 14.7 %collective-permute-start.11 = (f32[136,128]{0,1:T(8,128)S(1)}, f32[136,128]{0,1:T(8,128)S(1)}, u32[]{:S(2)}, u32[]{:S(2)}) collective-permute-start(f32[136,128]{0,1:T(8,128)S(1)} %add_add_fusion), channel_id=1, source_target_pairs={{0,16},{1,17},{2,18},{3,19},{4,20},{5,21},{6,22},{7,23},{8,24},{9,... | collective-permute-start | bytes 208904 | tf_op jit(solution)/shard_map/ppermute | solution.py:300
  47.9 14.7 %collective-permute-start.9 = (f32[136,128]{0,1:T(8,128)S(1)}, f32[136,128]{0,1:T(8,128)S(1)}, u32[]{:S(2)}, u32[]{:S(2)}) collective-permute-start(f32[136,128]{0,1:T(8,128)S(1)} %add_add_fusion), channel_id=1, source_target_pairs={{0,8},{1,9},{2,10},{3,11},{4,12},{5,13},{6,14},{7,15},{8,0},{9,1},... | collective-permute-start | bytes 208904 | tf_op jit(solution)/shard_map/ppermute | solution.py:300
  51.2 24.8 %collective-permute-start.1 = (f16[2,4,64,384]{3,2,1,0:T(8,128)(2,1)}, f16[2,4,64,384]{3,2,1,0:T(8,128)(2,1)}, u32[]{:S(2)}, u32[]{:S(2)}) collective-permute-start(f16[2,4,64,384]{3,2,1,0:T(8,128)(2,1)} %fusion.5), channel_id=1, source_target_pairs={{0,2},{1,3},{2,0},{3,1},{4,6},{5,7},{6,4},{7,5},{8,10},{9,11},{10,... | collective-permute-start | bytes 1179656 | tf_op jit(solution)/shard_map/ppermute | solution.py:300
  52.6 23.4 %collective-permute-start.6 = (f16[2,4,64,384]{3,2,1,0:T(8,128)(2,1)}, f16[2,4,64,384]{3,2,1,0:T(8,128)(2,1)}, u32[]{:S(2)}, u32[]{:S(2)}) collective-permute-start(f16[2,4,64,384]{3,2,1,0:T(8,128)(2,1)} %fusion.6), channel_id=1, source_target_pairs={{0,4},{1,5},{2,6},{3,7},{4,0},{5,1},{6,2},{7,3},{8,12},{9,13},{10,... | collective-permute-start | bytes 1179656 | tf_op jit(solution)/shard_map/ppermute | solution.py:300
  62.6 0.7 copy-start.6
  62.6 0.7 copy-start.7
  77.4 5.7 %collective-permute-start.3 = (f16[4,64,384]{2,1,0:T(8,128)(2,1)S(1)}, f16[4,64,384]{2,1,0:T(8,128)(2,1)S(1)}, u32[]{:S(2)}, u32[]{:S(2)}) collective-permute-start(f16[4,64,384]{2,1,0:T(8,128)(2,1)S(1)} %fusion.11), channel_id=1, source_target_pairs={{0,4},{1,5},{2,6},{3,7},{4,0},{5,1},{6,2},{7,3},{8,12},{9,13},{10,... | collective-permute-start | bytes 589832 | tf_op jit(solution)/shard_map/ppermute | solution.py:300
  78.9 5.7 %collective-permute-start.7 = (f16[4,64,384]{2,1,0:T(8,128)(2,1)S(1)}, f16[4,64,384]{2,1,0:T(8,128)(2,1)S(1)}, u32[]{:S(2)}, u32[]{:S(2)}) collective-permute-start(f16[4,64,384]{2,1,0:T(8,128)(2,1)S(1)} %fusion.12), channel_id=1, source_target_pairs={{0,2},{1,3},{2,0},{3,1},{4,6},{5,7},{6,4},{7,5},{8,10},{9,11},{10,... | collective-permute-start | bytes 589832 | tf_op jit(solution)/shard_map/ppermute | solution.py:300
  84.7 10.6 %collective-permute-start.8 = (f16[64,768]{1,0:T(8,128)(2,1)S(1)}, f16[64,768]{1,0:T(8,128)(2,1)S(1)}, u32[]{:S(2)}, u32[]{:S(2)}) collective-permute-start(f16[64,768]{1,0:T(8,128)(2,1)S(1)} %get-tuple-element.10), channel_id=1, source_target_pairs={{0,8},{1,9},{2,10},{3,11},{4,12},{5,13},{6,14},{7,15},{8,0},{9,1},... | collective-permute-start | bytes 294920 | tf_op jit(solution)/shard_map/ppermute | solution.py:300
  86.0 9.3 %collective-permute-start.10 = (f16[64,768]{1,0:T(8,128)(2,1)S(1)}, f16[64,768]{1,0:T(8,128)(2,1)S(1)}, u32[]{:S(2)}, u32[]{:S(2)}) collective-permute-start(f16[64,768]{1,0:T(8,128)(2,1)S(1)} %get-tuple-element.11), channel_id=1, source_target_pairs={{0,16},{1,17},{2,18},{3,19},{4,20},{5,21},{6,22},{7,23},{8,24},{9,... | collective-permute-start | bytes 294920 | tf_op jit(solution)/shard_map/ppermute | solution.py:300
  88.9 6.5 %collective-permute-start.12 = (f16[64,768]{1,0:T(8,128)(2,1)S(1)}, f16[64,768]{1,0:T(8,128)(2,1)S(1)}, u32[]{:S(2)}, u32[]{:S(2)}) collective-permute-start(f16[64,768]{1,0:T(8,128)(2,1)S(1)} %get-tuple-element.12), channel_id=1, source_target_pairs={{0,24},{1,25},{2,26},{3,27},{4,28},{5,29},{6,30},{7,31},{8,16},{9,... | collective-permute-start | bytes 294920 | tf_op jit(solution)/shard_map/ppermute | solution.py:300

commit v3 on v2

v3 whole, which is shorter than its diff:
```python
import functools

import jax
import jax.numpy as jnp
from jax import lax
from jax.experimental import pallas as pl
from jax.experimental.pallas import tpu as pltpu
from jax.sharding import PartitionSpec as P

OB = 512
KB = 256
P_SIZE = 128
STRIDE = OB // P_SIZE
WIDTH = OB + KB
HALF = WIDTH // 2
PAIR = 2
TOP_LEVEL = 12.0
HEAD = 16
INNER = (((1,), (1,)), ((), ()))
AXES = ("arc", "coef")

LANES = 128
BLOCK = 8
GROUP = 2
FACTOR_GROUP = 4
FIRST = 4
ROWS = (((1,), (0,)), ((), ()))
COLS = (((0,), (0,)), ((), ()))


def mm(a, b, dims=ROWS):
    return lax.dot_general(a, b, dims, preferred_element_type=jnp.float32)


def split3(value):
    high = value.astype(jnp.bfloat16)
    rest = value - high.astype(jnp.float32)
    middle = rest.astype(jnp.bfloat16)
    low = (rest - middle.astype(jnp.float32)).astype(jnp.bfloat16)
    return high, middle, low


def product_six(a, b):
    a0, a1, a2 = split3(a)
    b0, b1, b2 = split3(b)
    return (mm(a0, b2) + mm(a1, b1) + mm(a2, b0)) + (mm(a0, b1) + mm(a1, b0)) + mm(a0, b0)


def product_three(a, b):
    a0, a1, _ = split3(a)
    b0, b1, _ = split3(b)
    return (mm(a0, b1) + mm(a1, b0)) + mm(a0, b0)


def row_of(value, i):
    return jnp.broadcast_to(value[i : i + 1, :], (BLOCK, LANES))


def eliminate_group(rows, base):
    sub = lax.broadcasted_iota(jnp.int32, (BLOCK, LANES), 0)
    lane = lax.broadcasted_iota(jnp.int32, (BLOCK, LANES), 1)
    count = len(rows)
    for q in range(count):
        half, at = divmod(base + BLOCK * q, LANES)
        factors = [
            [
                jnp.broadcast_to(rows[r][half][:, at + j : at + j + 1], (BLOCK, LANES))
                for j in range(BLOCK)
            ]
            for r in range(count)
        ]
        inside = (lane >= at) & (lane < at + BLOCK)
        unit = (lane - at == sub).astype(jnp.float32)
        for r in range(count):
            rows[r][half] = jnp.where(inside, unit if r == q else 0.0, rows[r][half])
        columns, own = list(factors[q]), rows[q]
        a, b, d = row_of(columns[0], 0), row_of(columns[1], 0), row_of(columns[1], 1)
        for i in range(0, BLOCK, 2):
            scale = pl.reciprocal(a * d - b * b, approx=True)

            def step(value, i=i, a=a, b=b, d=d, scale=scale):
                first, second = row_of(value, i), row_of(value, i + 1)
                upper, lower = d * first - b * second, a * second - b * first
                new = value - (columns[i] * upper + columns[i + 1] * lower) * scale
                kept = jnp.where(sub == i + 1, lower * scale, new)
                return new, jnp.where(sub == i, upper * scale, kept)

            pairs = {j: step(columns[j]) for j in range(i + 2, BLOCK)}
            for h in range(len(own)):
                own[h] = step(own[h])[1]
            if i + 2 < BLOCK:
                one, two = pairs[i + 2][0], pairs[i + 3][0]
                a, b, d = row_of(one, i + 2), row_of(two, i + 2), row_of(two, i + 3)
            for j, pair in pairs.items():
                columns[j] = pair[1]
        for r in range(count):
            if r != q:
                for h in range(len(own)):
                    t = [factors[r][j] * row_of(own[h], j) for j in range(BLOCK)]
                    rows[r][h] = rows[r][h] - (
                        ((t[0] + t[1]) + (t[2] + t[3])) + ((t[4] + t[5]) + (t[6] + t[7]))
                    )
    return rows


def sweep_group(a_ref, base):
    n = a_ref.shape[0]
    depth = BLOCK * GROUP
    before = a_ref[base : base + depth, :]
    rows = [
        [
            a_ref[base + BLOCK * r : base + BLOCK * (r + 1), LANES * h : LANES * (h + 1)]
            for h in range(n // LANES)
        ]
        for r in range(GROUP)
    ]
    rows = eliminate_group(rows, base)
    after = jnp.concatenate([jnp.concatenate(row, axis=1) for row in rows], axis=0)
    column = lax.broadcasted_iota(jnp.int32, (depth, n), 1)
    row = lax.broadcasted_iota(jnp.int32, (depth, n), 0)
    inside = (column >= base) & (column < base + depth)
    before = jnp.where(inside, jnp.where(column - base == row, -1.0, 0.0), before)
    after = jnp.where(inside, -after, after)
    u0, u1, u2 = split3(before)
    w0, w1, w2 = split3(after)
    left = jnp.concatenate([u0, u0, u0, u1, u1, u2], axis=0).T
    right = jnp.concatenate([w0, w1, w2, w0, w1, w0], axis=0)

    def update(low, high):
        row = lax.broadcasted_iota(jnp.int32, (high - low, n), 0) + low
        column = lax.broadcasted_iota(jnp.int32, (high - low, n), 1)
        outside = ((row < base) | (row >= base + depth)) & (
            (column < base) | (column >= base + depth)
        )
        a_ref[low:high, :] = jnp.where(outside, a_ref[low:high, :], 0.0) - mm(left[low:high], right)

    after = base + depth
    for low, high in ((after, after + depth), (0, after), (after + depth, n)):
        if low < min(high, n):
            update(low, min(high, n))


def place_of():
    arc, coef = lax.axis_index("arc"), lax.axis_index("coef")
    return lax.div(arc, PAIR), lax.rem(arc, PAIR), lax.div(coef, PAIR), lax.rem(coef, PAIR)


def solve_rows(tile, gain_ref, local_rows):
    solved = mm(tile, gain_ref[2], INNER) + mm(tile, gain_ref[1], INNER)
    solved = (solved + mm(tile, gain_ref[0], INNER)).astype(jnp.bfloat16)
    return (tile.astype(jnp.float32) - mm(solved, local_rows)).astype(jnp.bfloat16)


def normal_kernel(count_ref, prior_ref, local_ref, rows_ref, normal_ref, work_ref):
    n, m = local_ref.shape
    used = lax.broadcasted_iota(jnp.int32, (n, m), 1) < count_ref[0]
    rows_ref[...] = jnp.where(used, local_ref[...].astype(jnp.float32), 0.0).astype(jnp.bfloat16)
    local_rows = rows_ref[...]
    row = lax.broadcasted_iota(jnp.int32, (n, n), 0)
    column = lax.broadcasted_iota(jnp.int32, (n, n), 1)
    prior = jnp.broadcast_to(prior_ref[...], (n, n))
    normal = mm(local_rows, local_rows, INNER) + jnp.where(row == column, prior, 0.0)
    work_ref[...] = normal
    normal_ref[...] = normal
    for p in range(FIRST):
        sweep_group(work_ref, p * BLOCK * GROUP)


def local_kernel(
    n_y, count_ref, band_ref, owner_ref, rows_ref, normal_ref, begun_ref, global_ref,
    send_ref, own_ref, gain_ref, work_ref,
):
    n, m = rows_ref.shape
    owned = n_y * PAIR * OB
    mine = n_y * OB
    count = count_ref[0]
    _, _, y, core = place_of()
    work_ref[...] = begun_ref[...]
    lane = lax.broadcasted_iota(jnp.int32, (LANES, LANES), 1)
    used = lax.broadcasted_iota(jnp.int32, (LANES, m), 1) < count

    def gather_rows(t):
        position, part = divmod(t * LANES, OB)
        core_away, y_away = divmod(position, n_y)
        owner = (y ^ y_away) * PAIR + (core ^ core_away)
        wanted = owner_ref[owner, part // LANES : part // LANES + 1, :]
        wanted = jnp.broadcast_to(wanted.astype(jnp.float32), (LANES, LANES)).T.astype(jnp.int32)
        hot = []
        for k in range(owned // LANES):
            sensed = band_ref[0, k * LANES // OB].astype(jnp.float32)
            hot.append(jnp.where(wanted == lane + k * LANES, sensed, 0.0).astype(jnp.bfloat16))
        got = mm(jnp.concatenate(hot, axis=1), global_ref[0:owned, :])
        got = jnp.where(used, got, 0.0).astype(jnp.bfloat16)
        if t * LANES < mine:
            own_ref[t * LANES : (t + 1) * LANES, :] = got
        else:
            send_ref[t * LANES - mine : (t + 1) * LANES - mine, :] = got

    steps = n // (BLOCK * GROUP) - FIRST
    tiles = owned // LANES
    for p in range(steps):
        sweep_group(work_ref, (FIRST + p) * BLOCK * GROUP)
        for t in range(p * tiles // steps, (p + 1) * tiles // steps):
            gather_rows(t)
    used = lax.broadcasted_iota(jnp.int32, (KB, m), 1) < count
    border = global_ref[owned:, :].astype(jnp.float32)
    send_ref[mine:, :] = jnp.where(used, border, 0.0).astype(jnp.bfloat16)

    inverse = -work_ref[...]
    local_rows = rows_ref[...]
    i0, i1, i2 = split3(inverse)
    gain = mm(i2, local_rows) + mm(i1, local_rows) + mm(i0, local_rows)
    left = local_rows.astype(jnp.float32) - product_six(normal_ref[...], gain)
    gain = gain + product_three(inverse, left)
    for i, part in enumerate(split3(gain)):
        gain_ref[i] = part
    for t in range((mine + KB) // KB):
        tile = send_ref[t * KB : (t + 1) * KB, :]
        send_ref[t * KB : (t + 1) * KB, :] = solve_rows(tile, gain_ref, local_rows)


def begin_normal(count, prior, local_rows):
    n, m = local_rows.shape
    array = pl.BlockSpec(memory_space=pltpu.VMEM)
    return pl.pallas_call(
        normal_kernel,
        out_shape=(
            jax.ShapeDtypeStruct((n, m), jnp.bfloat16),
            jax.ShapeDtypeStruct((n, n), jnp.float32),
            jax.ShapeDtypeStruct((n, n), jnp.float32),
        ),
        in_specs=[pl.BlockSpec(memory_space=pltpu.SMEM), array, array],
        out_specs=(array, array, array),
        compiler_params=pltpu.CompilerParams(vmem_limit_bytes=16 * 1024 * 1024),
        cost_estimate=pl.CostEstimate(flops=4 * 10**9, bytes_accessed=0, transcendentals=0),
        name="begin_normal",
    )(count, prior, local_rows)


def reduce_rows(count, band, owners, rows, normal, begun, global_rows, n_y):
    n, m = rows.shape
    scalar = pl.BlockSpec(memory_space=pltpu.SMEM)
    array = pl.BlockSpec(memory_space=pltpu.VMEM)
    shapes = ((n_y * OB + KB, m), (n_y * OB, m), (3, n, m))
    return pl.pallas_call(
        functools.partial(local_kernel, n_y),
        out_shape=tuple(jax.ShapeDtypeStruct(shape, jnp.bfloat16) for shape in shapes),
        in_specs=[scalar, scalar, array, array, array, array, array],
        out_specs=tuple(array for _ in shapes),
        scratch_shapes=[pltpu.VMEM((n, n), jnp.float32)],
        compiler_params=pltpu.CompilerParams(vmem_limit_bytes=24 * 1024 * 1024),
        name="reduce_rows",
    )(count, band, owners, rows, normal, begun, global_rows)


def own_product_kernel(
    n_y, n_z, own_ref, send_ref, gain_ref, rows_ref, mine_ref, prod_ref, left
):
    z, x, _, _ = place_of()
    border = send_ref[n_y * OB :, :]
    local_rows = rows_ref[...]
    for t in range(n_y * OB // KB):
        tile = own_ref[t * KB : (t + 1) * KB, :]
        mine_ref[t * KB : (t + 1) * KB, :] = solve_rows(tile, gain_ref, local_rows)
    for y in range(n_y):
        order_rows(n_z, z, x, mine_ref, y, left)
        prod_ref[y, :, :OB] = mm(left[...], mine_ref[y * OB : (y + 1) * OB, :], INNER)
        prod_ref[y, :, OB:] = mm(left[...], border, INNER)


def order_rows(n_z, z, x, rows_ref, y, left):
    rows = OB // (n_z * PAIR)
    for i in range(PAIR):
        for j in range(n_z):
            at = (i * n_z + j) * rows
            source = pl.multiple_of(y * OB + ((z ^ j) * PAIR + (x ^ i)) * rows, rows)
            left[at : at + rows, :] = rows_ref[pl.ds(source, rows), :]


def product_kernel(
    n_y, n_z, other_ref, prod_ref,
    keep_y_ref, send_y_ref, keep_x_ref, send_x_ref, level_ref, left, total,
):
    z, x, _, _ = place_of()
    half = OB // PAIR
    border = other_ref[n_y * OB :, :]
    top = jnp.zeros((BLOCK, LANES), jnp.float32)
    for y in range(n_y):
        order_rows(n_z, z, x, other_ref, y, left)
        own = other_ref[y * OB : (y + 1) * OB, :]
        total[y, :, :OB] = prod_ref[y, :, :OB] + mm(left[...], own, INNER)
        total[y, :, OB:] = prod_ref[y, :, OB:] + mm(left[...], border, INNER)
        for h in range(WIDTH // LANES):
            part = jnp.abs(total[y, :, h * LANES : (h + 1) * LANES])
            top = jnp.maximum(top, jnp.max(part.reshape(OB // BLOCK, BLOCK, LANES), axis=0))
    top = jnp.max(jnp.max(top, axis=0, keepdims=True), axis=1, keepdims=True)
    level = jnp.floor(jnp.log2(jnp.maximum(jnp.broadcast_to(top, (BLOCK, HALF)), 1e-30)))
    level_ref[...] = level
    scale = jnp.exp2(TOP_LEVEL - level[:1])
    keep_y_ref[...] = total[0, :, :HALF]
    for j in range(1, n_y):
        send_y_ref[j - 1, :HEAD, :] = jnp.broadcast_to(level[:1], (HEAD, HALF))
        send_y_ref[j - 1, HEAD:, :] = total[j, :, :HALF] * scale
    send_x_ref[:HEAD, :] = jnp.broadcast_to(level[:1], (HEAD, HALF))
    for y in range(n_y):
        keep_x_ref[y] = total[y, :half, HALF:]
        at = HEAD + y * half
        send_x_ref[at : at + half, :] = total[y, half:, HALF:] * scale


def panel_kernel(n_y, mine_ref, other_ref, level_ref, out_ref):
    pick = lax.broadcasted_iota(jnp.int32, (P_SIZE, OB), 1) == STRIDE * lax.broadcasted_iota(
        jnp.int32, (P_SIZE, OB), 0
    )
    pick = pick.astype(jnp.float32).astype(jnp.bfloat16)
    level = level_ref[:1, :P_SIZE]
    scale = jnp.exp2(TOP_LEVEL - level)
    for y in range(n_y):
        panel = jnp.zeros((P_SIZE, P_SIZE), jnp.float32)
        for ref in (mine_ref, other_ref):
            strip = mm(pick, ref[y * OB : (y + 1) * OB, :]).astype(jnp.bfloat16)
            panel = panel + mm(strip, strip, INNER)
        out_ref[y, :HEAD, :] = jnp.broadcast_to(level, (HEAD, P_SIZE))
        out_ref[y, HEAD:, :] = panel * scale


def own_products(own, send, gain, rows, n_y, n_z):
    array = pl.BlockSpec(memory_space=pltpu.VMEM)
    m = own.shape[1]
    return pl.pallas_call(
        functools.partial(own_product_kernel, n_y, n_z),
        out_shape=(
            jax.ShapeDtypeStruct(own.shape, jnp.bfloat16),
            jax.ShapeDtypeStruct((n_y, OB, WIDTH), jnp.float32),
        ),
        in_specs=[array, array, array, array],
        out_specs=(array, array),
        scratch_shapes=[pltpu.VMEM((OB, m), jnp.bfloat16)],
        compiler_params=pltpu.CompilerParams(vmem_limit_bytes=24 * 1024 * 1024),
        cost_estimate=pl.CostEstimate(
            flops=4 * n_y * OB * WIDTH * m, bytes_accessed=0, transcendentals=0
        ),
        name="own_products",
    )(own, send, gain, rows)


def products(other, own, n_y, n_z):
    array = pl.BlockSpec(memory_space=pltpu.VMEM)
    m = other.shape[1]
    half = OB // PAIR
    shapes = (
        (OB, HALF),
        (n_y - 1, HEAD + OB, HALF),
        (n_y, half, HALF),
        (HEAD + n_y * half, HALF),
        (BLOCK, HALF),
    )
    return pl.pallas_call(
        functools.partial(product_kernel, n_y, n_z),
        out_shape=tuple(jax.ShapeDtypeStruct(shape, jnp.float32) for shape in shapes),
        in_specs=[array, array],
        out_specs=tuple(array for _ in shapes),
        scratch_shapes=[
            pltpu.VMEM((OB, m), jnp.bfloat16),
            pltpu.VMEM((n_y, OB, WIDTH), jnp.float32),
        ],
        compiler_params=pltpu.CompilerParams(vmem_limit_bytes=24 * 1024 * 1024),
        name="products",
    )(other, own)


def panel_products(mine, other, level, n_y):
    array = pl.BlockSpec(memory_space=pltpu.VMEM)
    return pl.pallas_call(
        functools.partial(panel_kernel, n_y),
        out_shape=jax.ShapeDtypeStruct((n_y, HEAD + P_SIZE, P_SIZE), jnp.float32),
        in_specs=[array, array, array],
        out_specs=array,
        cost_estimate=pl.CostEstimate(
            flops=4 * n_y * P_SIZE * OB * mine.shape[1], bytes_accessed=0, transcendentals=0
        ),
        compiler_params=pltpu.CompilerParams(vmem_limit_bytes=8 * 1024 * 1024),
        name="panel_products",
    )(mine, other, level)


def factor_group(rows, base):
    sub = lax.broadcasted_iota(jnp.int32, (BLOCK, LANES), 0)
    count = len(rows)
    for q in range(count):
        at = base + BLOCK * q
        factors = [
            [
                jnp.broadcast_to(rows[r][:, at + j : at + j + 1], (BLOCK, LANES))
                for j in range(BLOCK)
            ]
            for r in range(q, count)
        ]
        columns, own = factors[0], rows[q]
        scales, entries = [], []
        for i in range(BLOCK):
            pivot = row_of(columns[i], i)
            scale = lax.rsqrt(pivot)
            scale = scale * (1.5 - 0.5 * pivot * scale * scale)
            scales.append(scale)
            scaled = row_of(own, i) * scale
            step = columns[i] * scale
            own = jnp.where(sub == i, scaled, jnp.where(sub > i, own - step * scaled, own))
            entries.append([row_of(columns[j], i) * scale for j in range(BLOCK)])
            for j in range(i + 1, BLOCK):
                columns[j] = columns[j] - step * entries[i][j]
        rows[q] = own
        for r in range(q + 1, count):
            value = rows[r]
            below = list(factors[r - q])
            for i in range(BLOCK):
                step = below[i] * scales[i]
                value = value - step * row_of(own, i)
                for j in range(i + 1, BLOCK):
                    below[j] = below[j] - step * entries[i][j]
            rows[r] = value
    return rows


def factor_kernel(panel_ref, prior_ref, out_ref, work_ref):
    n = work_ref.shape[0]
    depth = BLOCK * FACTOR_GROUP
    row = lax.broadcasted_iota(jnp.int32, (n, n), 0)
    column = lax.broadcasted_iota(jnp.int32, (n, n), 1)
    prior = jnp.broadcast_to(prior_ref[...], (n, n))
    work_ref[...] = panel_ref[...] + jnp.where(row == column, prior, 0.0)
    for p in range(n // depth):
        base = p * depth
        rows = [
            work_ref[base + BLOCK * r : base + BLOCK * (r + 1), :] for r in range(FACTOR_GROUP)
        ]
        done = jnp.concatenate(factor_group(rows, base), axis=0)
        work_ref[base : base + depth, :] = done
        if base + depth < n:
            d0, d1, d2 = split3(done)
            update = mm(
                jnp.concatenate([d0, d0, d0, d1, d1, d2], axis=0),
                jnp.concatenate([d0, d1, d2, d0, d1, d0], axis=0),
                COLS,
            )
            work_ref[base + depth :, :] = work_ref[base + depth :, :] - update[base + depth :, :]
    out_ref[...] = jnp.where(row <= column, work_ref[...], 0.0).T


def factor_panel(panel, prior):
    n = panel.shape[0]
    return pl.pallas_call(
        factor_kernel,
        out_shape=jax.ShapeDtypeStruct((n, n), jnp.float32),
        scratch_shapes=[pltpu.VMEM((n, n), jnp.float32)],
        cost_estimate=pl.CostEstimate(flops=n**3, bytes_accessed=12 * n * n, transcendentals=n),
        compiler_params=pltpu.CompilerParams(vmem_limit_bytes=8 * 1024 * 1024),
        name="factor_panel",
    )(panel, prior)


def level_of(message):
    return message[:1].astype(jnp.float32)


def values_of(message):
    return message[HEAD:].astype(jnp.float32) * jnp.exp2(level_of(message) - TOP_LEVEL)


def message_of(values, level):
    head = jnp.broadcast_to(level, (HEAD, values.shape[1]))
    return jnp.concatenate([head, values * jnp.exp2(TOP_LEVEL - level)]).astype(jnp.float16)


def fold(message):
    parts = HALF // P_SIZE
    step = message.shape[0] // parts
    return jnp.concatenate([message[i * step : (i + 1) * step] for i in range(parts)], axis=1)


def unfold(rows):
    parts = HALF // P_SIZE
    return jnp.concatenate([rows[:, i * P_SIZE : (i + 1) * P_SIZE] for i in range(parts)], axis=0)


def pairwise(terms):
    while len(terms) > 1:
        terms = [terms[2 * i] + terms[2 * i + 1] for i in range(len(terms) // 2)]
    return terms[0]


def per_device(
    local_design, global_design, local_prior, obs_count, band_mask, owner_columns, kaula_prior
):
    n_arc, n_coef = lax.axis_size("arc"), lax.axis_size("coef")
    n_z, n_y = n_arc // PAIR, n_coef // PAIR
    rows = OB // n_arc
    def swap(values, dz=0, dx=0, dy=0, dk=0):
        pairs = []
        for a in range(n_arc):
            for c in range(n_coef):
                to_a = ((a // PAIR) ^ dz) * PAIR + ((a % PAIR) ^ dx)
                to_c = ((c // PAIR) ^ dy) * PAIR + ((c % PAIR) ^ dk)
                pairs.append((a * n_coef + c, to_a * n_coef + to_c))
        return lax.ppermute(values, AXES, pairs)

    local_rows, normal, begun = begin_normal(obs_count, local_prior, local_design[0])
    send, own, gain = reduce_rows(
        obs_count,
        band_mask,
        owner_columns.reshape(n_coef, OB // LANES, LANES),
        local_rows,
        normal,
        begun,
        global_design[0],
        n_y,
    )
    other = swap(send, dk=1)
    mine, own = own_products(own, send, gain, local_rows, n_y, n_z)
    keep_y, send_y, keep_x, send_x, level = products(other, own, n_y, n_z)
    half = OB // PAIR
    grown = float(n_y.bit_length() - 1)

    from_y = [swap(send_y[j - 1].astype(jnp.float16), dy=j) for j in range(1, n_y)]
    from_x = swap(send_x.astype(jnp.float16), dx=1)
    panels = panel_products(mine, other, level, n_y).astype(jnp.float16)
    panel_z = [panels] + [swap(panels, dz=j) for j in range(1, n_z)]
    from_y, from_x, panel_z = lax.optimization_barrier((from_y, from_x, panel_z))

    left = functools.reduce(jnp.add, [values_of(message) for message in from_y], keep_y)
    left_level = functools.reduce(
        jnp.maximum, [level_of(message) for message in from_y], level[:1]
    ) + grown
    right = keep_x + values_of(from_x).reshape(n_y, half, HALF)
    right_level = jnp.maximum(level[:1], level_of(from_x)) + 1.0
    panel_level = functools.reduce(jnp.maximum, [level_of(p[0]) for p in panel_z])
    panel_level = panel_level + float(n_z.bit_length() - 1)
    panels = [
        message_of(pairwise([values_of(message[j]) for message in panel_z]), panel_level)
        for j in range(n_y)
    ]

    over_x = jnp.concatenate([message_of(left[half:], left_level), fold(panels[0])])
    over_y = [
        jnp.concatenate([message_of(right[j], right_level), fold(panels[j])])
        for j in range(1, n_y)
    ]
    over_x, over_y, panels = lax.optimization_barrier((over_x, over_y, panels))
    from_x = swap(over_x, dx=1)
    from_y = [swap(over_y[j - 1], dy=j) for j in range(1, n_y)]
    panel_xy = [swap(panels[j], dx=1, dy=j) for j in range(1, n_y)]
    tail = (HEAD + P_SIZE) * P_SIZE // HALF
    panel_y = [panels[0]] + [unfold(message[-tail:]) for message in from_y]
    panel_x = [unfold(from_x[-tail:])] + panel_xy
    from_x, from_y = from_x[:-tail], [message[:-tail] for message in from_y]
    left = left[:half] + values_of(from_x)
    left_level = jnp.maximum(left_level, level_of(from_x)) + 1.0
    right = functools.reduce(jnp.add, [values_of(message) for message in from_y], right[0])
    right_level = functools.reduce(
        jnp.maximum, [level_of(message) for message in from_y], right_level
    ) + grown

    total = jnp.concatenate([left, right], axis=1)
    level = jnp.concatenate([left_level, right_level], axis=1)
    over_z = [message_of(total[j * rows : (j + 1) * rows], level) for j in range(1, n_z)]
    over_z, panel_x, panel_y = lax.optimization_barrier((over_z, panel_x, panel_y))
    from_z = [swap(over_z[j - 1], dz=j) for j in range(1, n_z)]
    from_z[0], panel_x, panel_y = lax.optimization_barrier((from_z[0], panel_x, panel_y))
    panel = functools.reduce(jnp.add, [values_of(message) for message in panel_y])
    panel = panel + functools.reduce(jnp.add, [values_of(message) for message in panel_x])
    panel_factor = factor_panel(panel, kaula_prior)
    normal_rows = functools.reduce(
        jnp.add, [values_of(message) for message in from_z], total[:rows]
    )
    return normal_rows[None], panel_factor[None]


def solution(mesh):
    in_specs = (
        P(AXES, None, None),
        P(AXES, None, None),
        P(AXES, None),
        P(AXES),
        P(AXES, None),
        P(),
        P("coef", None),
    )
    out_specs = (P("coef", "arc", None), P("coef", None, None))
    return jax.shard_map(
        per_device, mesh=mesh, in_specs=in_specs, out_specs=out_specs, check_vma=False
    )
```

time: 96.8 us -> 61.4 us (0.63)
  other arithmetic: 19.5 us -> 2.13 us
  local copies, waits for them, and re-layouts: 12.5 us -> 1.7 us
  between operations: 11.3 us -> 1.59 us
  waiting for transfers between devices: 11.4 us -> 13.5 us
  Pallas kernels: 23.4 us -> 25.3 us
  starting transfers between devices: 18.1 us -> 17.1 us
    another operation x4 -> x6, other arithmetic: 12.5 us -> 0.26 us  [the longest x3 12.5 us: per_device(): jnp.linalg.cholesky(panel_z[0][:P_SIZE] + jnp.diag(kaula_prior[0]))]
    slice x10 -> x2, local copies, waits for them, and re-layouts: 6.14 us -> 0.03 us  [unfold(): rows[:, i * P_SIZE:(i + 1) * P_SIZE]]
    unnamed x19 -> x12, local copies, waits for them, and re-layouts: 6.05 us -> 1.64 us
    convert_element_type x5 -> x3, other arithmetic: 4.07 us -> 0.12 us  [the longest x1 0.05 us: per_device(): from_x = swap(send_x.astype(jnp.float16), dx=1)]
    ppermute x14 -> x12, waiting for transfers between devices: 11.4 us -> 13.5 us  [swap(): return lax.ppermute(values, AXES, pairs)]
    pallas_call x2 -> x6, Pallas kernels: 23.4 us -> 25.3 us  [the longest x1 12.4 us: reduce_rows(): pl.pallas_call(functools.partial(local_kernel, n_y), out_shape=tuple((jax...]
    add x5 -> x6, other arithmetic: 1.54 us -> 0.32 us  [the longest x1 0.1 us: per_device(): right = keep_x + values_of(from_x).reshape(n_y, half, HALF)]
    ppermute x14 -> x12, starting transfers between devices: 18.1 us -> 17.1 us  [swap(): return lax.ppermute(values, AXES, pairs)]
  transfers between devices with their start and end apart: 14 -> 12, of which waited for: 5 -> 7; matrix products, arithmetic and copies ran while one was open for 24% -> 1% of each run, Pallas kernels for 0% -> 16%
where the time goes in v3:
time: 61.4 us; the launch traced here: 61.3 us
  Pallas kernels  25.3 us (41%)
  starting transfers between devices  17.1 us (28%)
  waiting for transfers between devices  13.5 us (22%)
  other arithmetic  2.13 us (3%)
  local copies, waits for them, and re-layouts  1.7 us (3%)
  between operations  1.59 us (3%)
    ppermute x12, starting transfers between devices, swap(): return lax.ppermute(values, AXES, pairs)  17.1 us
    ppermute x12, waiting for transfers between devices, swap(): return lax.ppermute(values, AXES, pairs)  13.5 us
    pallas_call x1, Pallas kernels, reduce_rows(): pl.pallas_call(functools.partial(local_kernel, n_y), out_shape=tuple((jax...  12.4 us
    pallas_call x1, Pallas kernels, factor_panel(): pl.pallas_call(factor_kernel, out_shape=jax.ShapeDtypeStruct((n, n), jnp....  5.11 us
    pallas_call x1, Pallas kernels, own_products(): pl.pallas_call(functools.partial(own_product_kernel, n_y, n_z), out_shape...  3.53 us
    pallas_call x1, Pallas kernels, begin_normal(): pl.pallas_call(normal_kernel, out_shape=(jax.ShapeDtypeStruct((n, m), jnp...  2.21 us
    unnamed x12, local copies, waits for them, and re-layouts  1.64 us
  transfers between devices with their start and end apart: 12, of which 7 were waited for; matrix products, arithmetic and copies ran while one was open for 1% of the time, Pallas kernels for 16%

profile of v3, /device:TPU:0, one launch (start us, length us, event | category | flops | bytes accessed | tf_op | source)
XLA Modules:
  0.0 61.3 jit_solution(6931635928070372041)
XLA Ops:
  1.3 0.9 %copy-done.4 = bf16[1,256,512]{2,1,0:T(8,128)(2,1)S(1)} copy-done((bf16[1,256,512]{2,1,0:T(8,128)(2,1)S(1)}, bf16[1,256,512]{2,1,0:T(8,128)(2,1)}, u32[]{:S(2)}) %copy-start.4) | copy-done | bytes 262168
  2.2 0.7 %copy-done.5 = f32[1,256]{1,0:T(1,128)S(1)} copy-done((f32[1,256]{1,0:T(1,128)S(1)}, f32[1,256]{1,0:T(1,128)}, u32[]{:S(2)}) %copy-start.5) | copy-done | bytes 1048
  2.9 2.2 %begin_normal.1 = (bf16[256,512]{1,0:T(8,128)(2,1)S(1)}, f32[256,256]{1,0:T(8,128)S(1)}, f32[256,256]{1,0:T(8,128)S(1)}) custom-call(s32[1]{0:T(128)S(6)} %copy.9.count_ref, f32[1,256]{1,0:T(1,128)S(1)} %copy-done.5, bf16[256,512]{1,0:T(8,128)(2,1)S(1)} %bitcast.73), custom_call_target="tpu_custom_call" | custom-call | flops 4000000000 | tf_op jit(solution)/shard_map/begin_normal/pallas_call | solution.py:225
  5.2 12.4 %reduce_rows.1 = (bf16[1280,512]{1,0:T(8,128)(2,1)S(1)}, bf16[1024,512]{1,0:T(8,128)(2,1)S(1)}, bf16[3,256,512]{2,1,0:T(8,128)(2,1)S(1)}) custom-call(s32[1]{0:T(128)S(6)} %copy.9.count_ref, s32[1,4]{1,0:T(1,128)S(1)} %copy-done.2, s32[4,4,128]{2,1,0:T(4,128)S(1)} %bitcast.72, bf16[256,512]{1,0:T(8,128)(2,1)S(1)} %get-tuple-element.37.rows_ref, ...), custom_call_target="tpu_custom_call" | custom-call | tf_op jit(solution)/shard_map/reduce_rows/pallas_call | solution.py:245
  17.5 0.5 collective-permute-start
  18.0 3.5 %own_products.1 = (bf16[1024,512]{1,0:T(8,128)(2,1)S(1)}, f32[2,512,768]{2,1,0:T(8,128)S(1)}) custom-call(bf16[1024,512]{1,0:T(8,128)(2,1)S(1)} %get-tuple-element.41.own_ref, bf16[1280,512]{1,0:T(8,128)(2,1)S(1)} %get-tuple-element.40.send_ref, bf16[3,256,512]{2,1,0:T(8,128)(2,1)S(1)} %get-tuple-element.42.gain_ref, ...), custom_call_target="tpu_custom_call" | custom-call | flops 1610612736 | tf_op jit(solution)/shard_map/own_products/pallas_call | solution.py:330
  21.6 1.2 %products.1 = (f32[512,384]{1,0:T(8,128)S(1)}, f32[1,528,384]{2,1,0:T(8,128)S(1)}, f32[2,256,384]{2,1,0:T(8,128)S(1)}, f32[528,384]{1,0:T(8,128)S(1)}, f32[8,384]{1,0:T(8,128)S(1)}) custom-call(bf16[1280,512]{1,0:T(8,128)(2,1)S(1)} %collective-permute-done.other_ref, f32[2,512,768]{2,1,0:T(8,128)S(1)} %get-tuple-element.43.prod_ref), custom_call_target="tpu_custom_call" | custom-call | tf_op jit(solution)/shard_map/products/pallas_call | solution.py:358
  22.9 2.6 %collective-permute-start.1 = (f16[528,384]{1,0:T(8,128)(2,1)S(1)}, f16[528,384]{1,0:T(8,128)(2,1)S(1)}, u32[]{:S(2)}, u32[]{:S(2)}) collective-permute-start(f16[528,384]{1,0:T(8,128)(2,1)S(1)} %convert_bitcast_fusion), channel_id=1, source_target_pairs={{0,2},{1,3},{2,0},{3,1},{4,6},{5,7},{6,4},{7,5},{8,10},{9,11},{10,... | collective-permute-start | bytes 1216520 | tf_op jit(solution)/shard_map/ppermute | solution.py:505
  25.5 1.6 %collective-permute-start.2 = (f16[528,384]{1,0:T(8,128)(2,1)S(1)}, f16[528,384]{1,0:T(8,128)(2,1)S(1)}, u32[]{:S(2)}, u32[]{:S(2)}) collective-permute-start(f16[528,384]{1,0:T(8,128)(2,1)S(1)} %convert_element_type.239), channel_id=1, source_target_pairs={{0,4},{1,5},{2,6},{3,7},{4,0},{5,1},{6,2},{7,3},{8,12},{9,13},{10,... | collective-permute-start | bytes 1216520 | tf_op jit(solution)/shard_map/ppermute | solution.py:505
  27.1 0.9 %panel_products.1 = f32[2,144,128]{2,1,0:T(8,128)S(1)} custom-call(bf16[1024,512]{1,0:T(8,128)(2,1)S(1)} %get-tuple-element.47.mine_ref, bf16[1280,512]{1,0:T(8,128)(2,1)S(1)} %collective-permute-done.other_ref, f32[8,384]{1,0:T(8,128)S(1)} %get-tuple-element.48.level_ref), custom_call_target="tpu_custom_call" | custom-call | flops 268435456 | tf_op jit(solution)/shard_map/panel_products/pallas_call | solution.py:374
  28.0 1.6 %collective-permute-start.3 = (f16[2,144,128]{2,1,0:T(8,128)(2,1)S(1)}, f16[2,144,128]{2,1,0:T(8,128)(2,1)S(1)}, u32[]{:S(2)}, u32[]{:S(2)}) collective-permute-start(f16[2,144,128]{2,1,0:T(8,128)(2,1)S(1)} %convert_element_type.240), channel_id=1, source_target_pairs={{0,8},{1,9},{2,10},{3,11},{4,12},{5,13},{6,14},{7,15},{8,0},{9,1},... | collective-permute-start | bytes 221192 | tf_op jit(solution)/shard_map/ppermute | solution.py:505
  29.7 2.6 %collective-permute-start.4 = (f16[2,144,128]{2,1,0:T(8,128)(2,1)S(1)}, f16[2,144,128]{2,1,0:T(8,128)(2,1)S(1)}, u32[]{:S(2)}, u32[]{:S(2)}) collective-permute-start(f16[2,144,128]{2,1,0:T(8,128)(2,1)S(1)} %convert_element_type.240), channel_id=1, source_target_pairs={{0,16},{1,17},{2,18},{3,19},{4,20},{5,21},{6,22},{7,23},{8,24},{9,... | collective-permute-start | bytes 221192 | tf_op jit(solution)/shard_map/ppermute | solution.py:505
  32.5 5.1 %collective-permute-done.4 = f16[2,144,128]{2,1,0:T(8,128)(2,1)S(1)} collective-permute-done((f16[2,144,128]{2,1,0:T(8,128)(2,1)S(1)}, f16[2,144,128]{2,1,0:T(8,128)(2,1)S(1)}, u32[]{:S(2)}, u32[]{:S(2)}) %collective-permute-start.4) | collective-permute-done | bytes 73760 | tf_op jit(solution)/shard_map/ppermute | solution.py:505
  37.6 0.9 %collective-permute-done.5 = f16[2,144,128]{2,1,0:T(8,128)(2,1)S(1)} collective-permute-done((f16[2,144,128]{2,1,0:T(8,128)(2,1)S(1)}, f16[2,144,128]{2,1,0:T(8,128)(2,1)S(1)}, u32[]{:S(2)}, u32[]{:S(2)}) %collective-permute-start.5) | collective-permute-done | bytes 73760 | tf_op jit(solution)/shard_map/ppermute | solution.py:505
  39.4 0.6 collective-permute-start.7
  40.5 2.5 %collective-permute-start.8 = (f16[144,128]{1,0:T(8,128)(2,1)S(1)}, f16[144,128]{1,0:T(8,128)(2,1)S(1)}, u32[]{:S(2)}, u32[]{:S(2)}) collective-permute-start(f16[144,128]{1,0:T(8,128)(2,1)S(1)} %get-tuple-element.58), channel_id=1, source_target_pairs={{0,6},{1,7},{2,4},{3,5},{4,2},{5,3},{6,0},{7,1},{8,14},{9,15},{10,... | collective-permute-start | bytes 110600 | tf_op jit(solution)/shard_map/ppermute | solution.py:505
  42.9 3.1 %collective-permute-done.7 = f16[320,384]{1,0:T(8,128)(2,1)S(1)} collective-permute-done((f16[320,384]{1,0:T(8,128)(2,1)S(1)}, f16[320,384]{1,0:T(8,128)(2,1)S(1)}, u32[]{:S(2)}, u32[]{:S(2)}) %collective-permute-start.7) | collective-permute-done | bytes 245792 | tf_op jit(solution)/shard_map/ppermute | solution.py:505
  46.6 0.9 %collective-permute-done.8 = f16[144,128]{1,0:T(8,128)(2,1)S(1)} collective-permute-done((f16[144,128]{1,0:T(8,128)(2,1)S(1)}, f16[144,128]{1,0:T(8,128)(2,1)S(1)}, u32[]{:S(2)}, u32[]{:S(2)}) %collective-permute-start.8) | collective-permute-done | bytes 36896 | tf_op jit(solution)/shard_map/ppermute | solution.py:505
  47.5 1.5 %collective-permute-start.9 = (f16[80,768]{1,0:T(8,128)(2,1)S(1)}, f16[80,768]{1,0:T(8,128)(2,1)S(1)}, u32[]{:S(2)}, u32[]{:S(2)}) collective-permute-start(f16[80,768]{1,0:T(8,128)(2,1)S(1)} %get-tuple-element.60), channel_id=1, source_target_pairs={{0,8},{1,9},{2,10},{3,11},{4,12},{5,13},{6,14},{7,15},{8,0},{9,1},... | collective-permute-start | bytes 368648 | tf_op jit(solution)/shard_map/ppermute | solution.py:505
  49.0 2.9 %collective-permute-start.11 = (f16[80,768]{1,0:T(8,128)(2,1)S(1)}, f16[80,768]{1,0:T(8,128)(2,1)S(1)}, u32[]{:S(2)}, u32[]{:S(2)}) collective-permute-start(f16[80,768]{1,0:T(8,128)(2,1)S(1)} %get-tuple-element.67), channel_id=1, source_target_pairs={{0,24},{1,25},{2,26},{3,27},{4,28},{5,29},{6,30},{7,31},{8,16},{9,... | collective-permute-start | bytes 368648 | tf_op jit(solution)/shard_map/ppermute | solution.py:505
  51.9 1.9 %collective-permute-done.9 = f16[80,768]{1,0:T(8,128)(2,1)S(1)} collective-permute-done((f16[80,768]{1,0:T(8,128)(2,1)S(1)}, f16[80,768]{1,0:T(8,128)(2,1)S(1)}, u32[]{:S(2)}, u32[]{:S(2)}) %collective-permute-start.9) | collective-permute-done | bytes 122912 | tf_op jit(solution)/shard_map/ppermute | solution.py:505
  53.9 5.1 %factor_panel.1 = f32[128,128]{1,0:T(8,128)} custom-call(f32[128,128]{1,0:T(8,128)S(1)} %add_add_fusion.panel_ref, f32[1,128]{1,0:T(1,128)S(1)} %copy-done.3), custom_call_target="tpu_custom_call" | custom-call | flops 2097152 | bytes 196608 | tf_op jit(solution)/shard_map/factor_panel/pallas_call | solution.py:452
  59.1 1.4 %collective-permute-done.10 = f16[80,768]{1,0:T(8,128)(2,1)S(1)} collective-permute-done((f16[80,768]{1,0:T(8,128)(2,1)S(1)}, f16[80,768]{1,0:T(8,128)(2,1)S(1)}, u32[]{:S(2)}, u32[]{:S(2)}) %collective-permute-start.10) | collective-permute-done | bytes 122912 | tf_op jit(solution)/shard_map/ppermute | solution.py:505
  60.5 0.8 %fusion.11 = f32[1,64,768]{2,1,0:T(8,128)} fusion(f32[256,384]{1,0:T(8,128)S(1)} %slice_add_fusion, f32[256,384]{1,0:T(8,128)S(1)} %fusion, f16[80,768]{1,0:T(8,128)(2,1)S(1)} %collective-permute-done.11, f16[80,768]{1,0:T(8,128)(2,1)S(1)} %collective-permute-done.10, f32[768]{0:T(1024)S(1)} %fusion.34, f32[768]{0:T(1024)S(1)} %fusion.38, ...), kind=kLoop, calls=%fused_computation.29 | loop fusion | flops 491520 | bytes 1287168 | tf_op jit(solution)/shard_map/broadcast_in_dim | solution.py:575
  (61 shorter events, 2.3 us)
Async XLA Ops:
  1.3 1.0 %copy-start.4 = (bf16[1,256,512]{2,1,0:T(8,128)(2,1)S(1)}, bf16[1,256,512]{2,1,0:T(8,128)(2,1)}, u32[]{:S(2)}) copy-start(bf16[1,256,512]{2,1,0:T(8,128)(2,1)} %param.7) | copy-start | bytes 786436
  2.2 0.7 %copy-start.5 = (f32[1,256]{1,0:T(1,128)S(1)}, f32[1,256]{1,0:T(1,128)}, u32[]{:S(2)}) copy-start(f32[1,256]{1,0:T(1,128)} %prior_ref.2) | copy-start | bytes 3076
  2.9 2.2 %copy-start = (bf16[1,2304,512]{2,1,0:T(8,128)(2,1)S(1)}, bf16[1,2304,512]{2,1,0:T(8,128)(2,1)}, u32[]{:S(2)}) copy-start(bf16[1,2304,512]{2,1,0:T(8,128)(2,1)} %param.8) | copy-start | bytes 7077892
  2.9 2.2 %copy-start.1 = (s32[2048]{0:T(1024)S(1)}, s32[2048]{0:T(1024)}, u32[]{:S(2)}) copy-start(s32[2048]{0:T(1024)} %param.12) | copy-start | bytes 24580
  2.9 2.2 %copy-start.2 = (s32[1,4]{1,0:T(1,128)S(1)}, s32[1,4]{1,0:T(1,128)}, u32[]{:S(2)}) copy-start(s32[1,4]{1,0:T(1,128)} %band_ref.1) | copy-start | bytes 52
  17.5 4.1 %collective-permute-start = (bf16[1280,512]{1,0:T(8,128)(2,1)S(1)}, bf16[1280,512]{1,0:T(8,128)(2,1)S(1)}, u32[]{:S(2)}, u32[]{:S(2)}) collective-permute-start(bf16[1280,512]{1,0:T(8,128)(2,1)S(1)} %get-tuple-element.40.send_ref), channel_id=1, source_target_pairs={{0,1},{1,0},{2,3},{3,2},{4,5},{5,4},{6,7},{7,6},{8,9},{9,8},{10,11... | collective-permute-start | bytes 3932168 | tf_op jit(solution)/shard_map/ppermute | solution.py:505
  22.9 15.6 %collective-permute-start.1 = (f16[528,384]{1,0:T(8,128)(2,1)S(1)}, f16[528,384]{1,0:T(8,128)(2,1)S(1)}, u32[]{:S(2)}, u32[]{:S(2)}) collective-permute-start(f16[528,384]{1,0:T(8,128)(2,1)S(1)} %convert_bitcast_fusion), channel_id=1, source_target_pairs={{0,2},{1,3},{2,0},{3,1},{4,6},{5,7},{6,4},{7,5},{8,10},{9,11},{10,... | collective-permute-start | bytes 1216520 | tf_op jit(solution)/shard_map/ppermute | solution.py:505
  25.5 13.0 %collective-permute-start.2 = (f16[528,384]{1,0:T(8,128)(2,1)S(1)}, f16[528,384]{1,0:T(8,128)(2,1)S(1)}, u32[]{:S(2)}, u32[]{:S(2)}) collective-permute-start(f16[528,384]{1,0:T(8,128)(2,1)S(1)} %convert_element_type.239), channel_id=1, source_target_pairs={{0,4},{1,5},{2,6},{3,7},{4,0},{5,1},{6,2},{7,3},{8,12},{9,13},{10,... | collective-permute-start | bytes 1216520 | tf_op jit(solution)/shard_map/ppermute | solution.py:505
  28.0 4.5 %collective-permute-start.3 = (f16[2,144,128]{2,1,0:T(8,128)(2,1)S(1)}, f16[2,144,128]{2,1,0:T(8,128)(2,1)S(1)}, u32[]{:S(2)}, u32[]{:S(2)}) collective-permute-start(f16[2,144,128]{2,1,0:T(8,128)(2,1)S(1)} %convert_element_type.240), channel_id=1, source_target_pairs={{0,8},{1,9},{2,10},{3,11},{4,12},{5,13},{6,14},{7,15},{8,0},{9,1},... | collective-permute-start | bytes 221192 | tf_op jit(solution)/shard_map/ppermute | solution.py:505
  29.7 7.9 %collective-permute-start.4 = (f16[2,144,128]{2,1,0:T(8,128)(2,1)S(1)}, f16[2,144,128]{2,1,0:T(8,128)(2,1)S(1)}, u32[]{:S(2)}, u32[]{:S(2)}) collective-permute-start(f16[2,144,128]{2,1,0:T(8,128)(2,1)S(1)} %convert_element_type.240), channel_id=1, source_target_pairs={{0,16},{1,17},{2,18},{3,19},{4,20},{5,21},{6,22},{7,23},{8,24},{9,... | collective-permute-start | bytes 221192 | tf_op jit(solution)/shard_map/ppermute | solution.py:505
  32.3 6.3 %collective-permute-start.5 = (f16[2,144,128]{2,1,0:T(8,128)(2,1)S(1)}, f16[2,144,128]{2,1,0:T(8,128)(2,1)S(1)}, u32[]{:S(2)}, u32[]{:S(2)}) collective-permute-start(f16[2,144,128]{2,1,0:T(8,128)(2,1)S(1)} %convert_element_type.240), channel_id=1, source_target_pairs={{0,24},{1,25},{2,26},{3,27},{4,28},{5,29},{6,30},{7,31},{8,16},{9,... | collective-permute-start | bytes 221192 | tf_op jit(solution)/shard_map/ppermute | solution.py:505
  39.3 14.6 %copy-start.3 = (f32[1,128]{1,0:T(1,128)S(1)}, f32[1,128]{1,0:T(1,128)}, u32[]{:S(2)}) copy-start(f32[1,128]{1,0:T(1,128)} %prior_ref.3) | copy-start | bytes 1540
  39.4 6.7 %collective-permute-start.7 = (f16[320,384]{1,0:T(8,128)(2,1)S(1)}, f16[320,384]{1,0:T(8,128)(2,1)S(1)}, u32[]{:S(2)}, u32[]{:S(2)}) collective-permute-start(f16[320,384]{1,0:T(8,128)(2,1)S(1)} %maximum_maximum_fusion.1), channel_id=1, source_target_pairs={{0,2},{1,3},{2,0},{3,1},{4,6},{5,7},{6,4},{7,5},{8,10},{9,11},{10,... | collective-permute-start | bytes 737288 | tf_op jit(solution)/shard_map/ppermute | solution.py:505
  40.0 6.2 %collective-permute-start.6 = (f16[320,384]{1,0:T(8,128)(2,1)S(1)}, f16[320,384]{1,0:T(8,128)(2,1)S(1)}, u32[]{:S(2)}, u32[]{:S(2)}) collective-permute-start(f16[320,384]{1,0:T(8,128)(2,1)S(1)} %maximum_maximum_fusion), channel_id=1, source_target_pairs={{0,4},{1,5},{2,6},{3,7},{4,0},{5,1},{6,2},{7,3},{8,12},{9,13},{10,... | collective-permute-start | bytes 737288 | tf_op jit(solution)/shard_map/ppermute | solution.py:505
  40.5 7.0 %collective-permute-start.8 = (f16[144,128]{1,0:T(8,128)(2,1)S(1)}, f16[144,128]{1,0:T(8,128)(2,1)S(1)}, u32[]{:S(2)}, u32[]{:S(2)}) collective-permute-start(f16[144,128]{1,0:T(8,128)(2,1)S(1)} %get-tuple-element.58), channel_id=1, source_target_pairs={{0,6},{1,7},{2,4},{3,5},{4,2},{5,3},{6,0},{7,1},{8,14},{9,15},{10,... | collective-permute-start | bytes 110600 | tf_op jit(solution)/shard_map/ppermute | solution.py:505
  47.5 6.3 %collective-permute-start.9 = (f16[80,768]{1,0:T(8,128)(2,1)S(1)}, f16[80,768]{1,0:T(8,128)(2,1)S(1)}, u32[]{:S(2)}, u32[]{:S(2)}) collective-permute-start(f16[80,768]{1,0:T(8,128)(2,1)S(1)} %get-tuple-element.60), channel_id=1, source_target_pairs={{0,8},{1,9},{2,10},{3,11},{4,12},{5,13},{6,14},{7,15},{8,0},{9,1},... | collective-permute-start | bytes 368648 | tf_op jit(solution)/shard_map/ppermute | solution.py:505
  49.0 10.0 %collective-permute-start.11 = (f16[80,768]{1,0:T(8,128)(2,1)S(1)}, f16[80,768]{1,0:T(8,128)(2,1)S(1)}, u32[]{:S(2)}, u32[]{:S(2)}) collective-permute-start(f16[80,768]{1,0:T(8,128)(2,1)S(1)} %get-tuple-element.67), channel_id=1, source_target_pairs={{0,24},{1,25},{2,26},{3,27},{4,28},{5,29},{6,30},{7,31},{8,16},{9,... | collective-permute-start | bytes 368648 | tf_op jit(solution)/shard_map/ppermute | solution.py:505
  51.9 8.6 %collective-permute-start.10 = (f16[80,768]{1,0:T(8,128)(2,1)S(1)}, f16[80,768]{1,0:T(8,128)(2,1)S(1)}, u32[]{:S(2)}, u32[]{:S(2)}) collective-permute-start(f16[80,768]{1,0:T(8,128)(2,1)S(1)} %get-tuple-element.66), channel_id=1, source_target_pairs={{0,16},{1,17},{2,18},{3,19},{4,20},{5,21},{6,22},{7,23},{8,24},{9,... | collective-permute-start | bytes 368648 | tf_op jit(solution)/shard_map/ppermute | solution.py:505

commit v4 on v3

--- a/solution.py
+++ b/solution.py
@@ -15,7 +15,7 @@
 HALF = WIDTH // 2
 PAIR = 2
 TOP_LEVEL = 12.0
-HEAD = 16
+HEAD = 8
 INNER = (((1,), (1,)), ((), ()))
 AXES = ("arc", "coef")
 
@@ -24,6 +24,7 @@
 GROUP = 2
 FACTOR_GROUP = 4
 FIRST = 4
+TILE = 128
 ROWS = (((1,), (0,)), ((), ()))
 COLS = (((0,), (0,)), ((), ()))
 
@@ -38,18 +39,6 @@
     middle = rest.astype(jnp.bfloat16)
     low = (rest - middle.astype(jnp.float32)).astype(jnp.bfloat16)
     return high, middle, low
-
-
-def product_six(a, b):
-    a0, a1, a2 = split3(a)
-    b0, b1, b2 = split3(b)
-    return (mm(a0, b2) + mm(a1, b1) + mm(a2, b0)) + (mm(a0, b1) + mm(a1, b0)) + mm(a0, b0)
-
-
-def product_three(a, b):
-    a0, a1, _ = split3(a)
-    b0, b1, _ = split3(b)
-    return (mm(a0, b1) + mm(a1, b0)) + mm(a0, b0)
 
 
 def row_of(value, i):
@@ -146,12 +135,11 @@
 
 
 def solve_rows(tile, gain_ref, local_rows):
-    solved = mm(tile, gain_ref[2], INNER) + mm(tile, gain_ref[1], INNER)
-    solved = (solved + mm(tile, gain_ref[0], INNER)).astype(jnp.bfloat16)
+    solved = (mm(tile, gain_ref[1], INNER) + mm(tile, gain_ref[0], INNER)).astype(jnp.bfloat16)
     return (tile.astype(jnp.float32) - mm(solved, local_rows)).astype(jnp.bfloat16)
 
 
-def normal_kernel(count_ref, prior_ref, local_ref, rows_ref, normal_ref, work_ref):
+def normal_kernel(count_ref, prior_ref, local_ref, rows_ref, work_ref):
     n, m = local_ref.shape
     used = lax.broadcasted_iota(jnp.int32, (n, m), 1) < count_ref[0]
     rows_ref[...] = jnp.where(used, local_ref[...].astype(jnp.float32), 0.0).astype(jnp.bfloat16)
@@ -159,15 +147,13 @@
     row = lax.broadcasted_iota(jnp.int32, (n, n), 0)
     column = lax.broadcasted_iota(jnp.int32, (n, n), 1)
     prior = jnp.broadcast_to(prior_ref[...], (n, n))
-    normal = mm(local_rows, local_rows, INNER) + jnp.where(row == column, prior, 0.0)
-    work_ref[...] = normal
-    normal_ref[...] = normal
+    work_ref[...] = mm(local_rows, local_rows, INNER) + jnp.where(row == column, prior, 0.0)
     for p in range(FIRST):
         sweep_group(work_ref, p * BLOCK * GROUP)
 
 
 def local_kernel(
-    n_y, count_ref, band_ref, owner_ref, rows_ref, normal_ref, begun_ref, global_ref,
+    n_y, count_ref, band_ref, owner_ref, rows_ref, begun_ref, global_ref,
     send_ref, own_ref, gain_ref, work_ref,
 ):
     n, m = rows_ref.shape
@@ -176,28 +162,32 @@
     count = count_ref[0]
     _, _, y, core = place_of()
     work_ref[...] = begun_ref[...]
-    lane = lax.broadcasted_iota(jnp.int32, (LANES, LANES), 1)
-    used = lax.broadcasted_iota(jnp.int32, (LANES, m), 1) < count
+    lane = lax.broadcasted_iota(jnp.int32, (TILE, LANES), 1)
+    used = lax.broadcasted_iota(jnp.int32, (TILE, m), 1) < count
 
     def gather_rows(t):
-        position, part = divmod(t * LANES, OB)
+        position, part = divmod(t * TILE, OB)
         core_away, y_away = divmod(position, n_y)
         owner = (y ^ y_away) * PAIR + (core ^ core_away)
-        wanted = owner_ref[owner, part // LANES : part // LANES + 1, :]
-        wanted = jnp.broadcast_to(wanted.astype(jnp.float32), (LANES, LANES)).T.astype(jnp.int32)
+        wanted = []
+        for r in range(TILE // LANES):
+            at = part // LANES + r
+            ids = owner_ref[owner, at : at + 1, :].astype(jnp.float32)
+            wanted.append(jnp.broadcast_to(ids, (LANES, LANES)).T.astype(jnp.int32))
+        wanted = jnp.concatenate(wanted, axis=0)
         hot = []
         for k in range(owned // LANES):
             sensed = band_ref[0, k * LANES // OB].astype(jnp.float32)
             hot.append(jnp.where(wanted == lane + k * LANES, sensed, 0.0).astype(jnp.bfloat16))
         got = mm(jnp.concatenate(hot, axis=1), global_ref[0:owned, :])
         got = jnp.where(used, got, 0.0).astype(jnp.bfloat16)
-        if t * LANES < mine:
-            own_ref[t * LANES : (t + 1) * LANES, :] = got
+        if t * TILE < mine:
+            own_ref[t * TILE : (t + 1) * TILE, :] = got
         else:
-            send_ref[t * LANES - mine : (t + 1) * LANES - mine, :] = got
+            send_ref[t * TILE - mine : (t + 1) * TILE - mine, :] = got
 
     steps = n // (BLOCK * GROUP) - FIRST
-    tiles = owned // LANES
+    tiles = owned // TILE
     for p in range(steps):
         sweep_group(work_ref, (FIRST + p) * BLOCK * GROUP)
         for t in range(p * tiles // steps, (p + 1) * tiles // steps):
@@ -206,17 +196,12 @@
     border = global_ref[owned:, :].astype(jnp.float32)
     send_ref[mine:, :] = jnp.where(used, border, 0.0).astype(jnp.bfloat16)
 
-    inverse = -work_ref[...]
     local_rows = rows_ref[...]
-    i0, i1, i2 = split3(inverse)
+    i0, i1, i2 = split3(-work_ref[...])
     gain = mm(i2, local_rows) + mm(i1, local_rows) + mm(i0, local_rows)
-    left = local_rows.astype(jnp.float32) - product_six(normal_ref[...], gain)
-    gain = gain + product_three(inverse, left)
-    for i, part in enumerate(split3(gain)):
+    for i, part in enumerate(split3(gain)[:2]):
         gain_ref[i] = part
-    for t in range((mine + KB) // KB):
-        tile = send_ref[t * KB : (t + 1) * KB, :]
-        send_ref[t * KB : (t + 1) * KB, :] = solve_rows(tile, gain_ref, local_rows)
+    send_ref[...] = solve_rows(send_ref[...], gain_ref, local_rows)
 
 
 def begin_normal(count, prior, local_rows):
@@ -227,30 +212,29 @@
         out_shape=(
             jax.ShapeDtypeStruct((n, m), jnp.bfloat16),
             jax.ShapeDtypeStruct((n, n), jnp.float32),
-            jax.ShapeDtypeStruct((n, n), jnp.float32),
         ),
         in_specs=[pl.BlockSpec(memory_space=pltpu.SMEM), array, array],
-        out_specs=(array, array, array),
+        out_specs=(array, array),
         compiler_params=pltpu.CompilerParams(vmem_limit_bytes=16 * 1024 * 1024),
         cost_estimate=pl.CostEstimate(flops=4 * 10**9, bytes_accessed=0, transcendentals=0),
         name="begin_normal",
     )(count, prior, local_rows)
 
 
-def reduce_rows(count, band, owners, rows, normal, begun, global_rows, n_y):
+def reduce_rows(count, band, owners, rows, begun, global_rows, n_y):
     n, m = rows.shape
     scalar = pl.BlockSpec(memory_space=pltpu.SMEM)
     array = pl.BlockSpec(memory_space=pltpu.VMEM)
-    shapes = ((n_y * OB + KB, m), (n_y * OB, m), (3, n, m))
+    shapes = ((n_y * OB + KB, m), (n_y * OB, m), (2, n, m))
     return pl.pallas_call(
         functools.partial(local_kernel, n_y),
         out_shape=tuple(jax.ShapeDtypeStruct(shape, jnp.bfloat16) for shape in shapes),
-        in_specs=[scalar, scalar, array, array, array, array, array],
+        in_specs=[scalar, scalar, array, array, array, array],
         out_specs=tuple(array for _ in shapes),
         scratch_shapes=[pltpu.VMEM((n, n), jnp.float32)],
         compiler_params=pltpu.CompilerParams(vmem_limit_bytes=24 * 1024 * 1024),
         name="reduce_rows",
-    )(count, band, owners, rows, normal, begun, global_rows)
+    )(count, band, owners, rows, begun, global_rows)
 
 
 def own_product_kernel(
@@ -259,9 +243,9 @@
     z, x, _, _ = place_of()
     border = send_ref[n_y * OB :, :]
     local_rows = rows_ref[...]
-    for t in range(n_y * OB // KB):
-        tile = own_ref[t * KB : (t + 1) * KB, :]
-        mine_ref[t * KB : (t + 1) * KB, :] = solve_rows(tile, gain_ref, local_rows)
+    for t in range(n_y):
+        tile = own_ref[t * OB : (t + 1) * OB, :]
+        mine_ref[t * OB : (t + 1) * OB, :] = solve_rows(tile, gain_ref, local_rows)
     for y in range(n_y):
         order_rows(n_z, z, x, mine_ref, y, left)
         prod_ref[y, :, :OB] = mm(left[...], mine_ref[y * OB : (y + 1) * OB, :], INNER)
@@ -472,17 +456,6 @@
     return jnp.concatenate([head, values * jnp.exp2(TOP_LEVEL - level)]).astype(jnp.float16)
 
 
-def fold(message):
-    parts = HALF // P_SIZE
-    step = message.shape[0] // parts
-    return jnp.concatenate([message[i * step : (i + 1) * step] for i in range(parts)], axis=1)
-
-
-def unfold(rows):
-    parts = HALF // P_SIZE
-    return jnp.concatenate([rows[:, i * P_SIZE : (i + 1) * P_SIZE] for i in range(parts)], axis=0)
-
-
 def pairwise(terms):
     while len(terms) > 1:
         terms = [terms[2 * i] + terms[2 * i + 1] for i in range(len(terms) // 2)]
@@ -504,13 +477,12 @@
                 pairs.append((a * n_coef + c, to_a * n_coef + to_c))
         return lax.ppermute(values, AXES, pairs)
 
-    local_rows, normal, begun = begin_normal(obs_count, local_prior, local_design[0])
+    local_rows, begun = begin_normal(obs_count, local_prior, local_design[0])
     send, own, gain = reduce_rows(
         obs_count,
         band_mask,
         owner_columns.reshape(n_coef, OB // LANES, LANES),
         local_rows,
-        normal,
         begun,
         global_design[0],
         n_y,
@@ -525,7 +497,6 @@
     from_x = swap(send_x.astype(jnp.float16), dx=1)
     panels = panel_products(mine, other, level, n_y).astype(jnp.float16)
     panel_z = [panels] + [swap(panels, dz=j) for j in range(1, n_z)]
-    from_y, from_x, panel_z = lax.optimization_barrier((from_y, from_x, panel_z))
 
     left = functools.reduce(jnp.add, [values_of(message) for message in from_y], keep_y)
     left_level = functools.reduce(
@@ -533,26 +504,22 @@
     ) + grown
     right = keep_x + values_of(from_x).reshape(n_y, half, HALF)
     right_level = jnp.maximum(level[:1], level_of(from_x)) + 1.0
+
+    over_x = message_of(left[half:], left_level)
+    over_y = [message_of(right[j], right_level) for j in range(1, n_y)]
+    over_x, over_y = lax.optimization_barrier((over_x, over_y))
+    panel_z, _ = lax.optimization_barrier((panel_z, (over_x, over_y)))
+    from_x = swap(over_x, dx=1)
+    from_y = [swap(over_y[j - 1], dy=j) for j in range(1, n_y)]
+    from_x, from_y = lax.optimization_barrier((from_x, from_y))
     panel_level = functools.reduce(jnp.maximum, [level_of(p[0]) for p in panel_z])
     panel_level = panel_level + float(n_z.bit_length() - 1)
     panels = [
         message_of(pairwise([values_of(message[j]) for message in panel_z]), panel_level)
         for j in range(n_y)
     ]
-
-    over_x = jnp.concatenate([message_of(left[half:], left_level), fold(panels[0])])
-    over_y = [
-        jnp.concatenate([message_of(right[j], right_level), fold(panels[j])])
-        for j in range(1, n_y)
-    ]
-    over_x, over_y, panels = lax.optimization_barrier((over_x, over_y, panels))
-    from_x = swap(over_x, dx=1)
-    from_y = [swap(over_y[j - 1], dy=j) for j in range(1, n_y)]
-    panel_xy = [swap(panels[j], dx=1, dy=j) for j in range(1, n_y)]
-    tail = (HEAD + P_SIZE) * P_SIZE // HALF
-    panel_y = [panels[0]] + [unfold(message[-tail:]) for message in from_y]
-    panel_x = [unfold(from_x[-tail:])] + panel_xy
-    from_x, from_y = from_x[:-tail], [message[:-tail] for message in from_y]
+    panel_y = [panels[0]] + [swap(panels[j], dy=j) for j in range(1, n_y)]
+    panel_x = [swap(panels[j], dx=1, dy=j) for j in range(n_y)]
     left = left[:half] + values_of(from_x)
     left_level = jnp.maximum(left_level, level_of(from_x)) + 1.0
     right = functools.reduce(jnp.add, [values_of(message) for message in from_y], right[0])
@@ -563,12 +530,12 @@
     total = jnp.concatenate([left, right], axis=1)
     level = jnp.concatenate([left_level, right_level], axis=1)
     over_z = [message_of(total[j * rows : (j + 1) * rows], level) for j in range(1, n_z)]
-    over_z, panel_x, panel_y = lax.optimization_barrier((over_z, panel_x, panel_y))
     from_z = [swap(over_z[j - 1], dz=j) for j in range(1, n_z)]
-    from_z[0], panel_x, panel_y = lax.optimization_barrier((from_z[0], panel_x, panel_y))
+    panel_x, panel_y, _ = lax.optimization_barrier((panel_x, panel_y, over_z))
     panel = functools.reduce(jnp.add, [values_of(message) for message in panel_y])
     panel = panel + functools.reduce(jnp.add, [values_of(message) for message in panel_x])
     panel_factor = factor_panel(panel, kaula_prior)
+    from_z, panel_factor = lax.optimization_barrier((from_z, panel_factor))
     normal_rows = functools.reduce(
         jnp.add, [values_of(message) for message in from_z], total[:rows]
     )

time: 61.4 us -> 53.6 us (0.87)
  waiting for transfers between devices: 13.5 us -> 6.23 us
  Pallas kernels: 25.3 us -> 22.5 us
  starting transfers between devices: 17.1 us -> 19.4 us
    ppermute x12 -> x14, waiting for transfers between devices: 13.5 us -> 6.23 us  [swap(): return lax.ppermute(values, AXES, pairs)]
    ppermute x12 -> x14, starting transfers between devices: 17.1 us -> 19.4 us  [swap(): return lax.ppermute(values, AXES, pairs)]
    pallas_call x1, Pallas kernels: 12.4 us -> 10.1 us  [reduce_rows(): pl.pallas_call(functools.partial(local_kernel, n_y), out_shape=tuple((jax...]
    pallas_call x1, Pallas kernels: 3.53 us -> 2.75 us  [own_products(): pl.pallas_call(functools.partial(own_product_kernel, n_y, n_z), out_shape...]
  transfers between devices with their start and end apart: 12 -> 14, of which waited for: 7 -> 5; matrix products, arithmetic and copies ran while one was open for 1% -> 2% of each run, Pallas kernels for 16% -> 16%
where the time goes in v4:
time: 53.6 us; the launch traced here: 53.4 us
  Pallas kernels  22.5 us (42%)
  starting transfers between devices  19.4 us (36%)
  waiting for transfers between devices  6.23 us (12%)
  other arithmetic  2.02 us (4%)
  local copies, waits for them, and re-layouts  1.67 us (3%)
  between operations  1.59 us (3%)
    ppermute x14, starting transfers between devices, swap(): return lax.ppermute(values, AXES, pairs)  19.4 us
    pallas_call x1, Pallas kernels, reduce_rows(): pl.pallas_call(functools.partial(local_kernel, n_y), out_shape=tuple((jax...  10.1 us
    ppermute x14, waiting for transfers between devices, swap(): return lax.ppermute(values, AXES, pairs)  6.23 us
    pallas_call x1, Pallas kernels, factor_panel(): pl.pallas_call(factor_kernel, out_shape=jax.ShapeDtypeStruct((n, n), jnp....  5.11 us
    pallas_call x1, Pallas kernels, own_products(): pl.pallas_call(functools.partial(own_product_kernel, n_y, n_z), out_shape...  2.75 us
    pallas_call x1, Pallas kernels, begin_normal(): pl.pallas_call(normal_kernel, out_shape=(jax.ShapeDtypeStruct((n, m), jnp...  2.21 us
    unnamed x12, local copies, waits for them, and re-layouts  1.64 us
    pallas_call x1, Pallas kernels, products(): pl.pallas_call(functools.partial(product_kernel, n_y, n_z), out_shape=tup...  1.41 us
  transfers between devices with their start and end apart: 14, of which 5 were waited for; matrix products, arithmetic and copies ran while one was open for 2% of the time, Pallas kernels for 16%

profile of v4, /device:TPU:0, one launch (start us, length us, event | category | flops | bytes accessed | tf_op | source)
XLA Modules:
  0.0 53.4 jit_solution(4596056458663675812)
XLA Ops:
  1.3 0.9 %copy-done.4 = bf16[1,256,512]{2,1,0:T(8,128)(2,1)S(1)} copy-done((bf16[1,256,512]{2,1,0:T(8,128)(2,1)S(1)}, bf16[1,256,512]{2,1,0:T(8,128)(2,1)}, u32[]{:S(2)}) %copy-start.4) | copy-done | bytes 262168
  2.2 0.7 %copy-done.5 = f32[1,256]{1,0:T(1,128)S(1)} copy-done((f32[1,256]{1,0:T(1,128)S(1)}, f32[1,256]{1,0:T(1,128)}, u32[]{:S(2)}) %copy-start.5) | copy-done | bytes 1048
  2.9 2.2 %begin_normal.1 = (bf16[256,512]{1,0:T(8,128)(2,1)S(1)}, f32[256,256]{1,0:T(8,128)S(1)}) custom-call(s32[1]{0:T(128)S(6)} %copy.9.count_ref, f32[1,256]{1,0:T(1,128)S(1)} %copy-done.5, bf16[256,512]{1,0:T(8,128)(2,1)S(1)} %bitcast.73), custom_call_target="tpu_custom_call" | custom-call | flops 4000000000 | tf_op jit(solution)/shard_map/begin_normal/pallas_call | solution.py:210
  5.2 10.1 %reduce_rows.1 = (bf16[1280,512]{1,0:T(8,128)(2,1)S(1)}, bf16[1024,512]{1,0:T(8,128)(2,1)S(1)}, bf16[2,256,512]{2,1,0:T(8,128)(2,1)S(1)}) custom-call(s32[1]{0:T(128)S(6)} %copy.9.count_ref, s32[1,4]{1,0:T(1,128)S(1)} %copy-done.3, s32[4,4,128]{2,1,0:T(4,128)S(1)} %bitcast.72, bf16[256,512]{1,0:T(8,128)(2,1)S(1)} %get-tuple-element.30.rows_ref, ...), custom_call_target="tpu_custom_call" | custom-call | tf_op jit(solution)/shard_map/reduce_rows/pallas_call | solution.py:229
  15.2 0.5 collective-permute-start
  15.7 2.8 %own_products.1 = (bf16[1024,512]{1,0:T(8,128)(2,1)S(1)}, f32[2,512,768]{2,1,0:T(8,128)S(1)}) custom-call(bf16[1024,512]{1,0:T(8,128)(2,1)S(1)} %get-tuple-element.33.own_ref, bf16[1280,512]{1,0:T(8,128)(2,1)S(1)} %get-tuple-element.32.send_ref, bf16[2,256,512]{2,1,0:T(8,128)(2,1)S(1)} %get-tuple-element.34.gain_ref, ...), custom_call_target="tpu_custom_call" | custom-call | flops 1610612736 | tf_op jit(solution)/shard_map/own_products/pallas_call | solution.py:314
  18.5 1.4 %products.1 = (f32[512,384]{1,0:T(8,128)S(1)}, f32[1,520,384]{2,1,0:T(8,128)S(1)}, f32[2,256,384]{2,1,0:T(8,128)S(1)}, f32[520,384]{1,0:T(8,128)S(1)}, f32[8,384]{1,0:T(8,128)S(1)}) custom-call(bf16[1280,512]{1,0:T(8,128)(2,1)S(1)} %collective-permute-done.other_ref, f32[2,512,768]{2,1,0:T(8,128)S(1)} %get-tuple-element.35.prod_ref), custom_call_target="tpu_custom_call" | custom-call | tf_op jit(solution)/shard_map/products/pallas_call | solution.py:342
  20.0 2.8 %collective-permute-start.2 = (f16[520,384]{1,0:T(8,128)(2,1)S(1)}, f16[520,384]{1,0:T(8,128)(2,1)S(1)}, u32[]{:S(2)}, u32[]{:S(2)}) collective-permute-start(f16[520,384]{1,0:T(8,128)(2,1)S(1)} %convert_element_type.241), channel_id=1, source_target_pairs={{0,4},{1,5},{2,6},{3,7},{4,0},{5,1},{6,2},{7,3},{8,12},{9,13},{10,... | collective-permute-start | bytes 1198088 | tf_op jit(solution)/shard_map/ppermute | solution.py:478
  22.9 1.5 %collective-permute-start.1 = (f16[520,384]{1,0:T(8,128)(2,1)S(1)}, f16[520,384]{1,0:T(8,128)(2,1)S(1)}, u32[]{:S(2)}, u32[]{:S(2)}) collective-permute-start(f16[520,384]{1,0:T(8,128)(2,1)S(1)} %convert_bitcast_fusion), channel_id=1, source_target_pairs={{0,2},{1,3},{2,0},{3,1},{4,6},{5,7},{6,4},{7,5},{8,10},{9,11},{10,... | collective-permute-start | bytes 1198088 | tf_op jit(solution)/shard_map/ppermute | solution.py:478
  24.4 0.9 %panel_products.1 = f32[2,136,128]{2,1,0:T(8,128)S(1)} custom-call(bf16[1024,512]{1,0:T(8,128)(2,1)S(1)} %get-tuple-element.45.mine_ref, bf16[1280,512]{1,0:T(8,128)(2,1)S(1)} %collective-permute-done.other_ref, f32[8,384]{1,0:T(8,128)S(1)} %get-tuple-element.38.level_ref), custom_call_target="tpu_custom_call" | custom-call | flops 268435456 | tf_op jit(solution)/shard_map/panel_products/pallas_call | solution.py:358
  25.3 3.7 %collective-permute-start.10 = (f16[2,136,128]{2,1,0:T(8,128)(2,1)S(1)}, f16[2,136,128]{2,1,0:T(8,128)(2,1)S(1)}, u32[]{:S(2)}, u32[]{:S(2)}) collective-permute-start(f16[2,136,128]{2,1,0:T(8,128)(2,1)S(1)} %convert_element_type.248), channel_id=1, source_target_pairs={{0,24},{1,25},{2,26},{3,27},{4,28},{5,29},{6,30},{7,31},{8,16},{9,... | collective-permute-start | bytes 208904 | tf_op jit(solution)/shard_map/ppermute | solution.py:478
  29.0 0.8 %collective-permute-start.8 = (f16[2,136,128]{2,1,0:T(8,128)(2,1)S(1)}, f16[2,136,128]{2,1,0:T(8,128)(2,1)S(1)}, u32[]{:S(2)}, u32[]{:S(2)}) collective-permute-start(f16[2,136,128]{2,1,0:T(8,128)(2,1)S(1)} %convert_element_type.248), channel_id=1, source_target_pairs={{0,8},{1,9},{2,10},{3,11},{4,12},{5,13},{6,14},{7,15},{8,0},{9,1},... | collective-permute-start | bytes 208904 | tf_op jit(solution)/shard_map/ppermute | solution.py:478
  29.8 2.7 %collective-permute-done.2 = f16[520,384]{1,0:T(8,128)(2,1)S(1)} collective-permute-done((f16[520,384]{1,0:T(8,128)(2,1)S(1)}, f16[520,384]{1,0:T(8,128)(2,1)S(1)}, u32[]{:S(2)}, u32[]{:S(2)}) %collective-permute-start.2) | collective-permute-done | bytes 399392 | tf_op jit(solution)/shard_map/ppermute | solution.py:478
  32.5 1.5 %collective-permute-done.1 = f16[520,384]{1,0:T(8,128)(2,1)S(1)} collective-permute-done((f16[520,384]{1,0:T(8,128)(2,1)S(1)}, f16[520,384]{1,0:T(8,128)(2,1)S(1)}, u32[]{:S(2)}, u32[]{:S(2)}) %collective-permute-start.1) | collective-permute-done | bytes 399392 | tf_op jit(solution)/shard_map/ppermute | solution.py:478
  34.6 0.4 collective-permute-start.3
  35.1 1.7 %collective-permute-start.4 = (f16[264,384]{1,0:T(8,128)(2,1)S(1)}, f16[264,384]{1,0:T(8,128)(2,1)S(1)}, u32[]{:S(2)}, u32[]{:S(2)}) collective-permute-start(f16[264,384]{1,0:T(8,128)(2,1)S(1)} %pad_maximum_fusion.1), channel_id=1, source_target_pairs={{0,2},{1,3},{2,0},{3,1},{4,6},{5,7},{6,4},{7,5},{8,10},{9,11},{10,... | collective-permute-start | bytes 608264 | tf_op jit(solution)/shard_map/ppermute | solution.py:478
  37.3 2.6 %collective-permute-start.12 = (f16[136,128]{1,0:T(8,128)(2,1)S(1)}, f16[136,128]{1,0:T(8,128)(2,1)S(1)}, u32[]{:S(2)}, u32[]{:S(2)}) collective-permute-start(f16[136,128]{1,0:T(8,128)(2,1)S(1)} %get-tuple-element.90), channel_id=1, source_target_pairs={{0,6},{1,7},{2,4},{3,5},{4,2},{5,3},{6,0},{7,1},{8,14},{9,15},{10,... | collective-permute-start | bytes 104456 | tf_op jit(solution)/shard_map/ppermute | solution.py:478
  40.0 0.5 collective-permute-start.11
  40.5 1.0 %collective-permute-done.3 = f16[264,384]{1,0:T(8,128)(2,1)S(1)} collective-permute-done((f16[264,384]{1,0:T(8,128)(2,1)S(1)}, f16[264,384]{1,0:T(8,128)(2,1)S(1)}, u32[]{:S(2)}, u32[]{:S(2)}) %collective-permute-start.3) | collective-permute-done | bytes 202784 | tf_op jit(solution)/shard_map/ppermute | solution.py:478
  42.3 3.6 %collective-permute-start.7 = (f16[72,768]{1,0:T(8,128)(2,1)S(1)}, f16[72,768]{1,0:T(8,128)(2,1)S(1)}, u32[]{:S(2)}, u32[]{:S(2)}) collective-permute-start(f16[72,768]{1,0:T(8,128)(2,1)S(1)} %get-tuple-element.85), channel_id=1, source_target_pairs={{0,24},{1,25},{2,26},{3,27},{4,28},{5,29},{6,30},{7,31},{8,16},{9,... | collective-permute-start | bytes 331784 | tf_op jit(solution)/shard_map/ppermute | solution.py:478
  45.9 0.9 %collective-permute-start.5 = (f16[72,768]{1,0:T(8,128)(2,1)S(1)}, f16[72,768]{1,0:T(8,128)(2,1)S(1)}, u32[]{:S(2)}, u32[]{:S(2)}) collective-permute-start(f16[72,768]{1,0:T(8,128)(2,1)S(1)} %get-tuple-element.87), channel_id=1, source_target_pairs={{0,8},{1,9},{2,10},{3,11},{4,12},{5,13},{6,14},{7,15},{8,0},{9,1},... | collective-permute-start | bytes 331784 | tf_op jit(solution)/shard_map/ppermute | solution.py:478
  46.8 5.1 %factor_panel.1 = f32[128,128]{1,0:T(8,128)} custom-call(f32[128,128]{1,0:T(8,128)S(1)} %add_add_fusion.panel_ref, f32[1,128]{1,0:T(1,128)S(1)} %copy-done.2), custom_call_target="tpu_custom_call" | custom-call | flops 2097152 | bytes 196608 | tf_op jit(solution)/shard_map/factor_panel/pallas_call | solution.py:436
  51.9 0.6 %collective-permute-done.6 = f16[72,768]{1,0:T(8,128)(2,1)S(1)} collective-permute-done((f16[72,768]{1,0:T(8,128)(2,1)S(1)}, f16[72,768]{1,0:T(8,128)(2,1)S(1)}, u32[]{:S(2)}, u32[]{:S(2)}) %collective-permute-start.6) | collective-permute-done | bytes 110624 | tf_op jit(solution)/shard_map/ppermute | solution.py:478
  52.6 0.8 %fusion.11 = f32[1,64,768]{2,1,0:T(8,128)} fusion(f32[256,384]{1,0:T(8,128)S(1)} %slice_add_fusion, f32[256,384]{1,0:T(8,128)S(1)} %fusion, f32[768]{0:T(1024)S(1)} %exponential_reduce_fusion, f16[72,768]{1,0:T(8,128)(2,1)S(1)} %collective-permute-done.7, f32[768]{0:T(1024)S(1)} %exponential_reduce_fusion.1, f16[72,768]{1,0:T(8,128)(2,1)S(1)} %collective-permute-done.6, ...), kind=kLoop, calls=%fused_computation.26 | loop fusion | flops 491520 | bytes 1287168 | tf_op jit(solution)/shard_map/broadcast_in_dim | solution.py:542
  (61 shorter events, 2.1 us)
Async XLA Ops:
  1.3 1.0 %copy-start.4 = (bf16[1,256,512]{2,1,0:T(8,128)(2,1)S(1)}, bf16[1,256,512]{2,1,0:T(8,128)(2,1)}, u32[]{:S(2)}) copy-start(bf16[1,256,512]{2,1,0:T(8,128)(2,1)} %param.7) | copy-start | bytes 786436
  2.2 0.7 %copy-start.5 = (f32[1,256]{1,0:T(1,128)S(1)}, f32[1,256]{1,0:T(1,128)}, u32[]{:S(2)}) copy-start(f32[1,256]{1,0:T(1,128)} %prior_ref.2) | copy-start | bytes 3076
  2.9 2.2 %copy-start = (bf16[1,2304,512]{2,1,0:T(8,128)(2,1)S(1)}, bf16[1,2304,512]{2,1,0:T(8,128)(2,1)}, u32[]{:S(2)}) copy-start(bf16[1,2304,512]{2,1,0:T(8,128)(2,1)} %param.8) | copy-start | bytes 7077892
  2.9 2.2 %copy-start.1 = (s32[2048]{0:T(1024)S(1)}, s32[2048]{0:T(1024)}, u32[]{:S(2)}) copy-start(s32[2048]{0:T(1024)} %param.12) | copy-start | bytes 24580
  2.9 2.2 %copy-start.3 = (s32[1,4]{1,0:T(1,128)S(1)}, s32[1,4]{1,0:T(1,128)}, u32[]{:S(2)}) copy-start(s32[1,4]{1,0:T(1,128)} %band_ref.1) | copy-start | bytes 52
  15.2 3.3 %collective-permute-start = (bf16[1280,512]{1,0:T(8,128)(2,1)S(1)}, bf16[1280,512]{1,0:T(8,128)(2,1)S(1)}, u32[]{:S(2)}, u32[]{:S(2)}) collective-permute-start(bf16[1280,512]{1,0:T(8,128)(2,1)S(1)} %get-tuple-element.32.send_ref), channel_id=1, source_target_pairs={{0,1},{1,0},{2,3},{3,2},{4,5},{5,4},{6,7},{7,6},{8,9},{9,8},{10,11... | collective-permute-start | bytes 3932168 | tf_op jit(solution)/shard_map/ppermute | solution.py:478
  20.0 12.5 %collective-permute-start.2 = (f16[520,384]{1,0:T(8,128)(2,1)S(1)}, f16[520,384]{1,0:T(8,128)(2,1)S(1)}, u32[]{:S(2)}, u32[]{:S(2)}) collective-permute-start(f16[520,384]{1,0:T(8,128)(2,1)S(1)} %convert_element_type.241), channel_id=1, source_target_pairs={{0,4},{1,5},{2,6},{3,7},{4,0},{5,1},{6,2},{7,3},{8,12},{9,13},{10,... | collective-permute-start | bytes 1198088 | tf_op jit(solution)/shard_map/ppermute | solution.py:478
  22.9 11.1 %collective-permute-start.1 = (f16[520,384]{1,0:T(8,128)(2,1)S(1)}, f16[520,384]{1,0:T(8,128)(2,1)S(1)}, u32[]{:S(2)}, u32[]{:S(2)}) collective-permute-start(f16[520,384]{1,0:T(8,128)(2,1)S(1)} %convert_bitcast_fusion), channel_id=1, source_target_pairs={{0,2},{1,3},{2,0},{3,1},{4,6},{5,7},{6,4},{7,5},{8,10},{9,11},{10,... | collective-permute-start | bytes 1198088 | tf_op jit(solution)/shard_map/ppermute | solution.py:478
  25.3 11.4 %collective-permute-start.10 = (f16[2,136,128]{2,1,0:T(8,128)(2,1)S(1)}, f16[2,136,128]{2,1,0:T(8,128)(2,1)S(1)}, u32[]{:S(2)}, u32[]{:S(2)}) collective-permute-start(f16[2,136,128]{2,1,0:T(8,128)(2,1)S(1)} %convert_element_type.248), channel_id=1, source_target_pairs={{0,24},{1,25},{2,26},{3,27},{4,28},{5,29},{6,30},{7,31},{8,16},{9,... | collective-permute-start | bytes 208904 | tf_op jit(solution)/shard_map/ppermute | solution.py:478
  29.0 7.8 %collective-permute-start.9 = (f16[2,136,128]{2,1,0:T(8,128)(2,1)S(1)}, f16[2,136,128]{2,1,0:T(8,128)(2,1)S(1)}, u32[]{:S(2)}, u32[]{:S(2)}) collective-permute-start(f16[2,136,128]{2,1,0:T(8,128)(2,1)S(1)} %convert_element_type.248), channel_id=1, source_target_pairs={{0,16},{1,17},{2,18},{3,19},{4,20},{5,21},{6,22},{7,23},{8,24},{9,... | collective-permute-start | bytes 208904 | tf_op jit(solution)/shard_map/ppermute | solution.py:478
  29.0 7.8 %collective-permute-start.8 = (f16[2,136,128]{2,1,0:T(8,128)(2,1)S(1)}, f16[2,136,128]{2,1,0:T(8,128)(2,1)S(1)}, u32[]{:S(2)}, u32[]{:S(2)}) collective-permute-start(f16[2,136,128]{2,1,0:T(8,128)(2,1)S(1)} %convert_element_type.248), channel_id=1, source_target_pairs={{0,8},{1,9},{2,10},{3,11},{4,12},{5,13},{6,14},{7,15},{8,0},{9,1},... | collective-permute-start | bytes 208904 | tf_op jit(solution)/shard_map/ppermute | solution.py:478
  34.6 12.3 %copy-start.2 = (f32[1,128]{1,0:T(1,128)S(1)}, f32[1,128]{1,0:T(1,128)}, u32[]{:S(2)}) copy-start(f32[1,128]{1,0:T(1,128)} %prior_ref.3) | copy-start | bytes 1540
  34.6 6.8 %collective-permute-start.3 = (f16[264,384]{1,0:T(8,128)(2,1)S(1)}, f16[264,384]{1,0:T(8,128)(2,1)S(1)}, u32[]{:S(2)}, u32[]{:S(2)}) collective-permute-start(f16[264,384]{1,0:T(8,128)(2,1)S(1)} %pad_maximum_fusion), channel_id=1, source_target_pairs={{0,4},{1,5},{2,6},{3,7},{4,0},{5,1},{6,2},{7,3},{8,12},{9,13},{10,... | collective-permute-start | bytes 608264 | tf_op jit(solution)/shard_map/ppermute | solution.py:478
  35.1 6.8 %collective-permute-start.4 = (f16[264,384]{1,0:T(8,128)(2,1)S(1)}, f16[264,384]{1,0:T(8,128)(2,1)S(1)}, u32[]{:S(2)}, u32[]{:S(2)}) collective-permute-start(f16[264,384]{1,0:T(8,128)(2,1)S(1)} %pad_maximum_fusion.1), channel_id=1, source_target_pairs={{0,2},{1,3},{2,0},{3,1},{4,6},{5,7},{6,4},{7,5},{8,10},{9,11},{10,... | collective-permute-start | bytes 608264 | tf_op jit(solution)/shard_map/ppermute | solution.py:478
  36.9 8.9 %collective-permute-start.13 = (f16[136,128]{1,0:T(8,128)(2,1)S(1)}, f16[136,128]{1,0:T(8,128)(2,1)S(1)}, u32[]{:S(2)}, u32[]{:S(2)}) collective-permute-start(f16[136,128]{1,0:T(8,128)(2,1)S(1)} %get-tuple-element.90), channel_id=1, source_target_pairs={{0,2},{1,3},{2,0},{3,1},{4,6},{5,7},{6,4},{7,5},{8,10},{9,11},{10,... | collective-permute-start | bytes 104456 | tf_op jit(solution)/shard_map/ppermute | solution.py:478
  37.3 9.4 %collective-permute-start.12 = (f16[136,128]{1,0:T(8,128)(2,1)S(1)}, f16[136,128]{1,0:T(8,128)(2,1)S(1)}, u32[]{:S(2)}, u32[]{:S(2)}) collective-permute-start(f16[136,128]{1,0:T(8,128)(2,1)S(1)} %get-tuple-element.90), channel_id=1, source_target_pairs={{0,6},{1,7},{2,4},{3,5},{4,2},{5,3},{6,0},{7,1},{8,14},{9,15},{10,... | collective-permute-start | bytes 104456 | tf_op jit(solution)/shard_map/ppermute | solution.py:478
  40.0 6.8 %collective-permute-start.11 = (f16[136,128]{1,0:T(8,128)(2,1)S(1)}, f16[136,128]{1,0:T(8,128)(2,1)S(1)}, u32[]{:S(2)}, u32[]{:S(2)}) collective-permute-start(f16[136,128]{1,0:T(8,128)(2,1)S(1)} %get-tuple-element.50), channel_id=1, source_target_pairs={{0,4},{1,5},{2,6},{3,7},{4,0},{5,1},{6,2},{7,3},{8,12},{9,13},{10,... | collective-permute-start | bytes 104456 | tf_op jit(solution)/shard_map/ppermute | solution.py:478
  42.3 9.7 %collective-permute-start.7 = (f16[72,768]{1,0:T(8,128)(2,1)S(1)}, f16[72,768]{1,0:T(8,128)(2,1)S(1)}, u32[]{:S(2)}, u32[]{:S(2)}) collective-permute-start(f16[72,768]{1,0:T(8,128)(2,1)S(1)} %get-tuple-element.85), channel_id=1, source_target_pairs={{0,24},{1,25},{2,26},{3,27},{4,28},{5,29},{6,30},{7,31},{8,16},{9,... | collective-permute-start | bytes 331784 | tf_op jit(solution)/shard_map/ppermute | solution.py:478
  45.9 6.7 %collective-permute-start.6 = (f16[72,768]{1,0:T(8,128)(2,1)S(1)}, f16[72,768]{1,0:T(8,128)(2,1)S(1)}, u32[]{:S(2)}, u32[]{:S(2)}) collective-permute-start(f16[72,768]{1,0:T(8,128)(2,1)S(1)} %get-tuple-element.86), channel_id=1, source_target_pairs={{0,16},{1,17},{2,18},{3,19},{4,20},{5,21},{6,22},{7,23},{8,24},{9,... | collective-permute-start | bytes 331784 | tf_op jit(solution)/shard_map/ppermute | solution.py:478
  45.9 6.7 %collective-permute-start.5 = (f16[72,768]{1,0:T(8,128)(2,1)S(1)}, f16[72,768]{1,0:T(8,128)(2,1)S(1)}, u32[]{:S(2)}, u32[]{:S(2)}) collective-permute-start(f16[72,768]{1,0:T(8,128)(2,1)S(1)} %get-tuple-element.87), channel_id=1, source_target_pairs={{0,8},{1,9},{2,10},{3,11},{4,12},{5,13},{6,14},{7,15},{8,0},{9,1},... | collective-permute-start | bytes 331784 | tf_op jit(solution)/shard_map/ppermute | solution.py:478

commit v5 on v4

--- a/solution.py
+++ b/solution.py
@@ -12,7 +12,6 @@
 P_SIZE = 128
 STRIDE = OB // P_SIZE
 WIDTH = OB + KB
-HALF = WIDTH // 2
 PAIR = 2
 TOP_LEVEL = 12.0
 HEAD = 8
@@ -162,7 +161,7 @@
     count = count_ref[0]
     _, _, y, core = place_of()
     work_ref[...] = begun_ref[...]
-    lane = lax.broadcasted_iota(jnp.int32, (TILE, LANES), 1)
+    lane = lax.broadcasted_iota(jnp.int32, (TILE, LANES), 1).astype(jnp.int16)
     used = lax.broadcasted_iota(jnp.int32, (TILE, m), 1) < count
 
     def gather_rows(t):
@@ -173,12 +172,14 @@
         for r in range(TILE // LANES):
             at = part // LANES + r
             ids = owner_ref[owner, at : at + 1, :].astype(jnp.float32)
-            wanted.append(jnp.broadcast_to(ids, (LANES, LANES)).T.astype(jnp.int32))
+            ids = jnp.broadcast_to(ids, (LANES, LANES)).T
+            wanted.append(ids.astype(jnp.int32).astype(jnp.int16))
         wanted = jnp.concatenate(wanted, axis=0)
-        hot = []
+        hot, nothing = [], jnp.zeros((TILE, LANES), jnp.bfloat16)
         for k in range(owned // LANES):
-            sensed = band_ref[0, k * LANES // OB].astype(jnp.float32)
-            hot.append(jnp.where(wanted == lane + k * LANES, sensed, 0.0).astype(jnp.bfloat16))
+            sensed = band_ref[0, k * LANES // OB].astype(jnp.float32).astype(jnp.bfloat16)
+            sensed = jnp.full((TILE, LANES), sensed)
+            hot.append(jnp.where(wanted == lane + jnp.int16(k * LANES), sensed, nothing))
         got = mm(jnp.concatenate(hot, axis=1), global_ref[0:owned, :])
         got = jnp.where(used, got, 0.0).astype(jnp.bfloat16)
         if t * TILE < mine:
@@ -238,7 +239,7 @@
 
 
 def own_product_kernel(
-    n_y, n_z, own_ref, send_ref, gain_ref, rows_ref, mine_ref, prod_ref, left
+    n_y, n_z, own_ref, send_ref, gain_ref, rows_ref, mine_ref, square_ref, side_ref, left
 ):
     z, x, _, _ = place_of()
     border = send_ref[n_y * OB :, :]
@@ -247,9 +248,12 @@
         tile = own_ref[t * OB : (t + 1) * OB, :]
         mine_ref[t * OB : (t + 1) * OB, :] = solve_rows(tile, gain_ref, local_rows)
     for y in range(n_y):
+        for g in range(OB // LANES):
+            low, high = g * LANES, (g + 1) * LANES
+            rows = mine_ref[y * OB + low : y * OB + high, :]
+            square_ref[y, low:high, :high] = mm(rows, mine_ref[y * OB : y * OB + high, :], INNER)
         order_rows(n_z, z, x, mine_ref, y, left)
-        prod_ref[y, :, :OB] = mm(left[...], mine_ref[y * OB : (y + 1) * OB, :], INNER)
-        prod_ref[y, :, OB:] = mm(left[...], border, INNER)
+        side_ref[y] = mm(left[...], border, INNER)
 
 
 def order_rows(n_z, z, x, rows_ref, y, left):
@@ -261,35 +265,72 @@
             left[at : at + rows, :] = rows_ref[pl.ds(source, rows), :]
 
 
+def lower_blocks():
+    return [(g, t) for g in range(OB // LANES) for t in range(g + 1)]
+
+
 def product_kernel(
-    n_y, n_z, other_ref, prod_ref,
-    keep_y_ref, send_y_ref, keep_x_ref, send_x_ref, level_ref, left, total,
+    n_y, n_z, other_ref, square_ref, side_ref,
+    keep_y_ref, send_y_ref, keep_x_ref, send_x_ref, level_ref, left, square, side,
 ):
     z, x, _, _ = place_of()
     half = OB // PAIR
     border = other_ref[n_y * OB :, :]
     top = jnp.zeros((BLOCK, LANES), jnp.float32)
+
+    def raised(top, value):
+        count = value.shape[0]
+        value = jnp.abs(value).reshape(count // BLOCK, BLOCK, LANES)
+        return jnp.maximum(top, jnp.max(value, axis=0))
+
     for y in range(n_y):
+        for g in range(OB // LANES):
+            low, high = g * LANES, (g + 1) * LANES
+            rows = other_ref[y * OB + low : y * OB + high, :]
+            square[y, low:high, :high] = square_ref[y, low:high, :high] + mm(
+                rows, other_ref[y * OB : y * OB + high, :], INNER
+            )
+            for t in range(g + 1):
+                top = raised(top, square[y, low:high, t * LANES : (t + 1) * LANES])
         order_rows(n_z, z, x, other_ref, y, left)
-        own = other_ref[y * OB : (y + 1) * OB, :]
-        total[y, :, :OB] = prod_ref[y, :, :OB] + mm(left[...], own, INNER)
-        total[y, :, OB:] = prod_ref[y, :, OB:] + mm(left[...], border, INNER)
-        for h in range(WIDTH // LANES):
-            part = jnp.abs(total[y, :, h * LANES : (h + 1) * LANES])
-            top = jnp.maximum(top, jnp.max(part.reshape(OB // BLOCK, BLOCK, LANES), axis=0))
+        side[y] = side_ref[y] + mm(left[...], border, INNER)
+        for h in range(KB // LANES):
+            top = raised(top, side[y, :, h * LANES : (h + 1) * LANES])
     top = jnp.max(jnp.max(top, axis=0, keepdims=True), axis=1, keepdims=True)
-    level = jnp.floor(jnp.log2(jnp.maximum(jnp.broadcast_to(top, (BLOCK, HALF)), 1e-30)))
+    level = jnp.floor(jnp.log2(jnp.maximum(jnp.broadcast_to(top, (BLOCK, OB)), 1e-30)))
     level_ref[...] = level
-    scale = jnp.exp2(TOP_LEVEL - level[:1])
-    keep_y_ref[...] = total[0, :, :HALF]
+    scale = jnp.exp2(TOP_LEVEL - level[:1, :KB])
     for j in range(1, n_y):
-        send_y_ref[j - 1, :HEAD, :] = jnp.broadcast_to(level[:1], (HEAD, HALF))
-        send_y_ref[j - 1, HEAD:, :] = total[j, :, :HALF] * scale
-    send_x_ref[:HEAD, :] = jnp.broadcast_to(level[:1], (HEAD, HALF))
+        send_y_ref[j - 1, :HEAD, :] = jnp.broadcast_to(level[:1, :LANES], (HEAD, LANES))
+    for i, (g, t) in enumerate(lower_blocks()):
+        rows, columns = slice(g * LANES, (g + 1) * LANES), slice(t * LANES, (t + 1) * LANES)
+        keep_y_ref[i * LANES : (i + 1) * LANES, :] = square[0, rows, columns]
+        for j in range(1, n_y):
+            at = HEAD + i * LANES
+            send_y_ref[j - 1, at : at + LANES, :] = square[j, rows, columns] * scale[:, :LANES]
+    send_x_ref[:HEAD, :] = jnp.broadcast_to(level[:1, :KB], (HEAD, KB))
     for y in range(n_y):
-        keep_x_ref[y] = total[y, :half, HALF:]
+        keep_x_ref[y] = side[y, :half, :]
         at = HEAD + y * half
-        send_x_ref[at : at + half, :] = total[y, half:, HALF:] * scale
+        send_x_ref[at : at + half, :] = side[y, half:, :] * scale
+
+
+def expand_kernel(n_z, packed_ref, out_ref):
+    z, x, _, _ = place_of()
+    rows = OB // (n_z * PAIR)
+    place = {pair: i for i, pair in enumerate(lower_blocks())}
+    for g in range(OB // LANES):
+        for t in range(OB // LANES):
+            at = place[max(g, t), min(g, t)] * LANES
+            block = packed_ref[at : at + LANES, :]
+            block = block if t <= g else block.T
+            for b in range(LANES // rows):
+                arc = g * (LANES // rows) + b
+                to = (((arc % PAIR) ^ x) * n_z + ((arc // PAIR) ^ z)) * rows
+                to = pl.multiple_of(to, rows)
+                out_ref[pl.ds(to, rows), t * LANES : (t + 1) * LANES] = block[
+                    b * rows : (b + 1) * rows, :
+                ]
 
 
 def panel_kernel(n_y, mine_ref, other_ref, level_ref, out_ref):
@@ -299,13 +340,20 @@
     pick = pick.astype(jnp.float32).astype(jnp.bfloat16)
     level = level_ref[:1, :P_SIZE]
     scale = jnp.exp2(TOP_LEVEL - level)
+    half = P_SIZE // 2
+    row = lax.broadcasted_iota(jnp.int32, (half, P_SIZE), 0)
+    column = lax.broadcasted_iota(jnp.int32, (half, P_SIZE), 1) - half
     for y in range(n_y):
         panel = jnp.zeros((P_SIZE, P_SIZE), jnp.float32)
         for ref in (mine_ref, other_ref):
             strip = mm(pick, ref[y * OB : (y + 1) * OB, :]).astype(jnp.bfloat16)
             panel = panel + mm(strip, strip, INNER)
+        upper, lower = panel[:half], panel[half:]
+        corner = jnp.where(row >= column, pltpu.roll(upper, half, 1), lower)
+        spare = jnp.sum(jnp.where(row == column, lower, 0.0), axis=0, keepdims=True)
         out_ref[y, :HEAD, :] = jnp.broadcast_to(level, (HEAD, P_SIZE))
-        out_ref[y, HEAD:, :] = panel * scale
+        out_ref[y, HEAD : HEAD + half, :] = jnp.where(column < 0, lower, corner) * scale
+        out_ref[y, HEAD + half :, :] = jnp.broadcast_to(spare * scale, (BLOCK, P_SIZE))
 
 
 def own_products(own, send, gain, rows, n_y, n_z):
@@ -315,10 +363,11 @@
         functools.partial(own_product_kernel, n_y, n_z),
         out_shape=(
             jax.ShapeDtypeStruct(own.shape, jnp.bfloat16),
-            jax.ShapeDtypeStruct((n_y, OB, WIDTH), jnp.float32),
+            jax.ShapeDtypeStruct((n_y, OB, OB), jnp.float32),
+            jax.ShapeDtypeStruct((n_y, OB, KB), jnp.float32),
         ),
         in_specs=[array, array, array, array],
-        out_specs=(array, array),
+        out_specs=(array, array, array),
         scratch_shapes=[pltpu.VMEM((OB, m), jnp.bfloat16)],
         compiler_params=pltpu.CompilerParams(vmem_limit_bytes=24 * 1024 * 1024),
         cost_estimate=pl.CostEstimate(
@@ -328,36 +377,49 @@
     )(own, send, gain, rows)
 
 
-def products(other, own, n_y, n_z):
+def products(other, square, side, n_y, n_z):
     array = pl.BlockSpec(memory_space=pltpu.VMEM)
     m = other.shape[1]
-    half = OB // PAIR
+    half, packed = OB // PAIR, len(lower_blocks()) * LANES
     shapes = (
-        (OB, HALF),
-        (n_y - 1, HEAD + OB, HALF),
-        (n_y, half, HALF),
-        (HEAD + n_y * half, HALF),
-        (BLOCK, HALF),
+        (packed, LANES),
+        (n_y - 1, HEAD + packed, LANES),
+        (n_y, half, KB),
+        (HEAD + n_y * half, KB),
+        (BLOCK, OB),
     )
     return pl.pallas_call(
         functools.partial(product_kernel, n_y, n_z),
         out_shape=tuple(jax.ShapeDtypeStruct(shape, jnp.float32) for shape in shapes),
-        in_specs=[array, array],
+        in_specs=[array, array, array],
         out_specs=tuple(array for _ in shapes),
         scratch_shapes=[
             pltpu.VMEM((OB, m), jnp.bfloat16),
-            pltpu.VMEM((n_y, OB, WIDTH), jnp.float32),
+            pltpu.VMEM((n_y, OB, OB), jnp.float32),
+            pltpu.VMEM((n_y, OB, KB), jnp.float32),
         ],
         compiler_params=pltpu.CompilerParams(vmem_limit_bytes=24 * 1024 * 1024),
         name="products",
-    )(other, own)
+    )(other, square, side)
+
+
+def expand(packed, n_z):
+    array = pl.BlockSpec(memory_space=pltpu.VMEM)
+    return pl.pallas_call(
+        functools.partial(expand_kernel, n_z),
+        out_shape=jax.ShapeDtypeStruct((OB, OB), jnp.float32),
+        in_specs=[array],
+        out_specs=array,
+        compiler_params=pltpu.CompilerParams(vmem_limit_bytes=8 * 1024 * 1024),
+        name="expand",
+    )(packed)
 
 
 def panel_products(mine, other, level, n_y):
     array = pl.BlockSpec(memory_space=pltpu.VMEM)
     return pl.pallas_call(
         functools.partial(panel_kernel, n_y),
-        out_shape=jax.ShapeDtypeStruct((n_y, HEAD + P_SIZE, P_SIZE), jnp.float32),
+        out_shape=jax.ShapeDtypeStruct((n_y, HEAD + P_SIZE // 2 + BLOCK, P_SIZE), jnp.float32),
         in_specs=[array, array, array],
         out_specs=array,
         cost_estimate=pl.CostEstimate(
@@ -412,7 +474,17 @@
     row = lax.broadcasted_iota(jnp.int32, (n, n), 0)
     column = lax.broadcasted_iota(jnp.int32, (n, n), 1)
     prior = jnp.broadcast_to(prior_ref[...], (n, n))
-    work_ref[...] = panel_ref[...] + jnp.where(row == column, prior, 0.0)
+    half = n // 2
+    packed, spare = panel_ref[:half, :], panel_ref[half : half + 1, :]
+    diagonal = column[:half] - half == row[:half]
+    whole = jnp.concatenate(
+        [pltpu.roll(packed, half, 1), jnp.where(diagonal, spare, packed)], axis=0
+    )
+    known = ((row < half) & (column < half) & (row >= column)) | (
+        (row >= half) & ((column < half) | (row <= column))
+    )
+    whole = jnp.where(known, whole, whole.T)
+    work_ref[...] = whole + jnp.where(row == column, prior, 0.0)
     for p in range(n // depth):
         base = p * depth
         rows = [
@@ -432,7 +504,7 @@
 
 
 def factor_panel(panel, prior):
-    n = panel.shape[0]
+    n = panel.shape[1]
     return pl.pallas_call(
         factor_kernel,
         out_shape=jax.ShapeDtypeStruct((n, n), jnp.float32),
@@ -488,8 +560,8 @@
         n_y,
     )
     other = swap(send, dk=1)
-    mine, own = own_products(own, send, gain, local_rows, n_y, n_z)
-    keep_y, send_y, keep_x, send_x, level = products(other, own, n_y, n_z)
+    mine, square, side = own_products(own, send, gain, local_rows, n_y, n_z)
+    keep_y, send_y, keep_x, send_x, level = products(other, square, side, n_y, n_z)
     half = OB // PAIR
     grown = float(n_y.bit_length() - 1)
 
@@ -498,12 +570,15 @@
     panels = panel_products(mine, other, level, n_y).astype(jnp.float16)
     panel_z = [panels] + [swap(panels, dz=j) for j in range(1, n_z)]
 
-    left = functools.reduce(jnp.add, [values_of(message) for message in from_y], keep_y)
+    from_y, from_x = lax.optimization_barrier((from_y, from_x))
+    packed = functools.reduce(jnp.add, [values_of(message) for message in from_y], keep_y)
     left_level = functools.reduce(
-        jnp.maximum, [level_of(message) for message in from_y], level[:1]
+        jnp.maximum, [level_of(message) for message in from_y], level[:1, :LANES]
     ) + grown
-    right = keep_x + values_of(from_x).reshape(n_y, half, HALF)
-    right_level = jnp.maximum(level[:1], level_of(from_x)) + 1.0
+    left_level = jnp.concatenate([left_level] * (OB // LANES), axis=1)
+    left = expand(packed, n_z)
+    right = keep_x + values_of(from_x).reshape(n_y, half, KB)
+    right_level = jnp.maximum(level[:1, :KB], level_of(from_x)) + 1.0
 
     over_x = message_of(left[half:], left_level)
     over_y = [message_of(right[j], right_level) for j in range(1, n_y)]

time: 53.6 us -> 52.3 us (0.976)
  waiting for transfers between devices: 6.23 us -> 4.05 us
  starting transfers between devices: 19.4 us -> 20.6 us
    ppermute x14, waiting for transfers between devices: 6.23 us -> 4.05 us  [swap(): return lax.ppermute(values, AXES, pairs)]
    ppermute x14, starting transfers between devices: 19.4 us -> 20.6 us  [swap(): return lax.ppermute(values, AXES, pairs)]
  transfers between devices with their start and end apart: 14 -> 14, of which waited for: 5 -> 4; matrix products, arithmetic and copies ran while one was open for 2% -> 2% of each run, Pallas kernels for 16% -> 17%
where the time goes in v5:
time: 52.3 us; the launch traced here: 52.1 us
  Pallas kernels  22.4 us (43%)
  starting transfers between devices  20.6 us (39%)
  waiting for transfers between devices  4.05 us (8%)
  other arithmetic  1.81 us (3%)
  local copies, waits for them, and re-layouts  1.67 us (3%)
  between operations  1.6 us (3%)
    ppermute x14, starting transfers between devices, swap(): return lax.ppermute(values, AXES, pairs)  20.6 us
    pallas_call x1, Pallas kernels, reduce_rows(): pl.pallas_call(functools.partial(local_kernel, n_y), out_shape=tuple((jax...  9.62 us
    pallas_call x1, Pallas kernels, factor_panel(): pl.pallas_call(factor_kernel, out_shape=jax.ShapeDtypeStruct((n, n), jnp....  5.25 us
    ppermute x14, waiting for transfers between devices, swap(): return lax.ppermute(values, AXES, pairs)  4.05 us
    pallas_call x1, Pallas kernels, own_products(): pl.pallas_call(functools.partial(own_product_kernel, n_y, n_z), out_shape...  2.56 us
    pallas_call x1, Pallas kernels, begin_normal(): pl.pallas_call(normal_kernel, out_shape=(jax.ShapeDtypeStruct((n, m), jnp...  2.21 us
    unnamed x12, local copies, waits for them, and re-layouts  1.64 us
    pallas_call x1, Pallas kernels, products(): pl.pallas_call(functools.partial(product_kernel, n_y, n_z), out_shape=tup...  1.61 us
  transfers between devices with their start and end apart: 14, of which 4 were waited for; matrix products, arithmetic and copies ran while one was open for 2% of the time, Pallas kernels for 17%

profile of v5, /device:TPU:0, one launch (start us, length us, event | category | flops | bytes accessed | tf_op | source)
XLA Modules:
  0.0 52.1 jit_solution(3941498770701507262)
XLA Ops:
  1.3 0.9 %copy-done.4 = bf16[1,256,512]{2,1,0:T(8,128)(2,1)S(1)} copy-done((bf16[1,256,512]{2,1,0:T(8,128)(2,1)S(1)}, bf16[1,256,512]{2,1,0:T(8,128)(2,1)}, u32[]{:S(2)}) %copy-start.4) | copy-done | bytes 262168
  2.2 0.7 %copy-done.5 = f32[1,256]{1,0:T(1,128)S(1)} copy-done((f32[1,256]{1,0:T(1,128)S(1)}, f32[1,256]{1,0:T(1,128)}, u32[]{:S(2)}) %copy-start.5) | copy-done | bytes 1048
  2.9 2.2 %begin_normal.1 = (bf16[256,512]{1,0:T(8,128)(2,1)S(1)}, f32[256,256]{1,0:T(8,128)S(1)}) custom-call(s32[1]{0:T(128)S(6)} %copy.9.count_ref, f32[1,256]{1,0:T(1,128)S(1)} %copy-done.5, bf16[256,512]{1,0:T(8,128)(2,1)S(1)} %bitcast.82), custom_call_target="tpu_custom_call" | custom-call | flops 4000000000 | tf_op jit(solution)/shard_map/begin_normal/pallas_call | solution.py:211
  5.2 9.6 %reduce_rows.1 = (bf16[1280,512]{1,0:T(8,128)(2,1)S(1)}, bf16[1024,512]{1,0:T(8,128)(2,1)S(1)}, bf16[2,256,512]{2,1,0:T(8,128)(2,1)S(1)}) custom-call(s32[1]{0:T(128)S(6)} %copy.9.count_ref, s32[1,4]{1,0:T(1,128)S(1)} %copy-done.3, s32[4,4,128]{2,1,0:T(4,128)S(1)} %bitcast.81, bf16[256,512]{1,0:T(8,128)(2,1)S(1)} %get-tuple-element.33.rows_ref, ...), custom_call_target="tpu_custom_call" | custom-call | tf_op jit(solution)/shard_map/reduce_rows/pallas_call | solution.py:230
  14.8 0.5 collective-permute-start
  15.3 2.6 %own_products.1 = (bf16[1024,512]{1,0:T(8,128)(2,1)S(1)}, f32[2,512,512]{2,1,0:T(8,128)S(1)}, f32[2,512,256]{2,1,0:T(8,128)S(1)}) custom-call(bf16[1024,512]{1,0:T(8,128)(2,1)S(1)} %get-tuple-element.36.own_ref, bf16[1280,512]{1,0:T(8,128)(2,1)S(1)} %get-tuple-element.35.send_ref, bf16[2,256,512]{2,1,0:T(8,128)(2,1)S(1)} %get-tuple-element.37.gain_ref, ...), custom_call_target="tpu_custom_call" | custom-call | flops 1610612736 | tf_op jit(solution)/shard_map/own_products/pallas_call | solution.py:362
  18.0 1.6 %products.1 = (f32[1280,128]{1,0:T(8,128)S(1)}, f32[1,1288,128]{2,1,0:T(8,128)S(1)}, f32[2,256,256]{2,1,0:T(8,128)S(1)}, f32[520,256]{1,0:T(8,128)S(1)}, f32[8,512]{1,0:T(8,128)S(1)}) custom-call(bf16[1280,512]{1,0:T(8,128)(2,1)S(1)} %collective-permute-done.other_ref, f32[2,512,512]{2,1,0:T(8,128)S(1)} %get-tuple-element.38.square_ref, ...), custom_call_target="tpu_custom_call" | custom-call | tf_op jit(solution)/shard_map/products/pallas_call | solution.py:391
  19.6 3.0 %collective-permute-start.1 = (f16[1288,128]{1,0:T(8,128)(2,1)S(1)}, f16[1288,128]{1,0:T(8,128)(2,1)S(1)}, u32[]{:S(2)}, u32[]{:S(2)}) collective-permute-start(f16[1288,128]{1,0:T(8,128)(2,1)S(1)} %convert_bitcast_fusion), channel_id=1, source_target_pairs={{0,2},{1,3},{2,0},{3,1},{4,6},{5,7},{6,4},{7,5},{8,10},{9,11},{10,... | collective-permute-start | bytes 989192 | tf_op jit(solution)/shard_map/ppermute | solution.py:550
  22.6 1.6 %collective-permute-start.2 = (f16[520,256]{1,0:T(8,128)(2,1)S(1)}, f16[520,256]{1,0:T(8,128)(2,1)S(1)}, u32[]{:S(2)}, u32[]{:S(2)}) collective-permute-start(f16[520,256]{1,0:T(8,128)(2,1)S(1)} %convert_element_type.239), channel_id=1, source_target_pairs={{0,4},{1,5},{2,6},{3,7},{4,0},{5,1},{6,2},{7,3},{8,12},{9,13},{10,... | collective-permute-start | bytes 798728 | tf_op jit(solution)/shard_map/ppermute | solution.py:550
  24.2 1.0 %panel_products.1 = f32[2,80,128]{2,1,0:T(8,128)S(1)} custom-call(bf16[1024,512]{1,0:T(8,128)(2,1)S(1)} %get-tuple-element.51.mine_ref, bf16[1280,512]{1,0:T(8,128)(2,1)S(1)} %collective-permute-done.other_ref, f32[8,512]{1,0:T(8,128)S(1)} %get-tuple-element.44.level_ref), custom_call_target="tpu_custom_call" | custom-call | flops 268435456 | tf_op jit(solution)/shard_map/panel_products/pallas_call | solution.py:420
  25.2 3.6 %collective-permute-start.10 = (f16[2,80,128]{2,1,0:T(8,128)(2,1)S(1)}, f16[2,80,128]{2,1,0:T(8,128)(2,1)S(1)}, u32[]{:S(2)}, u32[]{:S(2)}) collective-permute-start(f16[2,80,128]{2,1,0:T(8,128)(2,1)S(1)} %convert_element_type.248), channel_id=1, source_target_pairs={{0,24},{1,25},{2,26},{3,27},{4,28},{5,29},{6,30},{7,31},{8,16},{9,... | collective-permute-start | bytes 122888 | tf_op jit(solution)/shard_map/ppermute | solution.py:550
  28.8 0.8 %collective-permute-start.9 = (f16[2,80,128]{2,1,0:T(8,128)(2,1)S(1)}, f16[2,80,128]{2,1,0:T(8,128)(2,1)S(1)}, u32[]{:S(2)}, u32[]{:S(2)}) collective-permute-start(f16[2,80,128]{2,1,0:T(8,128)(2,1)S(1)} %convert_element_type.248), channel_id=1, source_target_pairs={{0,16},{1,17},{2,18},{3,19},{4,20},{5,21},{6,22},{7,23},{8,24},{9,... | collective-permute-start | bytes 122888 | tf_op jit(solution)/shard_map/ppermute | solution.py:550
  29.6 1.2 %collective-permute-done.2 = f16[520,256]{1,0:T(8,128)(2,1)S(1)} collective-permute-done((f16[520,256]{1,0:T(8,128)(2,1)S(1)}, f16[520,256]{1,0:T(8,128)(2,1)S(1)}, u32[]{:S(2)}, u32[]{:S(2)}) %collective-permute-start.2) | collective-permute-done | bytes 266272 | tf_op jit(solution)/shard_map/ppermute | solution.py:550
  31.7 1.6 %collective-permute-start.3 = (f16[264,512]{1,0:T(8,128)(2,1)S(1)}, f16[264,512]{1,0:T(8,128)(2,1)S(1)}, u32[]{:S(2)}, u32[]{:S(2)}) collective-permute-start(f16[264,512]{1,0:T(8,128)(2,1)S(1)} %pad_maximum_fusion), channel_id=1, source_target_pairs={{0,4},{1,5},{2,6},{3,7},{4,0},{5,1},{6,2},{7,3},{8,12},{9,13},{10,... | collective-permute-start | bytes 811016 | tf_op jit(solution)/shard_map/ppermute | solution.py:550
  33.2 1.5 %collective-permute-start.4 = (f16[264,256]{1,0:T(8,128)(2,1)S(1)}, f16[264,256]{1,0:T(8,128)(2,1)S(1)}, u32[]{:S(2)}, u32[]{:S(2)}) collective-permute-start(f16[264,256]{1,0:T(8,128)(2,1)S(1)} %pad_maximum_fusion.5), channel_id=1, source_target_pairs={{0,2},{1,3},{2,0},{3,1},{4,6},{5,7},{6,4},{7,5},{8,10},{9,11},{10,... | collective-permute-start | bytes 405512 | tf_op jit(solution)/shard_map/ppermute | solution.py:550
  34.9 0.5 %collective-permute-start.12 = (f16[80,128]{1,0:T(8,128)(2,1)S(1)}, f16[80,128]{1,0:T(8,128)(2,1)S(1)}, u32[]{:S(2)}, u32[]{:S(2)}) collective-permute-start(f16[80,128]{1,0:T(8,128)(2,1)S(1)} %get-tuple-element.94), channel_id=1, source_target_pairs={{0,6},{1,7},{2,4},{3,5},{4,2},{5,3},{6,0},{7,1},{8,14},{9,15},{10,... | collective-permute-start | bytes 61448 | tf_op jit(solution)/shard_map/ppermute | solution.py:550
  35.4 1.5 %collective-permute-start.13 = (f16[80,128]{1,0:T(8,128)(2,1)S(1)}, f16[80,128]{1,0:T(8,128)(2,1)S(1)}, u32[]{:S(2)}, u32[]{:S(2)}) collective-permute-start(f16[80,128]{1,0:T(8,128)(2,1)S(1)} %get-tuple-element.94), channel_id=1, source_target_pairs={{0,2},{1,3},{2,0},{3,1},{4,6},{5,7},{6,4},{7,5},{8,10},{9,11},{10,... | collective-permute-start | bytes 61448 | tf_op jit(solution)/shard_map/ppermute | solution.py:550
  36.9 1.5 %collective-permute-start.11 = (f16[80,128]{1,0:T(8,128)(2,1)S(1)}, f16[80,128]{1,0:T(8,128)(2,1)S(1)}, u32[]{:S(2)}, u32[]{:S(2)}) collective-permute-start(f16[80,128]{1,0:T(8,128)(2,1)S(1)} %get-tuple-element.56), channel_id=1, source_target_pairs={{0,4},{1,5},{2,6},{3,7},{4,0},{5,1},{6,2},{7,3},{8,12},{9,13},{10,... | collective-permute-start | bytes 61448 | tf_op jit(solution)/shard_map/ppermute | solution.py:550
  38.4 1.5 %collective-permute-done.3 = f16[264,512]{1,0:T(8,128)(2,1)S(1)} collective-permute-done((f16[264,512]{1,0:T(8,128)(2,1)S(1)}, f16[264,512]{1,0:T(8,128)(2,1)S(1)}, u32[]{:S(2)}, u32[]{:S(2)}) %collective-permute-start.3) | collective-permute-done | bytes 270368 | tf_op jit(solution)/shard_map/ppermute | solution.py:550
  40.3 1.5 %collective-permute-start.5 = (f16[72,768]{1,0:T(8,128)(2,1)S(1)}, f16[72,768]{1,0:T(8,128)(2,1)S(1)}, u32[]{:S(2)}, u32[]{:S(2)}) collective-permute-start(f16[72,768]{1,0:T(8,128)(2,1)S(1)} %get-tuple-element.93), channel_id=1, source_target_pairs={{0,8},{1,9},{2,10},{3,11},{4,12},{5,13},{6,14},{7,15},{8,0},{9,1},... | collective-permute-start | bytes 331784 | tf_op jit(solution)/shard_map/ppermute | solution.py:550
  41.8 2.6 %collective-permute-start.6 = (f16[72,768]{1,0:T(8,128)(2,1)S(1)}, f16[72,768]{1,0:T(8,128)(2,1)S(1)}, u32[]{:S(2)}, u32[]{:S(2)}) collective-permute-start(f16[72,768]{1,0:T(8,128)(2,1)S(1)} %get-tuple-element.92), channel_id=1, source_target_pairs={{0,16},{1,17},{2,18},{3,19},{4,20},{5,21},{6,22},{7,23},{8,24},{9,... | collective-permute-start | bytes 331784 | tf_op jit(solution)/shard_map/ppermute | solution.py:550
  44.9 5.2 %factor_panel.1 = f32[128,128]{1,0:T(8,128)} custom-call(f32[72,128]{1,0:T(8,128)S(1)} %add_add_fusion.panel_ref, f32[1,128]{1,0:T(1,128)S(1)} %copy-done.2), custom_call_target="tpu_custom_call" | custom-call | flops 2097152 | bytes 196608 | tf_op jit(solution)/shard_map/factor_panel/pallas_call | solution.py:508
  50.1 1.2 %collective-permute-done.6 = f16[72,768]{1,0:T(8,128)(2,1)S(1)} collective-permute-done((f16[72,768]{1,0:T(8,128)(2,1)S(1)}, f16[72,768]{1,0:T(8,128)(2,1)S(1)}, u32[]{:S(2)}, u32[]{:S(2)}) %collective-permute-start.6) | collective-permute-done | bytes 110624 | tf_op jit(solution)/shard_map/ppermute | solution.py:550
  51.4 0.8 %fusion.11 = f32[1,64,768]{2,1,0:T(8,128)} fusion(f32[256,512]{1,0:T(8,128)S(1)} %slice_add_fusion, f32[256,256]{1,0:T(8,128)S(1)} %fusion.1, f32[768]{0:T(1024)S(1)} %exponential_reduce_fusion, f16[72,768]{1,0:T(8,128)(2,1)S(1)} %collective-permute-done.7, f32[768]{0:T(1024)S(1)} %exponential_reduce_fusion.1, f16[72,768]{1,0:T(8,128)(2,1)S(1)} %collective-permute-done.6, ...), kind=kLoop, calls=%fused_computation.25 | loop fusion | flops 491520 | bytes 1287168 | tf_op jit(solution)/shard_map/broadcast_in_dim | solution.py:617
  (62 shorter events, 1.8 us)
Async XLA Ops:
  1.3 1.0 %copy-start.4 = (bf16[1,256,512]{2,1,0:T(8,128)(2,1)S(1)}, bf16[1,256,512]{2,1,0:T(8,128)(2,1)}, u32[]{:S(2)}) copy-start(bf16[1,256,512]{2,1,0:T(8,128)(2,1)} %param.7) | copy-start | bytes 786436
  2.2 0.7 %copy-start.5 = (f32[1,256]{1,0:T(1,128)S(1)}, f32[1,256]{1,0:T(1,128)}, u32[]{:S(2)}) copy-start(f32[1,256]{1,0:T(1,128)} %prior_ref.2) | copy-start | bytes 3076
  2.9 2.2 %copy-start = (bf16[1,2304,512]{2,1,0:T(8,128)(2,1)S(1)}, bf16[1,2304,512]{2,1,0:T(8,128)(2,1)}, u32[]{:S(2)}) copy-start(bf16[1,2304,512]{2,1,0:T(8,128)(2,1)} %param.8) | copy-start | bytes 7077892
  2.9 2.2 %copy-start.1 = (s32[2048]{0:T(1024)S(1)}, s32[2048]{0:T(1024)}, u32[]{:S(2)}) copy-start(s32[2048]{0:T(1024)} %param.12) | copy-start | bytes 24580
  2.9 2.2 %copy-start.3 = (s32[1,4]{1,0:T(1,128)S(1)}, s32[1,4]{1,0:T(1,128)}, u32[]{:S(2)}) copy-start(s32[1,4]{1,0:T(1,128)} %band_ref.1) | copy-start | bytes 52
  14.8 3.2 %collective-permute-start = (bf16[1280,512]{1,0:T(8,128)(2,1)S(1)}, bf16[1280,512]{1,0:T(8,128)(2,1)S(1)}, u32[]{:S(2)}, u32[]{:S(2)}) collective-permute-start(bf16[1280,512]{1,0:T(8,128)(2,1)S(1)} %get-tuple-element.35.send_ref), channel_id=1, source_target_pairs={{0,1},{1,0},{2,3},{3,2},{4,5},{5,4},{6,7},{7,6},{8,9},{9,8},{10,11... | collective-permute-start | bytes 3932168 | tf_op jit(solution)/shard_map/ppermute | solution.py:550
  19.6 11.2 %collective-permute-start.1 = (f16[1288,128]{1,0:T(8,128)(2,1)S(1)}, f16[1288,128]{1,0:T(8,128)(2,1)S(1)}, u32[]{:S(2)}, u32[]{:S(2)}) collective-permute-start(f16[1288,128]{1,0:T(8,128)(2,1)S(1)} %convert_bitcast_fusion), channel_id=1, source_target_pairs={{0,2},{1,3},{2,0},{3,1},{4,6},{5,7},{6,4},{7,5},{8,10},{9,11},{10,... | collective-permute-start | bytes 989192 | tf_op jit(solution)/shard_map/ppermute | solution.py:550
  22.6 8.2 %collective-permute-start.2 = (f16[520,256]{1,0:T(8,128)(2,1)S(1)}, f16[520,256]{1,0:T(8,128)(2,1)S(1)}, u32[]{:S(2)}, u32[]{:S(2)}) collective-permute-start(f16[520,256]{1,0:T(8,128)(2,1)S(1)} %convert_element_type.239), channel_id=1, source_target_pairs={{0,4},{1,5},{2,6},{3,7},{4,0},{5,1},{6,2},{7,3},{8,12},{9,13},{10,... | collective-permute-start | bytes 798728 | tf_op jit(solution)/shard_map/ppermute | solution.py:550
  25.2 9.6 %collective-permute-start.10 = (f16[2,80,128]{2,1,0:T(8,128)(2,1)S(1)}, f16[2,80,128]{2,1,0:T(8,128)(2,1)S(1)}, u32[]{:S(2)}, u32[]{:S(2)}) collective-permute-start(f16[2,80,128]{2,1,0:T(8,128)(2,1)S(1)} %convert_element_type.248), channel_id=1, source_target_pairs={{0,24},{1,25},{2,26},{3,27},{4,28},{5,29},{6,30},{7,31},{8,16},{9,... | collective-permute-start | bytes 122888 | tf_op jit(solution)/shard_map/ppermute | solution.py:550
  28.8 5.9 %collective-permute-start.8 = (f16[2,80,128]{2,1,0:T(8,128)(2,1)S(1)}, f16[2,80,128]{2,1,0:T(8,128)(2,1)S(1)}, u32[]{:S(2)}, u32[]{:S(2)}) collective-permute-start(f16[2,80,128]{2,1,0:T(8,128)(2,1)S(1)} %convert_element_type.248), channel_id=1, source_target_pairs={{0,8},{1,9},{2,10},{3,11},{4,12},{5,13},{6,14},{7,15},{8,0},{9,1},... | collective-permute-start | bytes 122888 | tf_op jit(solution)/shard_map/ppermute | solution.py:550
  28.8 5.9 %collective-permute-start.9 = (f16[2,80,128]{2,1,0:T(8,128)(2,1)S(1)}, f16[2,80,128]{2,1,0:T(8,128)(2,1)S(1)}, u32[]{:S(2)}, u32[]{:S(2)}) collective-permute-start(f16[2,80,128]{2,1,0:T(8,128)(2,1)S(1)} %convert_element_type.248), channel_id=1, source_target_pairs={{0,16},{1,17},{2,18},{3,19},{4,20},{5,21},{6,22},{7,23},{8,24},{9,... | collective-permute-start | bytes 122888 | tf_op jit(solution)/shard_map/ppermute | solution.py:550
  31.6 13.2 %copy-start.2 = (f32[1,128]{1,0:T(1,128)S(1)}, f32[1,128]{1,0:T(1,128)}, u32[]{:S(2)}) copy-start(f32[1,128]{1,0:T(1,128)} %prior_ref.3) | copy-start | bytes 1540
  31.7 8.3 %collective-permute-start.3 = (f16[264,512]{1,0:T(8,128)(2,1)S(1)}, f16[264,512]{1,0:T(8,128)(2,1)S(1)}, u32[]{:S(2)}, u32[]{:S(2)}) collective-permute-start(f16[264,512]{1,0:T(8,128)(2,1)S(1)} %pad_maximum_fusion), channel_id=1, source_target_pairs={{0,4},{1,5},{2,6},{3,7},{4,0},{5,1},{6,2},{7,3},{8,12},{9,13},{10,... | collective-permute-start | bytes 811016 | tf_op jit(solution)/shard_map/ppermute | solution.py:550
  33.2 5.2 %collective-permute-start.4 = (f16[264,256]{1,0:T(8,128)(2,1)S(1)}, f16[264,256]{1,0:T(8,128)(2,1)S(1)}, u32[]{:S(2)}, u32[]{:S(2)}) collective-permute-start(f16[264,256]{1,0:T(8,128)(2,1)S(1)} %pad_maximum_fusion.5), channel_id=1, source_target_pairs={{0,2},{1,3},{2,0},{3,1},{4,6},{5,7},{6,4},{7,5},{8,10},{9,11},{10,... | collective-permute-start | bytes 405512 | tf_op jit(solution)/shard_map/ppermute | solution.py:550
  34.9 9.9 %collective-permute-start.12 = (f16[80,128]{1,0:T(8,128)(2,1)S(1)}, f16[80,128]{1,0:T(8,128)(2,1)S(1)}, u32[]{:S(2)}, u32[]{:S(2)}) collective-permute-start(f16[80,128]{1,0:T(8,128)(2,1)S(1)} %get-tuple-element.94), channel_id=1, source_target_pairs={{0,6},{1,7},{2,4},{3,5},{4,2},{5,3},{6,0},{7,1},{8,14},{9,15},{10,... | collective-permute-start | bytes 61448 | tf_op jit(solution)/shard_map/ppermute | solution.py:550
  35.4 9.4 %collective-permute-start.13 = (f16[80,128]{1,0:T(8,128)(2,1)S(1)}, f16[80,128]{1,0:T(8,128)(2,1)S(1)}, u32[]{:S(2)}, u32[]{:S(2)}) collective-permute-start(f16[80,128]{1,0:T(8,128)(2,1)S(1)} %get-tuple-element.94), channel_id=1, source_target_pairs={{0,2},{1,3},{2,0},{3,1},{4,6},{5,7},{6,4},{7,5},{8,10},{9,11},{10,... | collective-permute-start | bytes 61448 | tf_op jit(solution)/shard_map/ppermute | solution.py:550
  36.9 7.5 %collective-permute-start.11 = (f16[80,128]{1,0:T(8,128)(2,1)S(1)}, f16[80,128]{1,0:T(8,128)(2,1)S(1)}, u32[]{:S(2)}, u32[]{:S(2)}) collective-permute-start(f16[80,128]{1,0:T(8,128)(2,1)S(1)} %get-tuple-element.56), channel_id=1, source_target_pairs={{0,4},{1,5},{2,6},{3,7},{4,0},{5,1},{6,2},{7,3},{8,12},{9,13},{10,... | collective-permute-start | bytes 61448 | tf_op jit(solution)/shard_map/ppermute | solution.py:550
  40.3 9.8 %collective-permute-start.5 = (f16[72,768]{1,0:T(8,128)(2,1)S(1)}, f16[72,768]{1,0:T(8,128)(2,1)S(1)}, u32[]{:S(2)}, u32[]{:S(2)}) collective-permute-start(f16[72,768]{1,0:T(8,128)(2,1)S(1)} %get-tuple-element.93), channel_id=1, source_target_pairs={{0,8},{1,9},{2,10},{3,11},{4,12},{5,13},{6,14},{7,15},{8,0},{9,1},... | collective-permute-start | bytes 331784 | tf_op jit(solution)/shard_map/ppermute | solution.py:550
  41.8 9.5 %collective-permute-start.6 = (f16[72,768]{1,0:T(8,128)(2,1)S(1)}, f16[72,768]{1,0:T(8,128)(2,1)S(1)}, u32[]{:S(2)}, u32[]{:S(2)}) collective-permute-start(f16[72,768]{1,0:T(8,128)(2,1)S(1)} %get-tuple-element.92), channel_id=1, source_target_pairs={{0,16},{1,17},{2,18},{3,19},{4,20},{5,21},{6,22},{7,23},{8,24},{9,... | collective-permute-start | bytes 331784 | tf_op jit(solution)/shard_map/ppermute | solution.py:550
  44.4 6.9 %collective-permute-start.7 = (f16[72,768]{1,0:T(8,128)(2,1)S(1)}, f16[72,768]{1,0:T(8,128)(2,1)S(1)}, u32[]{:S(2)}, u32[]{:S(2)}) collective-permute-start(f16[72,768]{1,0:T(8,128)(2,1)S(1)} %get-tuple-element.91), channel_id=1, source_target_pairs={{0,24},{1,25},{2,26},{3,27},{4,28},{5,29},{6,30},{7,31},{8,16},{9,... | collective-permute-start | bytes 331784 | tf_op jit(solution)/shard_map/ppermute | solution.py:550

commit v6 on v5

--- a/solution.py
+++ b/solution.py
@@ -44,22 +44,23 @@
     return jnp.broadcast_to(value[i : i + 1, :], (BLOCK, LANES))
 
 
-def eliminate_group(rows, base):
+def eliminate_group(rows, base, extra):
     sub = lax.broadcasted_iota(jnp.int32, (BLOCK, LANES), 0)
     lane = lax.broadcasted_iota(jnp.int32, (BLOCK, LANES), 1)
     count = len(rows)
+    rows = rows + extra
     for q in range(count):
         half, at = divmod(base + BLOCK * q, LANES)
         factors = [
             [
-                jnp.broadcast_to(rows[r][half][:, at + j : at + j + 1], (BLOCK, LANES))
+                jnp.broadcast_to(row[half][:, at + j : at + j + 1], (BLOCK, LANES))
                 for j in range(BLOCK)
             ]
-            for r in range(count)
+            for row in rows
         ]
         inside = (lane >= at) & (lane < at + BLOCK)
         unit = (lane - at == sub).astype(jnp.float32)
-        for r in range(count):
+        for r in range(len(rows)):
             rows[r][half] = jnp.where(inside, unit if r == q else 0.0, rows[r][half])
         columns, own = list(factors[q]), rows[q]
         a, b, d = row_of(columns[0], 0), row_of(columns[1], 0), row_of(columns[1], 1)
@@ -81,7 +82,7 @@
                 a, b, d = row_of(one, i + 2), row_of(two, i + 2), row_of(two, i + 3)
             for j, pair in pairs.items():
                 columns[j] = pair[1]
-        for r in range(count):
+        for r in range(len(rows)):
             if r != q:
                 for h in range(len(own)):
                     t = [factors[r][j] * row_of(own[h], j) for j in range(BLOCK)]
@@ -95,22 +96,32 @@
     n = a_ref.shape[0]
     depth = BLOCK * GROUP
     before = a_ref[base : base + depth, :]
-    rows = [
-        [
-            a_ref[base + BLOCK * r : base + BLOCK * (r + 1), LANES * h : LANES * (h + 1)]
-            for h in range(n // LANES)
+
+    def blocks(start):
+        return [
+            [
+                a_ref[start + BLOCK * r : start + BLOCK * (r + 1), LANES * h : LANES * (h + 1)]
+                for h in range(n // LANES)
+            ]
+            for r in range(GROUP)
         ]
-        for r in range(GROUP)
-    ]
-    rows = eliminate_group(rows, base)
-    after = jnp.concatenate([jnp.concatenate(row, axis=1) for row in rows], axis=0)
+
+    def joined(rows):
+        return jnp.concatenate([jnp.concatenate(row, axis=1) for row in rows], axis=0)
+
+    after = base + depth
+    ahead = after < n
+    rows = eliminate_group(blocks(base), base, blocks(after) if ahead else [])
+    following, after_rows = joined(rows[GROUP:]) if ahead else None, joined(rows[:GROUP])
     column = lax.broadcasted_iota(jnp.int32, (depth, n), 1)
     row = lax.broadcasted_iota(jnp.int32, (depth, n), 0)
     inside = (column >= base) & (column < base + depth)
+    if following is not None:
+        a_ref[after : after + depth, :] = jnp.where(inside, -following, following)
     before = jnp.where(inside, jnp.where(column - base == row, -1.0, 0.0), before)
-    after = jnp.where(inside, -after, after)
+    after_rows = jnp.where(inside, -after_rows, after_rows)
     u0, u1, u2 = split3(before)
-    w0, w1, w2 = split3(after)
+    w0, w1, w2 = split3(after_rows)
     left = jnp.concatenate([u0, u0, u0, u1, u1, u2], axis=0).T
     right = jnp.concatenate([w0, w1, w2, w0, w1, w0], axis=0)
 
@@ -122,10 +133,9 @@
         )
         a_ref[low:high, :] = jnp.where(outside, a_ref[low:high, :], 0.0) - mm(left[low:high], right)
 
-    after = base + depth
-    for low, high in ((after, after + depth), (0, after), (after + depth, n)):
-        if low < min(high, n):
-            update(low, min(high, n))
+    for low, high in ((after + depth, n), (0, after)):
+        if low < high:
+            update(low, high)
 
 
 def place_of():
@@ -138,15 +148,19 @@
     return (tile.astype(jnp.float32) - mm(solved, local_rows)).astype(jnp.bfloat16)
 
 
-def normal_kernel(count_ref, prior_ref, local_ref, rows_ref, work_ref):
+def normal_kernel(count_ref, local_ref, rows_ref, normal_ref):
     n, m = local_ref.shape
     used = lax.broadcasted_iota(jnp.int32, (n, m), 1) < count_ref[0]
     rows_ref[...] = jnp.where(used, local_ref[...].astype(jnp.float32), 0.0).astype(jnp.bfloat16)
-    local_rows = rows_ref[...]
+    normal_ref[...] = mm(rows_ref[...], rows_ref[...], INNER)
+
+
+def sweep_kernel(prior_ref, normal_ref, work_ref):
+    n = normal_ref.shape[0]
     row = lax.broadcasted_iota(jnp.int32, (n, n), 0)
     column = lax.broadcasted_iota(jnp.int32, (n, n), 1)
     prior = jnp.broadcast_to(prior_ref[...], (n, n))
-    work_ref[...] = mm(local_rows, local_rows, INNER) + jnp.where(row == column, prior, 0.0)
+    work_ref[...] = normal_ref[...] + jnp.where(row == column, prior, 0.0)
     for p in range(FIRST):
         sweep_group(work_ref, p * BLOCK * GROUP)
 
@@ -188,10 +202,10 @@
             send_ref[t * TILE - mine : (t + 1) * TILE - mine, :] = got
 
     steps = n // (BLOCK * GROUP) - FIRST
-    tiles = owned // TILE
+    tiles, fill = owned // TILE, steps - 2
     for p in range(steps):
         sweep_group(work_ref, (FIRST + p) * BLOCK * GROUP)
-        for t in range(p * tiles // steps, (p + 1) * tiles // steps):
+        for t in range(p * tiles // fill, min(tiles, (p + 1) * tiles // fill)):
             gather_rows(t)
     used = lax.broadcasted_iota(jnp.int32, (KB, m), 1) < count
     border = global_ref[owned:, :].astype(jnp.float32)
@@ -208,18 +222,28 @@
 def begin_normal(count, prior, local_rows):
     n, m = local_rows.shape
     array = pl.BlockSpec(memory_space=pltpu.VMEM)
-    return pl.pallas_call(
+    rows, normal = pl.pallas_call(
         normal_kernel,
         out_shape=(
             jax.ShapeDtypeStruct((n, m), jnp.bfloat16),
             jax.ShapeDtypeStruct((n, n), jnp.float32),
         ),
-        in_specs=[pl.BlockSpec(memory_space=pltpu.SMEM), array, array],
+        in_specs=[pl.BlockSpec(memory_space=pltpu.SMEM), array],
         out_specs=(array, array),
         compiler_params=pltpu.CompilerParams(vmem_limit_bytes=16 * 1024 * 1024),
+        cost_estimate=pl.CostEstimate(flops=10**9, bytes_accessed=0, transcendentals=0),
+        name="normal",
+    )(count, local_rows)
+    begun = pl.pallas_call(
+        sweep_kernel,
+        out_shape=jax.ShapeDtypeStruct((n, n), jnp.float32),
+        in_specs=[array, array],
+        out_specs=array,
+        compiler_params=pltpu.CompilerParams(vmem_limit_bytes=16 * 1024 * 1024),
         cost_estimate=pl.CostEstimate(flops=4 * 10**9, bytes_accessed=0, transcendentals=0),
-        name="begin_normal",
-    )(count, prior, local_rows)
+        name="first_sweeps",
+    )(prior, normal)
+    return rows, begun
 
 
 def reduce_rows(count, band, owners, rows, begun, global_rows, n_y):
@@ -605,12 +629,14 @@
     total = jnp.concatenate([left, right], axis=1)
     level = jnp.concatenate([left_level, right_level], axis=1)
     over_z = [message_of(total[j * rows : (j + 1) * rows], level) for j in range(1, n_z)]
+    over_z = lax.optimization_barrier(over_z)
     from_z = [swap(over_z[j - 1], dz=j) for j in range(1, n_z)]
+    *from_z, from_near = from_z[1:] + from_z[:1]
     panel_x, panel_y, _ = lax.optimization_barrier((panel_x, panel_y, over_z))
     panel = functools.reduce(jnp.add, [values_of(message) for message in panel_y])
     panel = panel + functools.reduce(jnp.add, [values_of(message) for message in panel_x])
     panel_factor = factor_panel(panel, kaula_prior)
-    from_z, panel_factor = lax.optimization_barrier((from_z, panel_factor))
+    from_z, panel_factor = lax.optimization_barrier((from_z + [from_near], panel_factor))
     normal_rows = functools.reduce(
         jnp.add, [values_of(message) for message in from_z], total[:rows]
     )

time: 52.3 us -> 50.9 us (0.973)
  local copies, waits for them, and re-layouts: 1.67 us -> 1 us
  Pallas kernels: 22.4 us -> 21.8 us
    pallas_call x1, Pallas kernels: 2.21 us -> 0.27 us  [begin_normal(): pl.pallas_call(normal_kernel, out_shape=(jax.ShapeDtypeStruct((n, m), jnp...]
    pallas_call x0 -> x1, Pallas kernels: none -> 1.86 us  [begin_normal(): pl.pallas_call(sweep_kernel, out_shape=jax.ShapeDtypeStruct((n, n), jnp.f...]
    unnamed x12, local copies, waits for them, and re-layouts: 1.64 us -> 0.97 us
  transfers between devices with their start and end apart: 14 -> 14, of which waited for: 4 -> 5; matrix products, arithmetic and copies ran while one was open for 2% -> 2% of each run, Pallas kernels for 17% -> 18%
where the time goes in v6:
time: 50.9 us; the launch traced here: 50.7 us
  Pallas kernels  21.8 us (43%)
  starting transfers between devices  20.2 us (40%)
  waiting for transfers between devices  4.1 us (8%)
  other arithmetic  1.99 us (4%)
  between operations  1.65 us (3%)
  local copies, waits for them, and re-layouts  1 us (2%)
    ppermute x14, starting transfers between devices, swap(): return lax.ppermute(values, AXES, pairs)  20.2 us
    pallas_call x1, Pallas kernels, reduce_rows(): pl.pallas_call(functools.partial(local_kernel, n_y), out_shape=tuple((jax...  9.2 us
    pallas_call x1, Pallas kernels, factor_panel(): pl.pallas_call(factor_kernel, out_shape=jax.ShapeDtypeStruct((n, n), jnp....  5.25 us
    ppermute x14, waiting for transfers between devices, swap(): return lax.ppermute(values, AXES, pairs)  4.1 us
    pallas_call x1, Pallas kernels, own_products(): pl.pallas_call(functools.partial(own_product_kernel, n_y, n_z), out_shape...  2.56 us
    pallas_call x1, Pallas kernels, begin_normal(): pl.pallas_call(sweep_kernel, out_shape=jax.ShapeDtypeStruct((n, n), jnp.f...  1.86 us
    pallas_call x1, Pallas kernels, products(): pl.pallas_call(functools.partial(product_kernel, n_y, n_z), out_shape=tup...  1.42 us
  transfers between devices with their start and end apart: 14, of which 5 were waited for; matrix products, arithmetic and copies ran while one was open for 2% of the time, Pallas kernels for 18%

profile of v6, /device:TPU:0, one launch (start us, length us, event | category | flops | bytes accessed | tf_op | source)
XLA Modules:
  0.0 50.7 jit_solution(5663778097955013224)
XLA Ops:
  1.3 0.9 %copy-done.4 = bf16[1,256,512]{2,1,0:T(8,128)(2,1)S(1)} copy-done((bf16[1,256,512]{2,1,0:T(8,128)(2,1)S(1)}, bf16[1,256,512]{2,1,0:T(8,128)(2,1)}, u32[]{:S(2)}) %copy-start.4) | copy-done | bytes 262168
  2.6 1.9 %first_sweeps.1.begun_ref = f32[256,256]{1,0:T(8,128)S(1)} custom-call(f32[1,256]{1,0:T(1,128)S(1)} %copy-done.5, f32[256,256]{1,0:T(8,128)S(1)} %get-tuple-element.37.normal_ref), custom_call_target="tpu_custom_call" | custom-call | flops 4000000000 | tf_op jit(solution)/shard_map/first_sweeps/pallas_call | solution.py:237
  4.5 9.2 %reduce_rows.1 = (bf16[1280,512]{1,0:T(8,128)(2,1)S(1)}, bf16[1024,512]{1,0:T(8,128)(2,1)S(1)}, bf16[2,256,512]{2,1,0:T(8,128)(2,1)S(1)}) custom-call(s32[1]{0:T(128)S(6)} %copy.9.count_ref, s32[1,4]{1,0:T(1,128)S(1)} %copy-done.3, s32[4,4,128]{2,1,0:T(4,128)S(1)} %bitcast.81, bf16[256,512]{1,0:T(8,128)(2,1)S(1)} %get-tuple-element.36.rows_ref, ...), custom_call_target="tpu_custom_call" | custom-call | tf_op jit(solution)/shard_map/reduce_rows/pallas_call | solution.py:254
  13.7 0.5 %collective-permute-start = (bf16[1280,512]{1,0:T(8,128)(2,1)S(1)}, bf16[1280,512]{1,0:T(8,128)(2,1)S(1)}, u32[]{:S(2)}, u32[]{:S(2)}) collective-permute-start(bf16[1280,512]{1,0:T(8,128)(2,1)S(1)} %get-tuple-element.38.send_ref), channel_id=1, source_target_pairs={{0,1},{1,0},{2,3},{3,2},{4,5},{5,4},{6,7},{7,6},{8,9},{9,8},{10,11... | collective-permute-start | bytes 3932168 | tf_op jit(solution)/shard_map/ppermute | solution.py:574
  14.2 2.6 %own_products.1 = (bf16[1024,512]{1,0:T(8,128)(2,1)S(1)}, f32[2,512,512]{2,1,0:T(8,128)S(1)}, f32[2,512,256]{2,1,0:T(8,128)S(1)}) custom-call(bf16[1024,512]{1,0:T(8,128)(2,1)S(1)} %get-tuple-element.39.own_ref, bf16[1280,512]{1,0:T(8,128)(2,1)S(1)} %get-tuple-element.38.send_ref, bf16[2,256,512]{2,1,0:T(8,128)(2,1)S(1)} %get-tuple-element.40.gain_ref, ...), custom_call_target="tpu_custom_call" | custom-call | flops 1610612736 | tf_op jit(solution)/shard_map/own_products/pallas_call | solution.py:386
  16.9 1.4 %products.1 = (f32[1280,128]{1,0:T(8,128)S(1)}, f32[1,1288,128]{2,1,0:T(8,128)S(1)}, f32[2,256,256]{2,1,0:T(8,128)S(1)}, f32[520,256]{1,0:T(8,128)S(1)}, f32[8,512]{1,0:T(8,128)S(1)}) custom-call(bf16[1280,512]{1,0:T(8,128)(2,1)S(1)} %collective-permute-done.other_ref, f32[2,512,512]{2,1,0:T(8,128)S(1)} %get-tuple-element.41.square_ref, ...), custom_call_target="tpu_custom_call" | custom-call | tf_op jit(solution)/shard_map/products/pallas_call | solution.py:415
  18.5 2.9 %collective-permute-start.1 = (f16[1288,128]{1,0:T(8,128)(2,1)S(1)}, f16[1288,128]{1,0:T(8,128)(2,1)S(1)}, u32[]{:S(2)}, u32[]{:S(2)}) collective-permute-start(f16[1288,128]{1,0:T(8,128)(2,1)S(1)} %convert_bitcast_fusion), channel_id=1, source_target_pairs={{0,2},{1,3},{2,0},{3,1},{4,6},{5,7},{6,4},{7,5},{8,10},{9,11},{10,... | collective-permute-start | bytes 989192 | tf_op jit(solution)/shard_map/ppermute | solution.py:574
  21.5 1.6 %collective-permute-start.2 = (f16[520,256]{1,0:T(8,128)(2,1)S(1)}, f16[520,256]{1,0:T(8,128)(2,1)S(1)}, u32[]{:S(2)}, u32[]{:S(2)}) collective-permute-start(f16[520,256]{1,0:T(8,128)(2,1)S(1)} %convert_element_type.239), channel_id=1, source_target_pairs={{0,4},{1,5},{2,6},{3,7},{4,0},{5,1},{6,2},{7,3},{8,12},{9,13},{10,... | collective-permute-start | bytes 798728 | tf_op jit(solution)/shard_map/ppermute | solution.py:574
  23.1 1.0 %panel_products.1 = f32[2,80,128]{2,1,0:T(8,128)S(1)} custom-call(bf16[1024,512]{1,0:T(8,128)(2,1)S(1)} %get-tuple-element.57.mine_ref, bf16[1280,512]{1,0:T(8,128)(2,1)S(1)} %collective-permute-done.other_ref, f32[8,512]{1,0:T(8,128)S(1)} %get-tuple-element.47.level_ref), custom_call_target="tpu_custom_call" | custom-call | flops 268435456 | tf_op jit(solution)/shard_map/panel_products/pallas_call | solution.py:444
  24.1 3.7 %collective-permute-start.10 = (f16[2,80,128]{2,1,0:T(8,128)(2,1)S(1)}, f16[2,80,128]{2,1,0:T(8,128)(2,1)S(1)}, u32[]{:S(2)}, u32[]{:S(2)}) collective-permute-start(f16[2,80,128]{2,1,0:T(8,128)(2,1)S(1)} %convert_element_type.248), channel_id=1, source_target_pairs={{0,24},{1,25},{2,26},{3,27},{4,28},{5,29},{6,30},{7,31},{8,16},{9,... | collective-permute-start | bytes 122888 | tf_op jit(solution)/shard_map/ppermute | solution.py:574
  27.7 0.8 %collective-permute-start.9 = (f16[2,80,128]{2,1,0:T(8,128)(2,1)S(1)}, f16[2,80,128]{2,1,0:T(8,128)(2,1)S(1)}, u32[]{:S(2)}, u32[]{:S(2)}) collective-permute-start(f16[2,80,128]{2,1,0:T(8,128)(2,1)S(1)} %convert_element_type.248), channel_id=1, source_target_pairs={{0,16},{1,17},{2,18},{3,19},{4,20},{5,21},{6,22},{7,23},{8,24},{9,... | collective-permute-start | bytes 122888 | tf_op jit(solution)/shard_map/ppermute | solution.py:574
  28.5 1.2 %collective-permute-done.2 = f16[520,256]{1,0:T(8,128)(2,1)S(1)} collective-permute-done((f16[520,256]{1,0:T(8,128)(2,1)S(1)}, f16[520,256]{1,0:T(8,128)(2,1)S(1)}, u32[]{:S(2)}, u32[]{:S(2)}) %collective-permute-start.2) | collective-permute-done | bytes 266272 | tf_op jit(solution)/shard_map/ppermute | solution.py:574
  30.5 1.6 %collective-permute-start.3 = (f16[264,512]{1,0:T(8,128)(2,1)S(1)}, f16[264,512]{1,0:T(8,128)(2,1)S(1)}, u32[]{:S(2)}, u32[]{:S(2)}) collective-permute-start(f16[264,512]{1,0:T(8,128)(2,1)S(1)} %pad_maximum_fusion), channel_id=1, source_target_pairs={{0,4},{1,5},{2,6},{3,7},{4,0},{5,1},{6,2},{7,3},{8,12},{9,13},{10,... | collective-permute-start | bytes 811016 | tf_op jit(solution)/shard_map/ppermute | solution.py:574
  32.1 1.5 %collective-permute-start.4 = (f16[264,256]{1,0:T(8,128)(2,1)S(1)}, f16[264,256]{1,0:T(8,128)(2,1)S(1)}, u32[]{:S(2)}, u32[]{:S(2)}) collective-permute-start(f16[264,256]{1,0:T(8,128)(2,1)S(1)} %pad_maximum_fusion.5), channel_id=1, source_target_pairs={{0,2},{1,3},{2,0},{3,1},{4,6},{5,7},{6,4},{7,5},{8,10},{9,11},{10,... | collective-permute-start | bytes 405512 | tf_op jit(solution)/shard_map/ppermute | solution.py:574
  33.7 0.5 %collective-permute-start.12 = (f16[80,128]{1,0:T(8,128)(2,1)S(1)}, f16[80,128]{1,0:T(8,128)(2,1)S(1)}, u32[]{:S(2)}, u32[]{:S(2)}) collective-permute-start(f16[80,128]{1,0:T(8,128)(2,1)S(1)} %get-tuple-element.100), channel_id=1, source_target_pairs={{0,6},{1,7},{2,4},{3,5},{4,2},{5,3},{6,0},{7,1},{8,14},{9,15},{10,... | collective-permute-start | bytes 61448 | tf_op jit(solution)/shard_map/ppermute | solution.py:574
  34.3 1.5 %collective-permute-start.13 = (f16[80,128]{1,0:T(8,128)(2,1)S(1)}, f16[80,128]{1,0:T(8,128)(2,1)S(1)}, u32[]{:S(2)}, u32[]{:S(2)}) collective-permute-start(f16[80,128]{1,0:T(8,128)(2,1)S(1)} %get-tuple-element.100), channel_id=1, source_target_pairs={{0,2},{1,3},{2,0},{3,1},{4,6},{5,7},{6,4},{7,5},{8,10},{9,11},{10,... | collective-permute-start | bytes 61448 | tf_op jit(solution)/shard_map/ppermute | solution.py:574
  35.8 1.5 %collective-permute-start.11 = (f16[80,128]{1,0:T(8,128)(2,1)S(1)}, f16[80,128]{1,0:T(8,128)(2,1)S(1)}, u32[]{:S(2)}, u32[]{:S(2)}) collective-permute-start(f16[80,128]{1,0:T(8,128)(2,1)S(1)} %get-tuple-element.62), channel_id=1, source_target_pairs={{0,4},{1,5},{2,6},{3,7},{4,0},{5,1},{6,2},{7,3},{8,12},{9,13},{10,... | collective-permute-start | bytes 61448 | tf_op jit(solution)/shard_map/ppermute | solution.py:574
  37.3 1.5 %collective-permute-done.3 = f16[264,512]{1,0:T(8,128)(2,1)S(1)} collective-permute-done((f16[264,512]{1,0:T(8,128)(2,1)S(1)}, f16[264,512]{1,0:T(8,128)(2,1)S(1)}, u32[]{:S(2)}, u32[]{:S(2)}) %collective-permute-start.3) | collective-permute-done | bytes 270368 | tf_op jit(solution)/shard_map/ppermute | solution.py:574
  39.2 2.6 %collective-permute-start.5 = (f16[72,768]{1,0:T(8,128)(2,1)S(1)}, f16[72,768]{1,0:T(8,128)(2,1)S(1)}, u32[]{:S(2)}, u32[]{:S(2)}) collective-permute-start(f16[72,768]{1,0:T(8,128)(2,1)S(1)} %get-tuple-element.54), channel_id=1, source_target_pairs={{0,16},{1,17},{2,18},{3,19},{4,20},{5,21},{6,22},{7,23},{8,24},{9,... | collective-permute-start | bytes 331784 | tf_op jit(solution)/shard_map/ppermute | solution.py:574
  41.8 1.3 %collective-permute-start.6 = (f16[72,768]{1,0:T(8,128)(2,1)S(1)}, f16[72,768]{1,0:T(8,128)(2,1)S(1)}, u32[]{:S(2)}, u32[]{:S(2)}) collective-permute-start(f16[72,768]{1,0:T(8,128)(2,1)S(1)} %get-tuple-element.55), channel_id=1, source_target_pairs={{0,24},{1,25},{2,26},{3,27},{4,28},{5,29},{6,30},{7,31},{8,16},{9,... | collective-permute-start | bytes 331784 | tf_op jit(solution)/shard_map/ppermute | solution.py:574
  43.4 5.2 %factor_panel.1 = f32[128,128]{1,0:T(8,128)} custom-call(f32[72,128]{1,0:T(8,128)S(1)} %add_add_fusion.panel_ref, f32[1,128]{1,0:T(1,128)S(1)} %copy-done.2), custom_call_target="tpu_custom_call" | custom-call | flops 2097152 | bytes 196608 | tf_op jit(solution)/shard_map/factor_panel/pallas_call | solution.py:532
  48.6 0.5 %collective-permute-done.5 = f16[72,768]{1,0:T(8,128)(2,1)S(1)} collective-permute-done((f16[72,768]{1,0:T(8,128)(2,1)S(1)}, f16[72,768]{1,0:T(8,128)(2,1)S(1)}, u32[]{:S(2)}, u32[]{:S(2)}) %collective-permute-start.5) | collective-permute-done | bytes 110624 | tf_op jit(solution)/shard_map/ppermute | solution.py:574
  49.2 0.7 %collective-permute-done.7 = f16[72,768]{1,0:T(8,128)(2,1)S(1)} collective-permute-done((f16[72,768]{1,0:T(8,128)(2,1)S(1)}, f16[72,768]{1,0:T(8,128)(2,1)S(1)}, u32[]{:S(2)}, u32[]{:S(2)}) %collective-permute-start.7) | collective-permute-done | bytes 110624 | tf_op jit(solution)/shard_map/ppermute | solution.py:574
  50.0 0.8 %fusion.11 = f32[1,64,768]{2,1,0:T(8,128)} fusion(f32[256,512]{1,0:T(8,128)S(1)} %slice_add_fusion, f32[256,256]{1,0:T(8,128)S(1)} %fusion.1, f32[768]{0:T(1024)S(1)} %exponential_reduce_fusion, f16[72,768]{1,0:T(8,128)(2,1)S(1)} %collective-permute-done.7, f32[768]{0:T(1024)S(1)} %exponential_reduce_fusion.1, f16[72,768]{1,0:T(8,128)(2,1)S(1)} %collective-permute-done.6, ...), kind=kLoop, calls=%fused_computation.25 | loop fusion | flops 491520 | bytes 1287168 | tf_op jit(solution)/shard_map/broadcast_in_dim | solution.py:643
  (63 shorter events, 2.1 us)
Async XLA Ops:
  0.6 1.9 %copy-start.5 = (f32[1,256]{1,0:T(1,128)S(1)}, f32[1,256]{1,0:T(1,128)}, u32[]{:S(2)}) copy-start(f32[1,256]{1,0:T(1,128)} %prior_ref.2) | copy-start | bytes 3076
  1.3 1.0 %copy-start.4 = (bf16[1,256,512]{2,1,0:T(8,128)(2,1)S(1)}, bf16[1,256,512]{2,1,0:T(8,128)(2,1)}, u32[]{:S(2)}) copy-start(bf16[1,256,512]{2,1,0:T(8,128)(2,1)} %param.7) | copy-start | bytes 786436
  2.5 1.9 %copy-start = (bf16[1,2304,512]{2,1,0:T(8,128)(2,1)S(1)}, bf16[1,2304,512]{2,1,0:T(8,128)(2,1)}, u32[]{:S(2)}) copy-start(bf16[1,2304,512]{2,1,0:T(8,128)(2,1)} %param.8) | copy-start | bytes 7077892
  2.5 1.9 %copy-start.1 = (s32[2048]{0:T(1024)S(1)}, s32[2048]{0:T(1024)}, u32[]{:S(2)}) copy-start(s32[2048]{0:T(1024)} %param.12) | copy-start | bytes 24580
  2.6 1.9 %copy-start.3 = (s32[1,4]{1,0:T(1,128)S(1)}, s32[1,4]{1,0:T(1,128)}, u32[]{:S(2)}) copy-start(s32[1,4]{1,0:T(1,128)} %band_ref.1) | copy-start | bytes 52
  13.7 3.2 %collective-permute-start = (bf16[1280,512]{1,0:T(8,128)(2,1)S(1)}, bf16[1280,512]{1,0:T(8,128)(2,1)S(1)}, u32[]{:S(2)}, u32[]{:S(2)}) collective-permute-start(bf16[1280,512]{1,0:T(8,128)(2,1)S(1)} %get-tuple-element.38.send_ref), channel_id=1, source_target_pairs={{0,1},{1,0},{2,3},{3,2},{4,5},{5,4},{6,7},{7,6},{8,9},{9,8},{10,11... | collective-permute-start | bytes 3932168 | tf_op jit(solution)/shard_map/ppermute | solution.py:574
  18.5 11.2 %collective-permute-start.1 = (f16[1288,128]{1,0:T(8,128)(2,1)S(1)}, f16[1288,128]{1,0:T(8,128)(2,1)S(1)}, u32[]{:S(2)}, u32[]{:S(2)}) collective-permute-start(f16[1288,128]{1,0:T(8,128)(2,1)S(1)} %convert_bitcast_fusion), channel_id=1, source_target_pairs={{0,2},{1,3},{2,0},{3,1},{4,6},{5,7},{6,4},{7,5},{8,10},{9,11},{10,... | collective-permute-start | bytes 989192 | tf_op jit(solution)/shard_map/ppermute | solution.py:574
  21.5 8.2 %collective-permute-start.2 = (f16[520,256]{1,0:T(8,128)(2,1)S(1)}, f16[520,256]{1,0:T(8,128)(2,1)S(1)}, u32[]{:S(2)}, u32[]{:S(2)}) collective-permute-start(f16[520,256]{1,0:T(8,128)(2,1)S(1)} %convert_element_type.239), channel_id=1, source_target_pairs={{0,4},{1,5},{2,6},{3,7},{4,0},{5,1},{6,2},{7,3},{8,12},{9,13},{10,... | collective-permute-start | bytes 798728 | tf_op jit(solution)/shard_map/ppermute | solution.py:574
  24.1 9.5 %collective-permute-start.10 = (f16[2,80,128]{2,1,0:T(8,128)(2,1)S(1)}, f16[2,80,128]{2,1,0:T(8,128)(2,1)S(1)}, u32[]{:S(2)}, u32[]{:S(2)}) collective-permute-start(f16[2,80,128]{2,1,0:T(8,128)(2,1)S(1)} %convert_element_type.248), channel_id=1, source_target_pairs={{0,24},{1,25},{2,26},{3,27},{4,28},{5,29},{6,30},{7,31},{8,16},{9,... | collective-permute-start | bytes 122888 | tf_op jit(solution)/shard_map/ppermute | solution.py:574
  27.7 5.9 %collective-permute-start.8 = (f16[2,80,128]{2,1,0:T(8,128)(2,1)S(1)}, f16[2,80,128]{2,1,0:T(8,128)(2,1)S(1)}, u32[]{:S(2)}, u32[]{:S(2)}) collective-permute-start(f16[2,80,128]{2,1,0:T(8,128)(2,1)S(1)} %convert_element_type.248), channel_id=1, source_target_pairs={{0,8},{1,9},{2,10},{3,11},{4,12},{5,13},{6,14},{7,15},{8,0},{9,1},... | collective-permute-start | bytes 122888 | tf_op jit(solution)/shard_map/ppermute | solution.py:574
  27.7 5.9 %collective-permute-start.9 = (f16[2,80,128]{2,1,0:T(8,128)(2,1)S(1)}, f16[2,80,128]{2,1,0:T(8,128)(2,1)S(1)}, u32[]{:S(2)}, u32[]{:S(2)}) collective-permute-start(f16[2,80,128]{2,1,0:T(8,128)(2,1)S(1)} %convert_element_type.248), channel_id=1, source_target_pairs={{0,16},{1,17},{2,18},{3,19},{4,20},{5,21},{6,22},{7,23},{8,24},{9,... | collective-permute-start | bytes 122888 | tf_op jit(solution)/shard_map/ppermute | solution.py:574
  30.5 12.9 %copy-start.2 = (f32[1,128]{1,0:T(1,128)S(1)}, f32[1,128]{1,0:T(1,128)}, u32[]{:S(2)}) copy-start(f32[1,128]{1,0:T(1,128)} %prior_ref.3) | copy-start | bytes 1540
  30.5 8.3 %collective-permute-start.3 = (f16[264,512]{1,0:T(8,128)(2,1)S(1)}, f16[264,512]{1,0:T(8,128)(2,1)S(1)}, u32[]{:S(2)}, u32[]{:S(2)}) collective-permute-start(f16[264,512]{1,0:T(8,128)(2,1)S(1)} %pad_maximum_fusion), channel_id=1, source_target_pairs={{0,4},{1,5},{2,6},{3,7},{4,0},{5,1},{6,2},{7,3},{8,12},{9,13},{10,... | collective-permute-start | bytes 811016 | tf_op jit(solution)/shard_map/ppermute | solution.py:574
  32.1 5.2 %collective-permute-start.4 = (f16[264,256]{1,0:T(8,128)(2,1)S(1)}, f16[264,256]{1,0:T(8,128)(2,1)S(1)}, u32[]{:S(2)}, u32[]{:S(2)}) collective-permute-start(f16[264,256]{1,0:T(8,128)(2,1)S(1)} %pad_maximum_fusion.5), channel_id=1, source_target_pairs={{0,2},{1,3},{2,0},{3,1},{4,6},{5,7},{6,4},{7,5},{8,10},{9,11},{10,... | collective-permute-start | bytes 405512 | tf_op jit(solution)/shard_map/ppermute | solution.py:574
  33.7 9.6 %collective-permute-start.12 = (f16[80,128]{1,0:T(8,128)(2,1)S(1)}, f16[80,128]{1,0:T(8,128)(2,1)S(1)}, u32[]{:S(2)}, u32[]{:S(2)}) collective-permute-start(f16[80,128]{1,0:T(8,128)(2,1)S(1)} %get-tuple-element.100), channel_id=1, source_target_pairs={{0,6},{1,7},{2,4},{3,5},{4,2},{5,3},{6,0},{7,1},{8,14},{9,15},{10,... | collective-permute-start | bytes 61448 | tf_op jit(solution)/shard_map/ppermute | solution.py:574
  34.3 9.0 %collective-permute-start.13 = (f16[80,128]{1,0:T(8,128)(2,1)S(1)}, f16[80,128]{1,0:T(8,128)(2,1)S(1)}, u32[]{:S(2)}, u32[]{:S(2)}) collective-permute-start(f16[80,128]{1,0:T(8,128)(2,1)S(1)} %get-tuple-element.100), channel_id=1, source_target_pairs={{0,2},{1,3},{2,0},{3,1},{4,6},{5,7},{6,4},{7,5},{8,10},{9,11},{10,... | collective-permute-start | bytes 61448 | tf_op jit(solution)/shard_map/ppermute | solution.py:574
  35.8 7.3 %collective-permute-start.11 = (f16[80,128]{1,0:T(8,128)(2,1)S(1)}, f16[80,128]{1,0:T(8,128)(2,1)S(1)}, u32[]{:S(2)}, u32[]{:S(2)}) collective-permute-start(f16[80,128]{1,0:T(8,128)(2,1)S(1)} %get-tuple-element.62), channel_id=1, source_target_pairs={{0,4},{1,5},{2,6},{3,7},{4,0},{5,1},{6,2},{7,3},{8,12},{9,13},{10,... | collective-permute-start | bytes 61448 | tf_op jit(solution)/shard_map/ppermute | solution.py:574
  39.2 10.0 %collective-permute-start.5 = (f16[72,768]{1,0:T(8,128)(2,1)S(1)}, f16[72,768]{1,0:T(8,128)(2,1)S(1)}, u32[]{:S(2)}, u32[]{:S(2)}) collective-permute-start(f16[72,768]{1,0:T(8,128)(2,1)S(1)} %get-tuple-element.54), channel_id=1, source_target_pairs={{0,16},{1,17},{2,18},{3,19},{4,20},{5,21},{6,22},{7,23},{8,24},{9,... | collective-permute-start | bytes 331784 | tf_op jit(solution)/shard_map/ppermute | solution.py:574
  41.8 7.4 %collective-permute-start.6 = (f16[72,768]{1,0:T(8,128)(2,1)S(1)}, f16[72,768]{1,0:T(8,128)(2,1)S(1)}, u32[]{:S(2)}, u32[]{:S(2)}) collective-permute-start(f16[72,768]{1,0:T(8,128)(2,1)S(1)} %get-tuple-element.55), channel_id=1, source_target_pairs={{0,24},{1,25},{2,26},{3,27},{4,28},{5,29},{6,30},{7,31},{8,16},{9,... | collective-permute-start | bytes 331784 | tf_op jit(solution)/shard_map/ppermute | solution.py:574
  43.1 6.8 %collective-permute-start.7 = (f16[72,768]{1,0:T(8,128)(2,1)S(1)}, f16[72,768]{1,0:T(8,128)(2,1)S(1)}, u32[]{:S(2)}, u32[]{:S(2)}) collective-permute-start(f16[72,768]{1,0:T(8,128)(2,1)S(1)} %get-tuple-element.56), channel_id=1, source_target_pairs={{0,8},{1,9},{2,10},{3,11},{4,12},{5,13},{6,14},{7,15},{8,0},{9,1},... | collective-permute-start | bytes 331784 | tf_op jit(solution)/shard_map/ppermute | solution.py:574

commit v7 on v6

--- a/solution.py
+++ b/solution.py
@@ -339,7 +339,7 @@
         send_x_ref[at : at + half, :] = side[y, half:, :] * scale
 
 
-def expand_kernel(n_z, packed_ref, out_ref):
+def expand_kernel(n_z, packed_ref, level_ref, out_ref, send_ref):
     z, x, _, _ = place_of()
     rows = OB // (n_z * PAIR)
     place = {pair: i for i, pair in enumerate(lower_blocks())}
@@ -355,6 +355,9 @@
                 out_ref[pl.ds(to, rows), t * LANES : (t + 1) * LANES] = block[
                     b * rows : (b + 1) * rows, :
                 ]
+    level = level_ref[:1, :]
+    send_ref[:HEAD, :] = jnp.broadcast_to(level, (HEAD, OB))
+    send_ref[HEAD:, :] = out_ref[OB // PAIR :, :] * jnp.exp2(TOP_LEVEL - level)
 
 
 def panel_kernel(n_y, mine_ref, other_ref, level_ref, out_ref):
@@ -427,16 +430,19 @@
     )(other, square, side)
 
 
-def expand(packed, n_z):
+def expand(packed, level, n_z):
     array = pl.BlockSpec(memory_space=pltpu.VMEM)
     return pl.pallas_call(
         functools.partial(expand_kernel, n_z),
-        out_shape=jax.ShapeDtypeStruct((OB, OB), jnp.float32),
-        in_specs=[array],
-        out_specs=array,
+        out_shape=(
+            jax.ShapeDtypeStruct((OB, OB), jnp.float32),
+            jax.ShapeDtypeStruct((HEAD + OB // PAIR, OB), jnp.float32),
+        ),
+        in_specs=[array, array],
+        out_specs=(array, array),
         compiler_params=pltpu.CompilerParams(vmem_limit_bytes=8 * 1024 * 1024),
         name="expand",
-    )(packed)
+    )(packed, level)
 
 
 def panel_products(mine, other, level, n_y):
@@ -600,11 +606,11 @@
         jnp.maximum, [level_of(message) for message in from_y], level[:1, :LANES]
     ) + grown
     left_level = jnp.concatenate([left_level] * (OB // LANES), axis=1)
-    left = expand(packed, n_z)
+    left, over_x = expand(packed, left_level, n_z)
     right = keep_x + values_of(from_x).reshape(n_y, half, KB)
     right_level = jnp.maximum(level[:1, :KB], level_of(from_x)) + 1.0
 
-    over_x = message_of(left[half:], left_level)
+    over_x = over_x.astype(jnp.float16)
     over_y = [message_of(right[j], right_level) for j in range(1, n_y)]
     over_x, over_y = lax.optimization_barrier((over_x, over_y))
     panel_z, _ = lax.optimization_barrier((panel_z, (over_x, over_y)))

time: 50.9 us -> 50.8 us (level)
  no operation moved by 1% of the time
where the time goes in v7:
time: 50.8 us; the launch traced here: 50.6 us
  Pallas kernels  21.8 us (43%)
  starting transfers between devices  20.2 us (40%)
  waiting for transfers between devices  4.09 us (8%)
  other arithmetic  1.86 us (4%)
  between operations  1.65 us (3%)
  local copies, waits for them, and re-layouts  1 us (2%)
    ppermute x14, starting transfers between devices, swap(): return lax.ppermute(values, AXES, pairs)  20.2 us
    pallas_call x1, Pallas kernels, reduce_rows(): pl.pallas_call(functools.partial(local_kernel, n_y), out_shape=tuple((jax...  9.2 us
    pallas_call x1, Pallas kernels, factor_panel(): pl.pallas_call(factor_kernel, out_shape=jax.ShapeDtypeStruct((n, n), jnp....  5.25 us
    ppermute x14, waiting for transfers between devices, swap(): return lax.ppermute(values, AXES, pairs)  4.09 us
    pallas_call x1, Pallas kernels, own_products(): pl.pallas_call(functools.partial(own_product_kernel, n_y, n_z), out_shape...  2.56 us
    pallas_call x1, Pallas kernels, begin_normal(): pl.pallas_call(sweep_kernel, out_shape=jax.ShapeDtypeStruct((n, n), jnp.f...  1.86 us
    pallas_call x1, Pallas kernels, products(): pl.pallas_call(functools.partial(product_kernel, n_y, n_z), out_shape=tup...  1.42 us
  transfers between devices with their start and end apart: 14, of which 5 were waited for; matrix products, arithmetic and copies ran while one was open for 2% of the time, Pallas kernels for 18%

profile of v7, /device:TPU:0, one launch (start us, length us, event | category | flops | bytes accessed | tf_op | source)
XLA Modules:
  0.0 50.6 jit_solution(18300512755205189080)
XLA Ops:
  1.3 0.9 %copy-done.4 = bf16[1,256,512]{2,1,0:T(8,128)(2,1)S(1)} copy-done((bf16[1,256,512]{2,1,0:T(8,128)(2,1)S(1)}, bf16[1,256,512]{2,1,0:T(8,128)(2,1)}, u32[]{:S(2)}) %copy-start.4) | copy-done | bytes 262168
  2.6 1.9 %first_sweeps.1.begun_ref = f32[256,256]{1,0:T(8,128)S(1)} custom-call(f32[1,256]{1,0:T(1,128)S(1)} %copy-done.5, f32[256,256]{1,0:T(8,128)S(1)} %get-tuple-element.39.normal_ref), custom_call_target="tpu_custom_call" | custom-call | flops 4000000000 | tf_op jit(solution)/shard_map/first_sweeps/pallas_call | solution.py:237
  4.5 9.2 %reduce_rows.1 = (bf16[1280,512]{1,0:T(8,128)(2,1)S(1)}, bf16[1024,512]{1,0:T(8,128)(2,1)S(1)}, bf16[2,256,512]{2,1,0:T(8,128)(2,1)S(1)}) custom-call(s32[1]{0:T(128)S(6)} %copy.9.count_ref, s32[1,4]{1,0:T(1,128)S(1)} %copy-done.3, s32[4,4,128]{2,1,0:T(4,128)S(1)} %bitcast.80, bf16[256,512]{1,0:T(8,128)(2,1)S(1)} %get-tuple-element.38.rows_ref, ...), custom_call_target="tpu_custom_call" | custom-call | tf_op jit(solution)/shard_map/reduce_rows/pallas_call | solution.py:254
  13.7 0.5 %collective-permute-start = (bf16[1280,512]{1,0:T(8,128)(2,1)S(1)}, bf16[1280,512]{1,0:T(8,128)(2,1)S(1)}, u32[]{:S(2)}, u32[]{:S(2)}) collective-permute-start(bf16[1280,512]{1,0:T(8,128)(2,1)S(1)} %get-tuple-element.40.send_ref), channel_id=1, source_target_pairs={{0,1},{1,0},{2,3},{3,2},{4,5},{5,4},{6,7},{7,6},{8,9},{9,8},{10,11... | collective-permute-start | bytes 3932168 | tf_op jit(solution)/shard_map/ppermute | solution.py:580
  14.2 2.6 %own_products.1 = (bf16[1024,512]{1,0:T(8,128)(2,1)S(1)}, f32[2,512,512]{2,1,0:T(8,128)S(1)}, f32[2,512,256]{2,1,0:T(8,128)S(1)}) custom-call(bf16[1024,512]{1,0:T(8,128)(2,1)S(1)} %get-tuple-element.41.own_ref, bf16[1280,512]{1,0:T(8,128)(2,1)S(1)} %get-tuple-element.40.send_ref, bf16[2,256,512]{2,1,0:T(8,128)(2,1)S(1)} %get-tuple-element.42.gain_ref, ...), custom_call_target="tpu_custom_call" | custom-call | flops 1610612736 | tf_op jit(solution)/shard_map/own_products/pallas_call | solution.py:389
  16.9 1.4 %products.1 = (f32[1280,128]{1,0:T(8,128)S(1)}, f32[1,1288,128]{2,1,0:T(8,128)S(1)}, f32[2,256,256]{2,1,0:T(8,128)S(1)}, f32[520,256]{1,0:T(8,128)S(1)}, f32[8,512]{1,0:T(8,128)S(1)}) custom-call(bf16[1280,512]{1,0:T(8,128)(2,1)S(1)} %collective-permute-done.other_ref, f32[2,512,512]{2,1,0:T(8,128)S(1)} %get-tuple-element.43.square_ref, ...), custom_call_target="tpu_custom_call" | custom-call | tf_op jit(solution)/shard_map/products/pallas_call | solution.py:418
  18.5 2.9 %collective-permute-start.1 = (f16[1288,128]{1,0:T(8,128)(2,1)S(1)}, f16[1288,128]{1,0:T(8,128)(2,1)S(1)}, u32[]{:S(2)}, u32[]{:S(2)}) collective-permute-start(f16[1288,128]{1,0:T(8,128)(2,1)S(1)} %convert_bitcast_fusion), channel_id=1, source_target_pairs={{0,2},{1,3},{2,0},{3,1},{4,6},{5,7},{6,4},{7,5},{8,10},{9,11},{10,... | collective-permute-start | bytes 989192 | tf_op jit(solution)/shard_map/ppermute | solution.py:580
  21.5 1.6 %collective-permute-start.2 = (f16[520,256]{1,0:T(8,128)(2,1)S(1)}, f16[520,256]{1,0:T(8,128)(2,1)S(1)}, u32[]{:S(2)}, u32[]{:S(2)}) collective-permute-start(f16[520,256]{1,0:T(8,128)(2,1)S(1)} %convert_element_type.241), channel_id=1, source_target_pairs={{0,4},{1,5},{2,6},{3,7},{4,0},{5,1},{6,2},{7,3},{8,12},{9,13},{10,... | collective-permute-start | bytes 798728 | tf_op jit(solution)/shard_map/ppermute | solution.py:580
  23.1 1.0 %panel_products.1 = f32[2,80,128]{2,1,0:T(8,128)S(1)} custom-call(bf16[1024,512]{1,0:T(8,128)(2,1)S(1)} %get-tuple-element.61.mine_ref, bf16[1280,512]{1,0:T(8,128)(2,1)S(1)} %collective-permute-done.other_ref, f32[8,512]{1,0:T(8,128)S(1)} %get-tuple-element.49.level_ref), custom_call_target="tpu_custom_call" | custom-call | flops 268435456 | tf_op jit(solution)/shard_map/panel_products/pallas_call | solution.py:450
  24.1 3.7 %collective-permute-start.10 = (f16[2,80,128]{2,1,0:T(8,128)(2,1)S(1)}, f16[2,80,128]{2,1,0:T(8,128)(2,1)S(1)}, u32[]{:S(2)}, u32[]{:S(2)}) collective-permute-start(f16[2,80,128]{2,1,0:T(8,128)(2,1)S(1)} %convert_element_type.251), channel_id=1, source_target_pairs={{0,24},{1,25},{2,26},{3,27},{4,28},{5,29},{6,30},{7,31},{8,16},{9,... | collective-permute-start | bytes 122888 | tf_op jit(solution)/shard_map/ppermute | solution.py:580
  27.7 0.8 %collective-permute-start.9 = (f16[2,80,128]{2,1,0:T(8,128)(2,1)S(1)}, f16[2,80,128]{2,1,0:T(8,128)(2,1)S(1)}, u32[]{:S(2)}, u32[]{:S(2)}) collective-permute-start(f16[2,80,128]{2,1,0:T(8,128)(2,1)S(1)} %convert_element_type.251), channel_id=1, source_target_pairs={{0,16},{1,17},{2,18},{3,19},{4,20},{5,21},{6,22},{7,23},{8,24},{9,... | collective-permute-start | bytes 122888 | tf_op jit(solution)/shard_map/ppermute | solution.py:580
  28.5 1.2 %collective-permute-done.2 = f16[520,256]{1,0:T(8,128)(2,1)S(1)} collective-permute-done((f16[520,256]{1,0:T(8,128)(2,1)S(1)}, f16[520,256]{1,0:T(8,128)(2,1)S(1)}, u32[]{:S(2)}, u32[]{:S(2)}) %collective-permute-start.2) | collective-permute-done | bytes 266272 | tf_op jit(solution)/shard_map/ppermute | solution.py:580
  30.4 1.6 %collective-permute-start.3 = (f16[264,512]{1,0:T(8,128)(2,1)S(1)}, f16[264,512]{1,0:T(8,128)(2,1)S(1)}, u32[]{:S(2)}, u32[]{:S(2)}) collective-permute-start(f16[264,512]{1,0:T(8,128)(2,1)S(1)} %convert_element_type.244), channel_id=1, source_target_pairs={{0,4},{1,5},{2,6},{3,7},{4,0},{5,1},{6,2},{7,3},{8,12},{9,13},{10,... | collective-permute-start | bytes 811016 | tf_op jit(solution)/shard_map/ppermute | solution.py:580
  32.0 1.5 %collective-permute-start.4 = (f16[264,256]{1,0:T(8,128)(2,1)S(1)}, f16[264,256]{1,0:T(8,128)(2,1)S(1)}, u32[]{:S(2)}, u32[]{:S(2)}) collective-permute-start(f16[264,256]{1,0:T(8,128)(2,1)S(1)} %pad_maximum_fusion.4), channel_id=1, source_target_pairs={{0,2},{1,3},{2,0},{3,1},{4,6},{5,7},{6,4},{7,5},{8,10},{9,11},{10,... | collective-permute-start | bytes 405512 | tf_op jit(solution)/shard_map/ppermute | solution.py:580
  33.6 0.5 %collective-permute-start.12 = (f16[80,128]{1,0:T(8,128)(2,1)S(1)}, f16[80,128]{1,0:T(8,128)(2,1)S(1)}, u32[]{:S(2)}, u32[]{:S(2)}) collective-permute-start(f16[80,128]{1,0:T(8,128)(2,1)S(1)} %get-tuple-element.102), channel_id=1, source_target_pairs={{0,6},{1,7},{2,4},{3,5},{4,2},{5,3},{6,0},{7,1},{8,14},{9,15},{10,... | collective-permute-start | bytes 61448 | tf_op jit(solution)/shard_map/ppermute | solution.py:580
  34.2 1.5 %collective-permute-start.13 = (f16[80,128]{1,0:T(8,128)(2,1)S(1)}, f16[80,128]{1,0:T(8,128)(2,1)S(1)}, u32[]{:S(2)}, u32[]{:S(2)}) collective-permute-start(f16[80,128]{1,0:T(8,128)(2,1)S(1)} %get-tuple-element.102), channel_id=1, source_target_pairs={{0,2},{1,3},{2,0},{3,1},{4,6},{5,7},{6,4},{7,5},{8,10},{9,11},{10,... | collective-permute-start | bytes 61448 | tf_op jit(solution)/shard_map/ppermute | solution.py:580
  35.7 1.5 %collective-permute-start.11 = (f16[80,128]{1,0:T(8,128)(2,1)S(1)}, f16[80,128]{1,0:T(8,128)(2,1)S(1)}, u32[]{:S(2)}, u32[]{:S(2)}) collective-permute-start(f16[80,128]{1,0:T(8,128)(2,1)S(1)} %get-tuple-element.66), channel_id=1, source_target_pairs={{0,4},{1,5},{2,6},{3,7},{4,0},{5,1},{6,2},{7,3},{8,12},{9,13},{10,... | collective-permute-start | bytes 61448 | tf_op jit(solution)/shard_map/ppermute | solution.py:580
  37.2 1.5 %collective-permute-done.3 = f16[264,512]{1,0:T(8,128)(2,1)S(1)} collective-permute-done((f16[264,512]{1,0:T(8,128)(2,1)S(1)}, f16[264,512]{1,0:T(8,128)(2,1)S(1)}, u32[]{:S(2)}, u32[]{:S(2)}) %collective-permute-start.3) | collective-permute-done | bytes 270368 | tf_op jit(solution)/shard_map/ppermute | solution.py:580
  39.1 2.6 %collective-permute-start.5 = (f16[72,768]{1,0:T(8,128)(2,1)S(1)}, f16[72,768]{1,0:T(8,128)(2,1)S(1)}, u32[]{:S(2)}, u32[]{:S(2)}) collective-permute-start(f16[72,768]{1,0:T(8,128)(2,1)S(1)} %get-tuple-element.58), channel_id=1, source_target_pairs={{0,16},{1,17},{2,18},{3,19},{4,20},{5,21},{6,22},{7,23},{8,24},{9,... | collective-permute-start | bytes 331784 | tf_op jit(solution)/shard_map/ppermute | solution.py:580
  41.7 1.3 %collective-permute-start.6 = (f16[72,768]{1,0:T(8,128)(2,1)S(1)}, f16[72,768]{1,0:T(8,128)(2,1)S(1)}, u32[]{:S(2)}, u32[]{:S(2)}) collective-permute-start(f16[72,768]{1,0:T(8,128)(2,1)S(1)} %get-tuple-element.59), channel_id=1, source_target_pairs={{0,24},{1,25},{2,26},{3,27},{4,28},{5,29},{6,30},{7,31},{8,16},{9,... | collective-permute-start | bytes 331784 | tf_op jit(solution)/shard_map/ppermute | solution.py:580
  43.3 5.2 %factor_panel.1 = f32[128,128]{1,0:T(8,128)} custom-call(f32[72,128]{1,0:T(8,128)S(1)} %add_add_fusion.panel_ref, f32[1,128]{1,0:T(1,128)S(1)} %copy-done.2), custom_call_target="tpu_custom_call" | custom-call | flops 2097152 | bytes 196608 | tf_op jit(solution)/shard_map/factor_panel/pallas_call | solution.py:538
  48.5 0.5 %collective-permute-done.5 = f16[72,768]{1,0:T(8,128)(2,1)S(1)} collective-permute-done((f16[72,768]{1,0:T(8,128)(2,1)S(1)}, f16[72,768]{1,0:T(8,128)(2,1)S(1)}, u32[]{:S(2)}, u32[]{:S(2)}) %collective-permute-start.5) | collective-permute-done | bytes 110624 | tf_op jit(solution)/shard_map/ppermute | solution.py:580
  49.1 0.7 %collective-permute-done.7 = f16[72,768]{1,0:T(8,128)(2,1)S(1)} collective-permute-done((f16[72,768]{1,0:T(8,128)(2,1)S(1)}, f16[72,768]{1,0:T(8,128)(2,1)S(1)}, u32[]{:S(2)}, u32[]{:S(2)}) %collective-permute-start.7) | collective-permute-done | bytes 110624 | tf_op jit(solution)/shard_map/ppermute | solution.py:580
  49.9 0.8 %fusion.10 = f32[1,64,768]{2,1,0:T(8,128)} fusion(f32[256,512]{1,0:T(8,128)S(1)} %multiply_add_fusion.1, f32[256,256]{1,0:T(8,128)S(1)} %fusion, f32[768]{0:T(1024)S(1)} %exponential_reduce_fusion, f16[72,768]{1,0:T(8,128)(2,1)S(1)} %collective-permute-done.7, f32[768]{0:T(1024)S(1)} %exponential_reduce_fusion.1, ...), kind=kLoop, calls=%fused_computation.22 | loop fusion | flops 491520 | bytes 1287168 | tf_op jit(solution)/shard_map/broadcast_in_dim | solution.py:649
  (60 shorter events, 2.0 us)
Async XLA Ops:
  0.6 1.9 %copy-start.5 = (f32[1,256]{1,0:T(1,128)S(1)}, f32[1,256]{1,0:T(1,128)}, u32[]{:S(2)}) copy-start(f32[1,256]{1,0:T(1,128)} %prior_ref.2) | copy-start | bytes 3076
  1.3 1.0 %copy-start.4 = (bf16[1,256,512]{2,1,0:T(8,128)(2,1)S(1)}, bf16[1,256,512]{2,1,0:T(8,128)(2,1)}, u32[]{:S(2)}) copy-start(bf16[1,256,512]{2,1,0:T(8,128)(2,1)} %param.7) | copy-start | bytes 786436
  2.5 1.9 %copy-start = (bf16[1,2304,512]{2,1,0:T(8,128)(2,1)S(1)}, bf16[1,2304,512]{2,1,0:T(8,128)(2,1)}, u32[]{:S(2)}) copy-start(bf16[1,2304,512]{2,1,0:T(8,128)(2,1)} %param.8) | copy-start | bytes 7077892
  2.5 1.9 %copy-start.1 = (s32[2048]{0:T(1024)S(1)}, s32[2048]{0:T(1024)}, u32[]{:S(2)}) copy-start(s32[2048]{0:T(1024)} %param.12) | copy-start | bytes 24580
  2.6 1.9 %copy-start.3 = (s32[1,4]{1,0:T(1,128)S(1)}, s32[1,4]{1,0:T(1,128)}, u32[]{:S(2)}) copy-start(s32[1,4]{1,0:T(1,128)} %band_ref.1) | copy-start | bytes 52
  13.7 3.2 %collective-permute-start = (bf16[1280,512]{1,0:T(8,128)(2,1)S(1)}, bf16[1280,512]{1,0:T(8,128)(2,1)S(1)}, u32[]{:S(2)}, u32[]{:S(2)}) collective-permute-start(bf16[1280,512]{1,0:T(8,128)(2,1)S(1)} %get-tuple-element.40.send_ref), channel_id=1, source_target_pairs={{0,1},{1,0},{2,3},{3,2},{4,5},{5,4},{6,7},{7,6},{8,9},{9,8},{10,11... | collective-permute-start | bytes 3932168 | tf_op jit(solution)/shard_map/ppermute | solution.py:580
  18.5 11.2 %collective-permute-start.1 = (f16[1288,128]{1,0:T(8,128)(2,1)S(1)}, f16[1288,128]{1,0:T(8,128)(2,1)S(1)}, u32[]{:S(2)}, u32[]{:S(2)}) collective-permute-start(f16[1288,128]{1,0:T(8,128)(2,1)S(1)} %convert_bitcast_fusion), channel_id=1, source_target_pairs={{0,2},{1,3},{2,0},{3,1},{4,6},{5,7},{6,4},{7,5},{8,10},{9,11},{10,... | collective-permute-start | bytes 989192 | tf_op jit(solution)/shard_map/ppermute | solution.py:580
  21.5 8.2 %collective-permute-start.2 = (f16[520,256]{1,0:T(8,128)(2,1)S(1)}, f16[520,256]{1,0:T(8,128)(2,1)S(1)}, u32[]{:S(2)}, u32[]{:S(2)}) collective-permute-start(f16[520,256]{1,0:T(8,128)(2,1)S(1)} %convert_element_type.241), channel_id=1, source_target_pairs={{0,4},{1,5},{2,6},{3,7},{4,0},{5,1},{6,2},{7,3},{8,12},{9,13},{10,... | collective-permute-start | bytes 798728 | tf_op jit(solution)/shard_map/ppermute | solution.py:580
  24.1 9.5 %collective-permute-start.10 = (f16[2,80,128]{2,1,0:T(8,128)(2,1)S(1)}, f16[2,80,128]{2,1,0:T(8,128)(2,1)S(1)}, u32[]{:S(2)}, u32[]{:S(2)}) collective-permute-start(f16[2,80,128]{2,1,0:T(8,128)(2,1)S(1)} %convert_element_type.251), channel_id=1, source_target_pairs={{0,24},{1,25},{2,26},{3,27},{4,28},{5,29},{6,30},{7,31},{8,16},{9,... | collective-permute-start | bytes 122888 | tf_op jit(solution)/shard_map/ppermute | solution.py:580
  27.7 5.8 %collective-permute-start.8 = (f16[2,80,128]{2,1,0:T(8,128)(2,1)S(1)}, f16[2,80,128]{2,1,0:T(8,128)(2,1)S(1)}, u32[]{:S(2)}, u32[]{:S(2)}) collective-permute-start(f16[2,80,128]{2,1,0:T(8,128)(2,1)S(1)} %convert_element_type.251), channel_id=1, source_target_pairs={{0,8},{1,9},{2,10},{3,11},{4,12},{5,13},{6,14},{7,15},{8,0},{9,1},... | collective-permute-start | bytes 122888 | tf_op jit(solution)/shard_map/ppermute | solution.py:580
  27.7 5.8 %collective-permute-start.9 = (f16[2,80,128]{2,1,0:T(8,128)(2,1)S(1)}, f16[2,80,128]{2,1,0:T(8,128)(2,1)S(1)}, u32[]{:S(2)}, u32[]{:S(2)}) collective-permute-start(f16[2,80,128]{2,1,0:T(8,128)(2,1)S(1)} %convert_element_type.251), channel_id=1, source_target_pairs={{0,16},{1,17},{2,18},{3,19},{4,20},{5,21},{6,22},{7,23},{8,24},{9,... | collective-permute-start | bytes 122888 | tf_op jit(solution)/shard_map/ppermute | solution.py:580
  30.4 12.9 %copy-start.2 = (f32[1,128]{1,0:T(1,128)S(1)}, f32[1,128]{1,0:T(1,128)}, u32[]{:S(2)}) copy-start(f32[1,128]{1,0:T(1,128)} %prior_ref.3) | copy-start | bytes 1540
  30.4 8.3 %collective-permute-start.3 = (f16[264,512]{1,0:T(8,128)(2,1)S(1)}, f16[264,512]{1,0:T(8,128)(2,1)S(1)}, u32[]{:S(2)}, u32[]{:S(2)}) collective-permute-start(f16[264,512]{1,0:T(8,128)(2,1)S(1)} %convert_element_type.244), channel_id=1, source_target_pairs={{0,4},{1,5},{2,6},{3,7},{4,0},{5,1},{6,2},{7,3},{8,12},{9,13},{10,... | collective-permute-start | bytes 811016 | tf_op jit(solution)/shard_map/ppermute | solution.py:580
  32.0 5.2 %collective-permute-start.4 = (f16[264,256]{1,0:T(8,128)(2,1)S(1)}, f16[264,256]{1,0:T(8,128)(2,1)S(1)}, u32[]{:S(2)}, u32[]{:S(2)}) collective-permute-start(f16[264,256]{1,0:T(8,128)(2,1)S(1)} %pad_maximum_fusion.4), channel_id=1, source_target_pairs={{0,2},{1,3},{2,0},{3,1},{4,6},{5,7},{6,4},{7,5},{8,10},{9,11},{10,... | collective-permute-start | bytes 405512 | tf_op jit(solution)/shard_map/ppermute | solution.py:580
  33.6 9.6 %collective-permute-start.12 = (f16[80,128]{1,0:T(8,128)(2,1)S(1)}, f16[80,128]{1,0:T(8,128)(2,1)S(1)}, u32[]{:S(2)}, u32[]{:S(2)}) collective-permute-start(f16[80,128]{1,0:T(8,128)(2,1)S(1)} %get-tuple-element.102), channel_id=1, source_target_pairs={{0,6},{1,7},{2,4},{3,5},{4,2},{5,3},{6,0},{7,1},{8,14},{9,15},{10,... | collective-permute-start | bytes 61448 | tf_op jit(solution)/shard_map/ppermute | solution.py:580
  34.2 9.0 %collective-permute-start.13 = (f16[80,128]{1,0:T(8,128)(2,1)S(1)}, f16[80,128]{1,0:T(8,128)(2,1)S(1)}, u32[]{:S(2)}, u32[]{:S(2)}) collective-permute-start(f16[80,128]{1,0:T(8,128)(2,1)S(1)} %get-tuple-element.102), channel_id=1, source_target_pairs={{0,2},{1,3},{2,0},{3,1},{4,6},{5,7},{6,4},{7,5},{8,10},{9,11},{10,... | collective-permute-start | bytes 61448 | tf_op jit(solution)/shard_map/ppermute | solution.py:580
  35.7 7.3 %collective-permute-start.11 = (f16[80,128]{1,0:T(8,128)(2,1)S(1)}, f16[80,128]{1,0:T(8,128)(2,1)S(1)}, u32[]{:S(2)}, u32[]{:S(2)}) collective-permute-start(f16[80,128]{1,0:T(8,128)(2,1)S(1)} %get-tuple-element.66), channel_id=1, source_target_pairs={{0,4},{1,5},{2,6},{3,7},{4,0},{5,1},{6,2},{7,3},{8,12},{9,13},{10,... | collective-permute-start | bytes 61448 | tf_op jit(solution)/shard_map/ppermute | solution.py:580
  39.1 10.0 %collective-permute-start.5 = (f16[72,768]{1,0:T(8,128)(2,1)S(1)}, f16[72,768]{1,0:T(8,128)(2,1)S(1)}, u32[]{:S(2)}, u32[]{:S(2)}) collective-permute-start(f16[72,768]{1,0:T(8,128)(2,1)S(1)} %get-tuple-element.58), channel_id=1, source_target_pairs={{0,16},{1,17},{2,18},{3,19},{4,20},{5,21},{6,22},{7,23},{8,24},{9,... | collective-permute-start | bytes 331784 | tf_op jit(solution)/shard_map/ppermute | solution.py:580
  41.7 7.4 %collective-permute-start.6 = (f16[72,768]{1,0:T(8,128)(2,1)S(1)}, f16[72,768]{1,0:T(8,128)(2,1)S(1)}, u32[]{:S(2)}, u32[]{:S(2)}) collective-permute-start(f16[72,768]{1,0:T(8,128)(2,1)S(1)} %get-tuple-element.59), channel_id=1, source_target_pairs={{0,24},{1,25},{2,26},{3,27},{4,28},{5,29},{6,30},{7,31},{8,16},{9,... | collective-permute-start | bytes 331784 | tf_op jit(solution)/shard_map/ppermute | solution.py:580
  43.0 6.8 %collective-permute-start.7 = (f16[72,768]{1,0:T(8,128)(2,1)S(1)}, f16[72,768]{1,0:T(8,128)(2,1)S(1)}, u32[]{:S(2)}, u32[]{:S(2)}) collective-permute-start(f16[72,768]{1,0:T(8,128)(2,1)S(1)} %get-tuple-element.60), channel_id=1, source_target_pairs={{0,8},{1,9},{2,10},{3,11},{4,12},{5,13},{6,14},{7,15},{8,0},{9,1},... | collective-permute-start | bytes 331784 | tf_op jit(solution)/shard_map/ppermute | solution.py:580

commit v8 on v7

--- a/solution.py
+++ b/solution.py
@@ -22,7 +22,7 @@
 BLOCK = 8
 GROUP = 2
 FACTOR_GROUP = 4
-FIRST = 4
+FIRST = 3
 TILE = 128
 ROWS = (((1,), (0,)), ((), ()))
 COLS = (((0,), (0,)), ((), ()))

time: 50.8 us -> 50.5 us (level)
  no operation moved by 1% of the time
where the time goes in v8:
time: 50.5 us; the launch traced here: 50.3 us
  Pallas kernels  21.6 us (43%)
  starting transfers between devices  20.3 us (40%)
  waiting for transfers between devices  3.89 us (8%)
  other arithmetic  1.68 us (3%)
  between operations  1.62 us (3%)
  local copies, waits for them, and re-layouts  1.21 us (2%)
    ppermute x14, starting transfers between devices, swap(): return lax.ppermute(values, AXES, pairs)  20.3 us
    pallas_call x1, Pallas kernels, reduce_rows(): pl.pallas_call(functools.partial(local_kernel, n_y), out_shape=tuple((jax...  9.33 us
    pallas_call x1, Pallas kernels, factor_panel(): pl.pallas_call(factor_kernel, out_shape=jax.ShapeDtypeStruct((n, n), jnp....  5.25 us
    ppermute x14, waiting for transfers between devices, swap(): return lax.ppermute(values, AXES, pairs)  3.89 us
    pallas_call x1, Pallas kernels, own_products(): pl.pallas_call(functools.partial(own_product_kernel, n_y, n_z), out_shape...  2.57 us
    pallas_call x1, Pallas kernels, products(): pl.pallas_call(functools.partial(product_kernel, n_y, n_z), out_shape=tup...  1.42 us
    pallas_call x1, Pallas kernels, begin_normal(): pl.pallas_call(sweep_kernel, out_shape=jax.ShapeDtypeStruct((n, n), jnp.f...  1.41 us
    unnamed x12, local copies, waits for them, and re-layouts  1.19 us
  transfers between devices with their start and end apart: 14, of which 5 were waited for; matrix products, arithmetic and copies ran while one was open for 2% of the time, Pallas kernels for 18%

profile of v8, /device:TPU:0, one launch (start us, length us, event | category | flops | bytes accessed | tf_op | source)
XLA Modules:
  0.0 50.3 jit_solution(18306856631745057755)
XLA Ops:
  1.3 0.9 %copy-done.4 = bf16[1,256,512]{2,1,0:T(8,128)(2,1)S(1)} copy-done((bf16[1,256,512]{2,1,0:T(8,128)(2,1)S(1)}, bf16[1,256,512]{2,1,0:T(8,128)(2,1)}, u32[]{:S(2)}) %copy-start.4) | copy-done | bytes 262168
  2.6 1.4 %first_sweeps.1.begun_ref = f32[256,256]{1,0:T(8,128)S(1)} custom-call(f32[1,256]{1,0:T(1,128)S(1)} %copy-done.5, f32[256,256]{1,0:T(8,128)S(1)} %get-tuple-element.39.normal_ref), custom_call_target="tpu_custom_call" | custom-call | flops 4000000000 | tf_op jit(solution)/shard_map/first_sweeps/pallas_call | solution.py:237
  4.2 9.3 %reduce_rows.1 = (bf16[1280,512]{1,0:T(8,128)(2,1)S(1)}, bf16[1024,512]{1,0:T(8,128)(2,1)S(1)}, bf16[2,256,512]{2,1,0:T(8,128)(2,1)S(1)}) custom-call(s32[1]{0:T(128)S(6)} %copy.9.count_ref, s32[1,4]{1,0:T(1,128)S(1)} %copy-done.3, s32[4,4,128]{2,1,0:T(4,128)S(1)} %bitcast.80, bf16[256,512]{1,0:T(8,128)(2,1)S(1)} %get-tuple-element.38.rows_ref, ...), custom_call_target="tpu_custom_call" | custom-call | tf_op jit(solution)/shard_map/reduce_rows/pallas_call | solution.py:254
  13.5 0.5 %collective-permute-start = (bf16[1280,512]{1,0:T(8,128)(2,1)S(1)}, bf16[1280,512]{1,0:T(8,128)(2,1)S(1)}, u32[]{:S(2)}, u32[]{:S(2)}) collective-permute-start(bf16[1280,512]{1,0:T(8,128)(2,1)S(1)} %get-tuple-element.40.send_ref), channel_id=1, source_target_pairs={{0,1},{1,0},{2,3},{3,2},{4,5},{5,4},{6,7},{7,6},{8,9},{9,8},{10,11... | collective-permute-start | bytes 3932168 | tf_op jit(solution)/shard_map/ppermute | solution.py:580
  14.1 2.6 %own_products.1 = (bf16[1024,512]{1,0:T(8,128)(2,1)S(1)}, f32[2,512,512]{2,1,0:T(8,128)S(1)}, f32[2,512,256]{2,1,0:T(8,128)S(1)}) custom-call(bf16[1024,512]{1,0:T(8,128)(2,1)S(1)} %get-tuple-element.41.own_ref, bf16[1280,512]{1,0:T(8,128)(2,1)S(1)} %get-tuple-element.40.send_ref, bf16[2,256,512]{2,1,0:T(8,128)(2,1)S(1)} %get-tuple-element.42.gain_ref, ...), custom_call_target="tpu_custom_call" | custom-call | flops 1610612736 | tf_op jit(solution)/shard_map/own_products/pallas_call | solution.py:389
  16.7 1.4 %products.1 = (f32[1280,128]{1,0:T(8,128)S(1)}, f32[1,1288,128]{2,1,0:T(8,128)S(1)}, f32[2,256,256]{2,1,0:T(8,128)S(1)}, f32[520,256]{1,0:T(8,128)S(1)}, f32[8,512]{1,0:T(8,128)S(1)}) custom-call(bf16[1280,512]{1,0:T(8,128)(2,1)S(1)} %collective-permute-done.other_ref, f32[2,512,512]{2,1,0:T(8,128)S(1)} %get-tuple-element.43.square_ref, ...), custom_call_target="tpu_custom_call" | custom-call | tf_op jit(solution)/shard_map/products/pallas_call | solution.py:418
  18.2 2.9 %collective-permute-start.1 = (f16[1288,128]{1,0:T(8,128)(2,1)S(1)}, f16[1288,128]{1,0:T(8,128)(2,1)S(1)}, u32[]{:S(2)}, u32[]{:S(2)}) collective-permute-start(f16[1288,128]{1,0:T(8,128)(2,1)S(1)} %convert_bitcast_fusion), channel_id=1, source_target_pairs={{0,2},{1,3},{2,0},{3,1},{4,6},{5,7},{6,4},{7,5},{8,10},{9,11},{10,... | collective-permute-start | bytes 989192 | tf_op jit(solution)/shard_map/ppermute | solution.py:580
  21.2 1.6 %collective-permute-start.2 = (f16[520,256]{1,0:T(8,128)(2,1)S(1)}, f16[520,256]{1,0:T(8,128)(2,1)S(1)}, u32[]{:S(2)}, u32[]{:S(2)}) collective-permute-start(f16[520,256]{1,0:T(8,128)(2,1)S(1)} %convert_element_type.241), channel_id=1, source_target_pairs={{0,4},{1,5},{2,6},{3,7},{4,0},{5,1},{6,2},{7,3},{8,12},{9,13},{10,... | collective-permute-start | bytes 798728 | tf_op jit(solution)/shard_map/ppermute | solution.py:580
  22.8 1.1 %panel_products.1 = f32[2,80,128]{2,1,0:T(8,128)S(1)} custom-call(bf16[1024,512]{1,0:T(8,128)(2,1)S(1)} %get-tuple-element.61.mine_ref, bf16[1280,512]{1,0:T(8,128)(2,1)S(1)} %collective-permute-done.other_ref, f32[8,512]{1,0:T(8,128)S(1)} %get-tuple-element.49.level_ref), custom_call_target="tpu_custom_call" | custom-call | flops 268435456 | tf_op jit(solution)/shard_map/panel_products/pallas_call | solution.py:450
  23.9 3.7 %collective-permute-start.10 = (f16[2,80,128]{2,1,0:T(8,128)(2,1)S(1)}, f16[2,80,128]{2,1,0:T(8,128)(2,1)S(1)}, u32[]{:S(2)}, u32[]{:S(2)}) collective-permute-start(f16[2,80,128]{2,1,0:T(8,128)(2,1)S(1)} %convert_element_type.251), channel_id=1, source_target_pairs={{0,24},{1,25},{2,26},{3,27},{4,28},{5,29},{6,30},{7,31},{8,16},{9,... | collective-permute-start | bytes 122888 | tf_op jit(solution)/shard_map/ppermute | solution.py:580
  27.6 0.8 %collective-permute-start.9 = (f16[2,80,128]{2,1,0:T(8,128)(2,1)S(1)}, f16[2,80,128]{2,1,0:T(8,128)(2,1)S(1)}, u32[]{:S(2)}, u32[]{:S(2)}) collective-permute-start(f16[2,80,128]{2,1,0:T(8,128)(2,1)S(1)} %convert_element_type.251), channel_id=1, source_target_pairs={{0,16},{1,17},{2,18},{3,19},{4,20},{5,21},{6,22},{7,23},{8,24},{9,... | collective-permute-start | bytes 122888 | tf_op jit(solution)/shard_map/ppermute | solution.py:580
  28.4 1.0 %collective-permute-done.2 = f16[520,256]{1,0:T(8,128)(2,1)S(1)} collective-permute-done((f16[520,256]{1,0:T(8,128)(2,1)S(1)}, f16[520,256]{1,0:T(8,128)(2,1)S(1)}, u32[]{:S(2)}, u32[]{:S(2)}) %collective-permute-start.2) | collective-permute-done | bytes 266272 | tf_op jit(solution)/shard_map/ppermute | solution.py:580
  30.1 1.6 %collective-permute-start.3 = (f16[264,512]{1,0:T(8,128)(2,1)S(1)}, f16[264,512]{1,0:T(8,128)(2,1)S(1)}, u32[]{:S(2)}, u32[]{:S(2)}) collective-permute-start(f16[264,512]{1,0:T(8,128)(2,1)S(1)} %convert_element_type.244), channel_id=1, source_target_pairs={{0,4},{1,5},{2,6},{3,7},{4,0},{5,1},{6,2},{7,3},{8,12},{9,13},{10,... | collective-permute-start | bytes 811016 | tf_op jit(solution)/shard_map/ppermute | solution.py:580
  31.7 1.5 %collective-permute-start.4 = (f16[264,256]{1,0:T(8,128)(2,1)S(1)}, f16[264,256]{1,0:T(8,128)(2,1)S(1)}, u32[]{:S(2)}, u32[]{:S(2)}) collective-permute-start(f16[264,256]{1,0:T(8,128)(2,1)S(1)} %pad_maximum_fusion.4), channel_id=1, source_target_pairs={{0,2},{1,3},{2,0},{3,1},{4,6},{5,7},{6,4},{7,5},{8,10},{9,11},{10,... | collective-permute-start | bytes 405512 | tf_op jit(solution)/shard_map/ppermute | solution.py:580
  33.3 0.5 %collective-permute-start.12 = (f16[80,128]{1,0:T(8,128)(2,1)S(1)}, f16[80,128]{1,0:T(8,128)(2,1)S(1)}, u32[]{:S(2)}, u32[]{:S(2)}) collective-permute-start(f16[80,128]{1,0:T(8,128)(2,1)S(1)} %get-tuple-element.102), channel_id=1, source_target_pairs={{0,6},{1,7},{2,4},{3,5},{4,2},{5,3},{6,0},{7,1},{8,14},{9,15},{10,... | collective-permute-start | bytes 61448 | tf_op jit(solution)/shard_map/ppermute | solution.py:580
  33.9 1.5 %collective-permute-start.13 = (f16[80,128]{1,0:T(8,128)(2,1)S(1)}, f16[80,128]{1,0:T(8,128)(2,1)S(1)}, u32[]{:S(2)}, u32[]{:S(2)}) collective-permute-start(f16[80,128]{1,0:T(8,128)(2,1)S(1)} %get-tuple-element.102), channel_id=1, source_target_pairs={{0,2},{1,3},{2,0},{3,1},{4,6},{5,7},{6,4},{7,5},{8,10},{9,11},{10,... | collective-permute-start | bytes 61448 | tf_op jit(solution)/shard_map/ppermute | solution.py:580
  35.4 1.5 %collective-permute-start.11 = (f16[80,128]{1,0:T(8,128)(2,1)S(1)}, f16[80,128]{1,0:T(8,128)(2,1)S(1)}, u32[]{:S(2)}, u32[]{:S(2)}) collective-permute-start(f16[80,128]{1,0:T(8,128)(2,1)S(1)} %get-tuple-element.66), channel_id=1, source_target_pairs={{0,4},{1,5},{2,6},{3,7},{4,0},{5,1},{6,2},{7,3},{8,12},{9,13},{10,... | collective-permute-start | bytes 61448 | tf_op jit(solution)/shard_map/ppermute | solution.py:580
  36.9 1.5 %collective-permute-done.3 = f16[264,512]{1,0:T(8,128)(2,1)S(1)} collective-permute-done((f16[264,512]{1,0:T(8,128)(2,1)S(1)}, f16[264,512]{1,0:T(8,128)(2,1)S(1)}, u32[]{:S(2)}, u32[]{:S(2)}) %collective-permute-start.3) | collective-permute-done | bytes 270368 | tf_op jit(solution)/shard_map/ppermute | solution.py:580
  38.8 2.6 %collective-permute-start.5 = (f16[72,768]{1,0:T(8,128)(2,1)S(1)}, f16[72,768]{1,0:T(8,128)(2,1)S(1)}, u32[]{:S(2)}, u32[]{:S(2)}) collective-permute-start(f16[72,768]{1,0:T(8,128)(2,1)S(1)} %get-tuple-element.58), channel_id=1, source_target_pairs={{0,16},{1,17},{2,18},{3,19},{4,20},{5,21},{6,22},{7,23},{8,24},{9,... | collective-permute-start | bytes 331784 | tf_op jit(solution)/shard_map/ppermute | solution.py:580
  41.4 1.3 %collective-permute-start.6 = (f16[72,768]{1,0:T(8,128)(2,1)S(1)}, f16[72,768]{1,0:T(8,128)(2,1)S(1)}, u32[]{:S(2)}, u32[]{:S(2)}) collective-permute-start(f16[72,768]{1,0:T(8,128)(2,1)S(1)} %get-tuple-element.59), channel_id=1, source_target_pairs={{0,24},{1,25},{2,26},{3,27},{4,28},{5,29},{6,30},{7,31},{8,16},{9,... | collective-permute-start | bytes 331784 | tf_op jit(solution)/shard_map/ppermute | solution.py:580
  43.0 5.2 %factor_panel.1 = f32[128,128]{1,0:T(8,128)} custom-call(f32[72,128]{1,0:T(8,128)S(1)} %add_add_fusion.panel_ref, f32[1,128]{1,0:T(1,128)S(1)} %copy-done.2), custom_call_target="tpu_custom_call" | custom-call | flops 2097152 | bytes 196608 | tf_op jit(solution)/shard_map/factor_panel/pallas_call | solution.py:538
  48.3 0.5 collective-permute-done.5
  48.8 0.7 %collective-permute-done.7 = f16[72,768]{1,0:T(8,128)(2,1)S(1)} collective-permute-done((f16[72,768]{1,0:T(8,128)(2,1)S(1)}, f16[72,768]{1,0:T(8,128)(2,1)S(1)}, u32[]{:S(2)}, u32[]{:S(2)}) %collective-permute-start.7) | collective-permute-done | bytes 110624 | tf_op jit(solution)/shard_map/ppermute | solution.py:580
  49.6 0.8 %fusion.10 = f32[1,64,768]{2,1,0:T(8,128)} fusion(f32[256,512]{1,0:T(8,128)S(1)} %multiply_add_fusion.1, f32[256,256]{1,0:T(8,128)S(1)} %fusion, f32[768]{0:T(1024)S(1)} %exponential_reduce_fusion, f16[72,768]{1,0:T(8,128)(2,1)S(1)} %collective-permute-done.7, f32[768]{0:T(1024)S(1)} %exponential_reduce_fusion.1, ...), kind=kLoop, calls=%fused_computation.22 | loop fusion | flops 491520 | bytes 1287168 | tf_op jit(solution)/shard_map/broadcast_in_dim | solution.py:649
  (60 shorter events, 2.1 us)
Async XLA Ops:
  0.6 1.9 %copy-start.5 = (f32[1,256]{1,0:T(1,128)S(1)}, f32[1,256]{1,0:T(1,128)}, u32[]{:S(2)}) copy-start(f32[1,256]{1,0:T(1,128)} %prior_ref.2) | copy-start | bytes 3076
  1.3 1.0 %copy-start.4 = (bf16[1,256,512]{2,1,0:T(8,128)(2,1)S(1)}, bf16[1,256,512]{2,1,0:T(8,128)(2,1)}, u32[]{:S(2)}) copy-start(bf16[1,256,512]{2,1,0:T(8,128)(2,1)} %param.7) | copy-start | bytes 786436
  2.5 1.7 %copy-start = (bf16[1,2304,512]{2,1,0:T(8,128)(2,1)S(1)}, bf16[1,2304,512]{2,1,0:T(8,128)(2,1)}, u32[]{:S(2)}) copy-start(bf16[1,2304,512]{2,1,0:T(8,128)(2,1)} %param.8) | copy-start | bytes 7077892
  2.5 1.7 %copy-start.1 = (s32[2048]{0:T(1024)S(1)}, s32[2048]{0:T(1024)}, u32[]{:S(2)}) copy-start(s32[2048]{0:T(1024)} %param.12) | copy-start | bytes 24580
  2.6 1.6 %copy-start.3 = (s32[1,4]{1,0:T(1,128)S(1)}, s32[1,4]{1,0:T(1,128)}, u32[]{:S(2)}) copy-start(s32[1,4]{1,0:T(1,128)} %band_ref.1) | copy-start | bytes 52
  13.5 3.2 %collective-permute-start = (bf16[1280,512]{1,0:T(8,128)(2,1)S(1)}, bf16[1280,512]{1,0:T(8,128)(2,1)S(1)}, u32[]{:S(2)}, u32[]{:S(2)}) collective-permute-start(bf16[1280,512]{1,0:T(8,128)(2,1)S(1)} %get-tuple-element.40.send_ref), channel_id=1, source_target_pairs={{0,1},{1,0},{2,3},{3,2},{4,5},{5,4},{6,7},{7,6},{8,9},{9,8},{10,11... | collective-permute-start | bytes 3932168 | tf_op jit(solution)/shard_map/ppermute | solution.py:580
  18.2 11.2 %collective-permute-start.1 = (f16[1288,128]{1,0:T(8,128)(2,1)S(1)}, f16[1288,128]{1,0:T(8,128)(2,1)S(1)}, u32[]{:S(2)}, u32[]{:S(2)}) collective-permute-start(f16[1288,128]{1,0:T(8,128)(2,1)S(1)} %convert_bitcast_fusion), channel_id=1, source_target_pairs={{0,2},{1,3},{2,0},{3,1},{4,6},{5,7},{6,4},{7,5},{8,10},{9,11},{10,... | collective-permute-start | bytes 989192 | tf_op jit(solution)/shard_map/ppermute | solution.py:580
  21.2 8.2 %collective-permute-start.2 = (f16[520,256]{1,0:T(8,128)(2,1)S(1)}, f16[520,256]{1,0:T(8,128)(2,1)S(1)}, u32[]{:S(2)}, u32[]{:S(2)}) collective-permute-start(f16[520,256]{1,0:T(8,128)(2,1)S(1)} %convert_element_type.241), channel_id=1, source_target_pairs={{0,4},{1,5},{2,6},{3,7},{4,0},{5,1},{6,2},{7,3},{8,12},{9,13},{10,... | collective-permute-start | bytes 798728 | tf_op jit(solution)/shard_map/ppermute | solution.py:580
  23.9 9.3 %collective-permute-start.10 = (f16[2,80,128]{2,1,0:T(8,128)(2,1)S(1)}, f16[2,80,128]{2,1,0:T(8,128)(2,1)S(1)}, u32[]{:S(2)}, u32[]{:S(2)}) collective-permute-start(f16[2,80,128]{2,1,0:T(8,128)(2,1)S(1)} %convert_element_type.251), channel_id=1, source_target_pairs={{0,24},{1,25},{2,26},{3,27},{4,28},{5,29},{6,30},{7,31},{8,16},{9,... | collective-permute-start | bytes 122888 | tf_op jit(solution)/shard_map/ppermute | solution.py:580
  27.6 5.6 %collective-permute-start.8 = (f16[2,80,128]{2,1,0:T(8,128)(2,1)S(1)}, f16[2,80,128]{2,1,0:T(8,128)(2,1)S(1)}, u32[]{:S(2)}, u32[]{:S(2)}) collective-permute-start(f16[2,80,128]{2,1,0:T(8,128)(2,1)S(1)} %convert_element_type.251), channel_id=1, source_target_pairs={{0,8},{1,9},{2,10},{3,11},{4,12},{5,13},{6,14},{7,15},{8,0},{9,1},... | collective-permute-start | bytes 122888 | tf_op jit(solution)/shard_map/ppermute | solution.py:580
  27.6 5.6 %collective-permute-start.9 = (f16[2,80,128]{2,1,0:T(8,128)(2,1)S(1)}, f16[2,80,128]{2,1,0:T(8,128)(2,1)S(1)}, u32[]{:S(2)}, u32[]{:S(2)}) collective-permute-start(f16[2,80,128]{2,1,0:T(8,128)(2,1)S(1)} %convert_element_type.251), channel_id=1, source_target_pairs={{0,16},{1,17},{2,18},{3,19},{4,20},{5,21},{6,22},{7,23},{8,24},{9,... | collective-permute-start | bytes 122888 | tf_op jit(solution)/shard_map/ppermute | solution.py:580
  30.1 12.9 %copy-start.2 = (f32[1,128]{1,0:T(1,128)S(1)}, f32[1,128]{1,0:T(1,128)}, u32[]{:S(2)}) copy-start(f32[1,128]{1,0:T(1,128)} %prior_ref.3) | copy-start | bytes 1540
  30.1 8.3 %collective-permute-start.3 = (f16[264,512]{1,0:T(8,128)(2,1)S(1)}, f16[264,512]{1,0:T(8,128)(2,1)S(1)}, u32[]{:S(2)}, u32[]{:S(2)}) collective-permute-start(f16[264,512]{1,0:T(8,128)(2,1)S(1)} %convert_element_type.244), channel_id=1, source_target_pairs={{0,4},{1,5},{2,6},{3,7},{4,0},{5,1},{6,2},{7,3},{8,12},{9,13},{10,... | collective-permute-start | bytes 811016 | tf_op jit(solution)/shard_map/ppermute | solution.py:580
  31.7 5.2 %collective-permute-start.4 = (f16[264,256]{1,0:T(8,128)(2,1)S(1)}, f16[264,256]{1,0:T(8,128)(2,1)S(1)}, u32[]{:S(2)}, u32[]{:S(2)}) collective-permute-start(f16[264,256]{1,0:T(8,128)(2,1)S(1)} %pad_maximum_fusion.4), channel_id=1, source_target_pairs={{0,2},{1,3},{2,0},{3,1},{4,6},{5,7},{6,4},{7,5},{8,10},{9,11},{10,... | collective-permute-start | bytes 405512 | tf_op jit(solution)/shard_map/ppermute | solution.py:580
  33.3 9.6 %collective-permute-start.12 = (f16[80,128]{1,0:T(8,128)(2,1)S(1)}, f16[80,128]{1,0:T(8,128)(2,1)S(1)}, u32[]{:S(2)}, u32[]{:S(2)}) collective-permute-start(f16[80,128]{1,0:T(8,128)(2,1)S(1)} %get-tuple-element.102), channel_id=1, source_target_pairs={{0,6},{1,7},{2,4},{3,5},{4,2},{5,3},{6,0},{7,1},{8,14},{9,15},{10,... | collective-permute-start | bytes 61448 | tf_op jit(solution)/shard_map/ppermute | solution.py:580
  33.9 9.1 %collective-permute-start.13 = (f16[80,128]{1,0:T(8,128)(2,1)S(1)}, f16[80,128]{1,0:T(8,128)(2,1)S(1)}, u32[]{:S(2)}, u32[]{:S(2)}) collective-permute-start(f16[80,128]{1,0:T(8,128)(2,1)S(1)} %get-tuple-element.102), channel_id=1, source_target_pairs={{0,2},{1,3},{2,0},{3,1},{4,6},{5,7},{6,4},{7,5},{8,10},{9,11},{10,... | collective-permute-start | bytes 61448 | tf_op jit(solution)/shard_map/ppermute | solution.py:580
  35.4 7.3 %collective-permute-start.11 = (f16[80,128]{1,0:T(8,128)(2,1)S(1)}, f16[80,128]{1,0:T(8,128)(2,1)S(1)}, u32[]{:S(2)}, u32[]{:S(2)}) collective-permute-start(f16[80,128]{1,0:T(8,128)(2,1)S(1)} %get-tuple-element.66), channel_id=1, source_target_pairs={{0,4},{1,5},{2,6},{3,7},{4,0},{5,1},{6,2},{7,3},{8,12},{9,13},{10,... | collective-permute-start | bytes 61448 | tf_op jit(solution)/shard_map/ppermute | solution.py:580
  38.8 10.0 %collective-permute-start.5 = (f16[72,768]{1,0:T(8,128)(2,1)S(1)}, f16[72,768]{1,0:T(8,128)(2,1)S(1)}, u32[]{:S(2)}, u32[]{:S(2)}) collective-permute-start(f16[72,768]{1,0:T(8,128)(2,1)S(1)} %get-tuple-element.58), channel_id=1, source_target_pairs={{0,16},{1,17},{2,18},{3,19},{4,20},{5,21},{6,22},{7,23},{8,24},{9,... | collective-permute-start | bytes 331784 | tf_op jit(solution)/shard_map/ppermute | solution.py:580
  41.4 7.4 %collective-permute-start.6 = (f16[72,768]{1,0:T(8,128)(2,1)S(1)}, f16[72,768]{1,0:T(8,128)(2,1)S(1)}, u32[]{:S(2)}, u32[]{:S(2)}) collective-permute-start(f16[72,768]{1,0:T(8,128)(2,1)S(1)} %get-tuple-element.59), channel_id=1, source_target_pairs={{0,24},{1,25},{2,26},{3,27},{4,28},{5,29},{6,30},{7,31},{8,16},{9,... | collective-permute-start | bytes 331784 | tf_op jit(solution)/shard_map/ppermute | solution.py:580
  42.7 6.8 %collective-permute-start.7 = (f16[72,768]{1,0:T(8,128)(2,1)S(1)}, f16[72,768]{1,0:T(8,128)(2,1)S(1)}, u32[]{:S(2)}, u32[]{:S(2)}) collective-permute-start(f16[72,768]{1,0:T(8,128)(2,1)S(1)} %get-tuple-element.60), channel_id=1, source_target_pairs={{0,8},{1,9},{2,10},{3,11},{4,12},{5,13},{6,14},{7,15},{8,0},{9,1},... | collective-permute-start | bytes 331784 | tf_op jit(solution)/shard_map/ppermute | solution.py:580
